TPU v7x, 32 devices: a whole 2x2x4 slice. The times are simulated.
32 devices in a mesh: ctx: 16 (over z, y, core), kvh: 2 (over x).
Axes of the slice: x: 2, y: 2, z: 4, core: 2. Of those that a mesh axis runs over, the one named last changes fastest.
Arguments:
- queries: bfloat16 [2048, 2048], P(('ctx', 'kvh')), may hold values from -180 to 180
- keys: bfloat16 [2048, 256], P(('ctx', 'kvh')), may hold values from -6 to 6
- values: bfloat16 [2048, 256], P(('ctx', 'kvh')), may hold values from -6 to 6
Outputs:
- attended: bfloat16 [2048, 2048], P(('ctx', 'kvh'))
All inputs are finite; a program needn't handle non-finite values.
Results may differ from a plain program's by a relative error of at most 0.006.
Values may be sent and summed in bfloat16 or wider, within the bound.
No kernel may reach another device: no remote copies, remote signals or barrier semaphores. Data moves between devices by JAX's collectives and lax.ppermute only.
A program may use at most 64 MiB of HBM per device.

v0:
```python
import math

import jax
import jax.numpy as jnp
from jax import lax
from jax.sharding import PartitionSpec as P

HD = 128


def update_state(state_now, query_tile, query_place, key_part, value_part, key_place):
    largest_old, totals_old, summed_old = state_now
    factor = 1.0 / math.sqrt(query_tile.shape[2])
    scores = (
        jnp.einsum("qhd,kd->hqk", query_tile, key_part, preferred_element_type=jnp.float32) * factor
    )
    visible = key_place[None, None, :] <= query_place[None, :, None]
    scores = jnp.where(visible, scores, -1e30)
    largest_new = jnp.maximum(largest_old, jnp.max(scores, axis=-1))
    weights = jnp.where(visible, jnp.exp(scores - largest_new[:, :, None]), 0.0)
    totals_new = jnp.sum(weights, axis=-1)
    product = jnp.einsum(
        "hqk,kd->hqd", weights.astype(jnp.bfloat16), value_part, preferred_element_type=jnp.float32
    )
    return (largest_new, totals_new, product)


def mirror_forward(payload, devices):
    height, width = payload.shape
    pieces = payload.reshape(height, devices, width // devices)
    spread = lax.all_to_all(pieces, "ctx", split_axis=1, concat_axis=1, tiled=True)
    flipped = jnp.flip(spread, axis=1)
    collected = lax.all_to_all(flipped, "ctx", split_axis=1, concat_axis=1, tiled=True)
    return collected.reshape(height, width)


def mirror_return(payload, devices):
    height, width = payload.shape
    pieces = payload.reshape(height, devices, width // devices)
    spread = lax.all_to_all(pieces, "ctx", split_axis=1, concat_axis=1, tiled=True)
    flipped = jnp.flip(spread, axis=1)
    collected = lax.all_to_all(flipped, "ctx", split_axis=1, concat_axis=1, tiled=True)
    return collected.reshape(height, width)


def per_device(queries, keys, values):
    query_rows, key_rows, value_rows = (
        lax.all_to_all(queries, "kvh", split_axis=1, concat_axis=0, tiled=True),
        lax.all_to_all(keys, "kvh", split_axis=1, concat_axis=0, tiled=True),
        lax.all_to_all(values, "kvh", split_axis=1, concat_axis=0, tiled=True),
    )
    devices = lax.axis_size("ctx")
    position = lax.axis_index("ctx")
    block_rows = query_rows.shape[0]
    halfway = block_rows // 2
    query_width = query_rows.shape[1]
    groups = query_width // HD
    joined = jnp.concatenate(
        [query_rows[halfway:], key_rows[halfway:], value_rows[halfway:]], axis=1
    )
    moved = mirror_forward(joined, devices)
    carried = (
        moved[:, :query_width],
        moved[:, query_width : query_width + HD],
        moved[:, query_width + HD :],
    )
    query_local = jnp.concatenate([query_rows[:halfway], carried[0]], axis=0)
    key_local = jnp.concatenate([key_rows[:halfway], carried[1]], axis=0)
    value_local = jnp.concatenate([value_rows[:halfway], carried[2]], axis=0)
    query_halves = (2 * position, 2 * devices - 1 - 2 * position)
    query_tiles = [
        query_local[which * halfway : (which + 1) * halfway].reshape(halfway, groups, HD)
        for which in range(2)
    ]
    query_places = [
        query_halves[which] * halfway + jnp.arange(halfway, dtype=jnp.int32) for which in range(2)
    ]

    def key_positions(gathered_index):
        source = gathered_index // block_rows
        within = gathered_index % block_rows
        second_half = 2 * devices - 1 - 2 * source
        owner_half = jnp.where(within < halfway, 2 * source, second_half)
        return owner_half * halfway + within % halfway

    def fold_blocks(running, pieces):
        key_part, value_part = pieces
        key_place = key_positions(jnp.arange(key_part.shape[0], dtype=jnp.int32))
        earliest = jnp.min(key_place)
        updated = []
        for which in range(2):

            def advance(state_now, which=which):
                return update_state(
                    state_now,
                    query_tiles[which],
                    query_places[which],
                    key_part,
                    value_part,
                    key_place,
                )

            def unchanged(state_now):
                return state_now

            needed = earliest <= query_halves[which] * halfway + halfway - 1
            updated.append(lax.cond(needed, advance, unchanged, running[which]))
        return tuple(updated)

    start_state = (
        jnp.full((groups, halfway), -1e30, jnp.float32),
        jnp.zeros((groups, halfway), jnp.float32),
        jnp.zeros((groups, halfway, HD), jnp.float32),
    )
    finished = fold_blocks(
        (start_state, start_state),
        (
            lax.all_gather(key_local, "ctx", axis=0, tiled=True),
            lax.all_gather(value_local, "ctx", axis=0, tiled=True),
        ),
    )
    output_halves = []
    for which in range(2):
        largest_end, totals_end, summed_end = finished[which]
        normed = summed_end / totals_end[:, :, None]
        output_halves.append(
            jnp.transpose(normed, (1, 0, 2)).reshape(halfway, groups * HD).astype(jnp.bfloat16)
        )
    returned = mirror_return(output_halves[1], devices)
    output_rows = jnp.concatenate([output_halves[0], returned], axis=0)
    return lax.all_to_all(output_rows, "kvh", split_axis=0, concat_axis=1, tiled=True)


def solution(mesh):
    placed = (P(("ctx", "kvh"), None), P(("ctx", "kvh"), None), P(("ctx", "kvh"), None))
    return jax.shard_map(
        per_device, mesh=mesh, in_specs=placed, out_specs=P(("ctx", "kvh"), None), check_vma=False
    )
```

profile of v0, /device:TPU:0, one launch (start us, length us, event | category | flops | bytes accessed | tf_op | source)
XLA Modules:
  0.0 132.4 jit_solution(14150385409731757138)
XLA Ops:
  0.0 0.0 copy-start
  0.0 0.8 copy-done
  0.8 0.6 copy_bitcast_fusion.2
  1.4 4.2 %all-to-all-start.2 = ((bf16[64,2,128]{2,0,1:T(8,128)(2,1)}), bf16[64,2,128]{2,0,1:T(8,128)(2,1)S(1)}, u32[]{:S(2)}, u32[]{:S(2)}) async-start(bf16[64,2,128]{2,0,1:T(8,128)(2,1)} %copy_bitcast_fusion.2), calls=%async_computation.2 | async-start | bytes 65536 | tf_op jit(solution)/shard_map/all_to_all | solution.py:50
  5.6 1.4 %copy_bitcast_fusion.3 = bf16[64,2,128]{2,0,1:T(8,128)(2,1)} fusion(bf16[64,256]{1,0:T(8,128)(2,1)} %param.8), kind=kLoop, calls=%fused_computation.47 | loop fusion | bytes 65536 | tf_op jit(solution)/shard_map/all_to_all | solution.py:49
  6.9 1.7 %copy.59 = bf16[8,2,8,1024]{3,2,0,1:T(8,128)(2,1)} copy(bf16[8,2,8,1024]{3,2,1,0:T(8,128)(2,1)} %bitcast.105) | data formatting | bytes 524288 | tf_op jit(solution)/shard_map/all_to_all | solution.py:48
  8.6 0.9 all-to-all-done.2
  9.5 3.3 %all-to-all-start.1 = ((bf16[64,2,128]{2,0,1:T(8,128)(2,1)}), bf16[64,2,128]{2,0,1:T(8,128)(2,1)S(1)}, u32[]{:S(2)}, u32[]{:S(2)}) async-start(bf16[64,2,128]{2,0,1:T(8,128)(2,1)} %copy_bitcast_fusion.3), calls=%async_computation.1 | async-start | bytes 65536 | tf_op jit(solution)/shard_map/all_to_all | solution.py:49
  12.8 3.9 %all-to-all-done.1 = bf16[64,2,128]{2,0,1:T(8,128)(2,1)S(1)} async-done(((bf16[64,2,128]{2,0,1:T(8,128)(2,1)}), bf16[64,2,128]{2,0,1:T(8,128)(2,1)S(1)}, u32[]{:S(2)}, u32[]{:S(2)}) %all-to-all-start.1) | async-done | bytes 32800 | tf_op jit(solution)/shard_map/all_to_all | solution.py:49
  16.7 3.4 %all-to-all-start = ((bf16[64,2,1024]{2,0,1:T(8,128)(2,1)}), bf16[64,2,1024]{2,0,1:T(8,128)(2,1)S(1)}, u32[]{:S(2)}, u32[]{:S(2)}) async-start(bf16[64,2,1024]{2,0,1:T(8,128)(2,1)} %bitcast.95), calls=%async_computation | async-start | bytes 524288 | tf_op jit(solution)/shard_map/all_to_all | solution.py:48
  20.2 5.1 %all-to-all-done = bf16[64,2,1024]{2,0,1:T(8,128)(2,1)S(1)} async-done(((bf16[64,2,1024]{2,0,1:T(8,128)(2,1)}), bf16[64,2,1024]{2,0,1:T(8,128)(2,1)S(1)}, u32[]{:S(2)}, u32[]{:S(2)}) %all-to-all-start) | async-done | bytes 262176 | tf_op jit(solution)/shard_map/all_to_all | solution.py:48
  25.4 0.4 reshape.114
  25.8 0.1 copy.30
  25.8 16.3 %all_to_all.87 = bf16[64,16,80]{2,0,1:T(8,128)(2,1)S(1)} all-to-all(bf16[64,16,80]{2,0,1:T(8,128)(2,1)S(1)} %copy.30), channel_id=1, replica_groups=mesh['ctx'=16,'kvh'=2] {'ctx'}, dimensions={1} | all-to-all | bytes 327680 | tf_op jit(solution)/shard_map/all_to_all | solution.py:31
  42.1 0.7 rev.8
  42.8 3.5 %all-to-all-start.4 = ((bf16[64,16,80]{2,0,1:T(8,128)(2,1)}), bf16[64,16,80]{2,0,1:T(8,128)(2,1)S(1)}, u32[]{:S(2)}, u32[]{:S(2)}) async-start(bf16[64,16,80]{2,0,1:T(8,128)(2,1)} %rev.8), calls=%async_computation.4 | async-start | bytes 524288 | tf_op jit(solution)/shard_map/all_to_all | solution.py:33
  46.4 0.6 fusion.41
  47.6 8.8 %all-to-all-done.4 = bf16[64,16,80]{2,0,1:T(8,128)(2,1)S(1)} async-done(((bf16[64,16,80]{2,0,1:T(8,128)(2,1)}), bf16[64,16,80]{2,0,1:T(8,128)(2,1)S(1)}, u32[]{:S(2)}, u32[]{:S(2)}) %all-to-all-start.4) | async-done | bytes 163872 | tf_op jit(solution)/shard_map/all_to_all | solution.py:33
  56.4 0.2 copy.31
  56.6 0.3 reshape.115
  56.8 20.2 %all_gather.7 = bf16[2048,128]{1,0:T(8,128)(2,1)S(1)} all-gather(bf16[128,128]{1,0:T(8,128)(2,1)S(1)} %pad_maximum_fusion.3), channel_id=1, replica_groups=mesh['ctx'=16,'kvh'=2] {'ctx'}, dimensions={0}, use_global_device_ids=true | all-gather | bytes 557056 | tf_op jit(solution)/shard_map/all_gather | solution.py:119
  77.1 18.9 %all_gather.6 = bf16[2048,128]{1,0:T(8,128)(2,1)S(1)} all-gather(bf16[128,128]{1,0:T(8,128)(2,1)S(1)} %pad_maximum_fusion.2), channel_id=1, replica_groups=mesh['ctx'=16,'kvh'=2] {'ctx'}, dimensions={0}, use_global_device_ids=true | all-gather | bytes 557056 | tf_op jit(solution)/shard_map/all_gather | solution.py:118
  95.9 3.5 %conditional.3 = (f32[8,64]{1,0:T(8,128)S(1)}, f32[8,64,128]{2,1,0:T(8,128)S(1)}) conditional(s32[]{:T(128)} %convert_element_type.35, () %tuple.23, (s32[2048]{0:T(1024)S(1)}, s32[]{:T(128)}, s32[64]{0:T(128)S(1)}, bf16[64,1280]{1,0:T(8,128)(2,1)S(1)}, bf16[2048,128]{1,0:T(8,128)(2,1)S(1)}, /*index=5*/bf16[2048,128]{1,0:T(8,128)(2,1)S(1)}) %tuple.24), branch_computations={%region_5.6_spmd, %region_6.9_spmd} | conditional | flops 550633024 | bytes 14570260 | solution.py:107
  95.9 0.1 broadcast_compare_fusion.1
  96.1 0.9 fusion.13
  97.0 1.2 fusion.16
  98.2 1.3 fusion.15
  99.5 0.1 fusion.28
  99.6 0.1 copy.33
  99.7 0.1 convert_element_type.38
  99.8 0.1 copy.60
  99.9 0.2 reshape.121
  100.2 10.8 %all_to_all.88 = bf16[16,2,2048]{2,1,0:T(2,128)(2,1)S(1)} all-to-all(bf16[16,2,2048]{2,1,0:T(2,128)(2,1)S(1)} %reshape.121), channel_id=1, replica_groups=mesh['ctx'=16,'kvh'=2] {'ctx'}, dimensions={0} | all-to-all | bytes 262144 | tf_op jit(solution)/shard_map/all_to_all | solution.py:40
  111.0 0.2 reshape.122
  111.2 0.9 reshape.123
  112.1 3.5 %all-to-all-start.6 = ((bf16[16,2,2048]{2,1,0:T(2,128)(2,1)}), bf16[16,2,2048]{2,1,0:T(2,128)(2,1)S(1)}, u32[]{:S(2)}, u32[]{:S(2)}) async-start(bf16[16,2,2048]{2,1,0:T(2,128)(2,1)} %reshape.123), calls=%async_computation.6 | async-start | bytes 262144 | tf_op jit(solution)/shard_map/all_to_all | solution.py:42
  116.2 3.6 %conditional.2 = (f32[8,64]{1,0:T(8,128)S(1)}, f32[8,64,128]{2,1,0:T(8,128)S(1)}) conditional(s32[]{:T(128)} %convert_element_type.31, () %tuple.21, (s32[2048]{0:T(1024)S(1)}, s32[]{:T(128)}, s32[64]{0:T(128)S(1)}, bf16[2,64,1024]{2,1,0:T(8,128)(2,1)S(1)}, bf16[2048,128]{1,0:T(8,128)(2,1)S(1)}, /*index=5*/bf16[2048,128]{1,0:T(8,128)(2,1)S(1)}) %tuple.37), branch_computations={%region_1.2_spmd, %region_2.5_spmd} | conditional | flops 550633024 | bytes 15094548 | solution.py:107
  116.2 0.1 broadcast_compare_fusion
  116.4 0.9 fusion
  117.4 1.2 fusion.3
  118.5 1.3 fusion.2
  119.8 0.1 copy_bitcast_fusion.1
  120.0 3.6 %all-to-all-done.6 = bf16[16,2,2048]{2,1,0:T(2,128)(2,1)S(1)} async-done(((bf16[16,2,2048]{2,1,0:T(2,128)(2,1)}), bf16[16,2,2048]{2,1,0:T(2,128)(2,1)S(1)}, u32[]{:S(2)}, u32[]{:S(2)}) %all-to-all-start.6) | async-done | bytes 131104 | tf_op jit(solution)/shard_map/all_to_all | solution.py:42
  123.5 0.2 reshape.124
  123.7 0.2 copy.35
  123.9 0.2 reshape.116
  124.1 7.6 %all_to_all.89 = bf16[2,64,1024]{2,1,0:T(8,128)(2,1)S(1)} all-to-all(bf16[2,64,1024]{2,1,0:T(8,128)(2,1)S(1)} %bitcast.99), channel_id=1, replica_groups=mesh['ctx'=16,'kvh'=2] {'kvh'}, dimensions={0} | all-to-all | bytes 524288 | tf_op jit(solution)/shard_map/all_to_all | solution.py:131
  131.7 0.7 copy.43
  (18 shorter events, 0.2 us)
Async XLA Ops:
  0.0 0.8 copy-start
  1.4 8.2 %all-to-all-start.2 = ((bf16[64,2,128]{2,0,1:T(8,128)(2,1)}), bf16[64,2,128]{2,0,1:T(8,128)(2,1)S(1)}, u32[]{:S(2)}, u32[]{:S(2)}) async-start(bf16[64,2,128]{2,0,1:T(8,128)(2,1)} %copy_bitcast_fusion.2), calls=%async_computation.2 | async-start | bytes 65536 | tf_op jit(solution)/shard_map/all_to_all | solution.py:50
  9.5 7.2 %all-to-all-start.1 = ((bf16[64,2,128]{2,0,1:T(8,128)(2,1)}), bf16[64,2,128]{2,0,1:T(8,128)(2,1)S(1)}, u32[]{:S(2)}, u32[]{:S(2)}) async-start(bf16[64,2,128]{2,0,1:T(8,128)(2,1)} %copy_bitcast_fusion.3), calls=%async_computation.1 | async-start | bytes 65536 | tf_op jit(solution)/shard_map/all_to_all | solution.py:49
  16.7 8.6 %all-to-all-start = ((bf16[64,2,1024]{2,0,1:T(8,128)(2,1)}), bf16[64,2,1024]{2,0,1:T(8,128)(2,1)S(1)}, u32[]{:S(2)}, u32[]{:S(2)}) async-start(bf16[64,2,1024]{2,0,1:T(8,128)(2,1)} %bitcast.95), calls=%async_computation | async-start | bytes 524288 | tf_op jit(solution)/shard_map/all_to_all | solution.py:48
  42.8 13.5 %all-to-all-start.4 = ((bf16[64,16,80]{2,0,1:T(8,128)(2,1)}), bf16[64,16,80]{2,0,1:T(8,128)(2,1)S(1)}, u32[]{:S(2)}, u32[]{:S(2)}) async-start(bf16[64,16,80]{2,0,1:T(8,128)(2,1)} %rev.8), calls=%async_computation.4 | async-start | bytes 524288 | tf_op jit(solution)/shard_map/all_to_all | solution.py:33
  112.1 11.4 %all-to-all-start.6 = ((bf16[16,2,2048]{2,1,0:T(2,128)(2,1)}), bf16[16,2,2048]{2,1,0:T(2,128)(2,1)S(1)}, u32[]{:S(2)}, u32[]{:S(2)}) async-start(bf16[16,2,2048]{2,1,0:T(2,128)(2,1)} %reshape.123), calls=%async_computation.6 | async-start | bytes 262144 | tf_op jit(solution)/shard_map/all_to_all | solution.py:42
where the time goes:
time: 133 us; the launch traced here: 132 us
  blocking collectives  73.7 us (55%)
  waiting for transfers between devices  22.3 us (17%)
  starting transfers between devices  17.9 us (13%)
  local copies, waits for them, and re-layouts  9.02 us (7%)
  matrix products  4.17 us (3%)
  other arithmetic  3.83 us (3%)
  between operations  1.35 us (1%)
    all_gather x1, blocking collectives, per_device(): lax.all_gather(value_local, 'ctx', axis=0, tiled=True)  20.2 us
    all_gather x1, blocking collectives, per_device(): lax.all_gather(key_local, 'ctx', axis=0, tiled=True)  18.9 us
    all_to_all x1, blocking collectives, mirror_forward(): lax.all_to_all(pieces, 'ctx', split_axis=1, concat_axis=1, tiled=True)  16.3 us
    all_to_all x1, blocking collectives, mirror_return(): lax.all_to_all(pieces, 'ctx', split_axis=1, concat_axis=1, tiled=True)  10.8 us
    all_to_all x1, waiting for transfers between devices, mirror_forward(): lax.all_to_all(flipped, 'ctx', split_axis=1, concat_axis=1, tiled=True)  8.78 us
    all_to_all x1, blocking collectives, per_device(): lax.all_to_all(output_rows, 'kvh', split_axis=0, concat_axis=1, tiled=True)  7.56 us
    all_to_all x1, waiting for transfers between devices, per_device(): lax.all_to_all(queries, 'kvh', split_axis=1, concat_axis=0, tiled=True)  5.15 us
    all_to_all x1, starting transfers between devices, per_device(): lax.all_to_all(values, 'kvh', split_axis=1, concat_axis=0, tiled=True)  4.21 us
  transfers between devices with their start and end apart: 5, of which 5 were waited for; matrix products, arithmetic and copies ran while one was open for 6% of the time, Pallas kernels for 0%

commit v1 on v0

v1 whole, which is shorter than its diff:
```python
import functools
import math

import jax
import jax.numpy as jnp
from jax import lax
from jax.experimental import pallas as pl
from jax.experimental.pallas import tpu as pltpu
from jax.sharding import PartitionSpec as P

HD = 128
AXES = ("ctx", "kvh")
CORES = 2
HIDDEN = -1e30


class Layout:
    def __init__(self, mesh_shape):
        ctx, self.across = mesh_shape["ctx"], mesh_shape["kvh"]
        self.lines = 2
        self.planes = ctx // (CORES * self.lines)
        self.size = ctx * self.across
        self.mixed = self.lines == self.across

    def split(self, rank):
        column = rank % self.across
        core = rank // self.across % CORES
        line = rank // (self.across * CORES) % self.lines
        plane = rank // (self.across * CORES * self.lines)
        return plane, line, core, column

    def join(self, plane, line, core, column):
        return ((plane * self.lines + line) * CORES + core) * self.across + column

    def moved(self, place, first, second):
        plane, line, core, column = place
        if self.mixed:
            by_line = jnp.where(core == 0, second, first) if not isinstance(core, int) else (first if core else second)
            by_column = first + second - by_line
        else:
            by_line, by_column = second, first
        return plane, (line + by_line) % self.lines, core, (column + by_column) % self.across

    def firsts(self):
        return self.across

    def seconds(self):
        return self.lines

    def pairs(self, move):
        found = []
        for rank in range(self.size):
            target = move(self.split(rank))
            if target is not None:
                found.append((rank, self.join(*target)))
        return found


def gather_pieces(layout, block):
    def up(steps):
        def move(place):
            plane, line, core, column = place
            return (plane + steps, line, core, column) if plane + steps < layout.planes else None

        return layout.pairs(move)

    def on(first, second):
        return layout.pairs(lambda place: layout.moved(place, first, second))

    other = layout.pairs(lambda place: (place[0], place[1], 1 - place[2], place[3]))
    column = [block] + [lax.ppermute(block, AXES, up(steps)) for steps in range(1, layout.planes)]
    column = jnp.concatenate(column, axis=0)
    held = {(0, 0): column}
    for first in range(1, layout.firsts()):
        held[first, 0] = lax.ppermute(column, AXES, on(first, 0))
    for second in range(1, layout.seconds()):
        held[0, second] = lax.ppermute(column, AXES, on(0, second))
    for first in range(1, layout.firsts()):
        for second in range(1, layout.seconds()):
            held[first, second] = lax.ppermute(held[first, 0], AXES, on(0, second))
    places = sorted(held)
    own = [held[place] for place in places]
    swapped = [lax.ppermute(piece, AXES, other) for piece in own]
    return places, own + swapped


def attend_kernel(layout, places, rows, *refs):
    query_ref, refs = refs[0], refs[1:]
    count = 2 * len(places)
    key_refs, value_refs, out_ref, score_ref = refs[:count], refs[count : 2 * count], refs[-2], refs[-1]
    rank = lax.axis_index("ctx") * layout.across + lax.axis_index("kvh")
    plane, line, core, column = layout.split(rank)
    heads = query_ref.shape[1] // HD
    width = key_refs[0].shape[0]
    query = jnp.concatenate([query_ref[:, h * HD : (h + 1) * HD] for h in range(heads)], axis=0)
    along = lax.broadcasted_iota(jnp.int32, (1, width), 1)
    for at in range(count):
        first, second = places[at % len(places)]
        own_core = at < len(places)
        there = core if own_core else 1 - core
        _, source_line, _, source_column = layout.moved((plane, line, there, column), -first, -second)
        bias = jnp.zeros((1, width), jnp.float32)
        for steps in range(layout.planes):
            source = layout.join(plane - steps, source_line, there, source_column)
            hidden = jnp.logical_or(plane < steps, source > rank)
            level = jnp.where(hidden, jnp.float32(HIDDEN), jnp.float32(0.0))
            bias = jnp.where(along // rows == steps, level, bias)
        scores = lax.dot_general(
            query, key_refs[at][...], (((1,), (1,)), ((), ())), preferred_element_type=jnp.float32
        )
        scores = scores + bias
        if at == 0:
            token = lax.broadcasted_iota(jnp.int32, scores.shape, 0) % rows
            place = lax.broadcasted_iota(jnp.int32, scores.shape, 1)
            scores = jnp.where(jnp.logical_and(place < rows, place > token), HIDDEN, scores)
        score_ref[:, at * width : (at + 1) * width] = scores
    scale = math.log2(math.e) / math.sqrt(HD)
    largest = jnp.max(score_ref[...], axis=1, keepdims=True) * scale
    totals = jnp.zeros((heads * rows, 1), jnp.float32)
    summed = jnp.zeros((heads * rows, HD), jnp.float32)
    for at in range(count):
        weights = jnp.exp2(score_ref[:, at * width : (at + 1) * width] * scale - largest)
        totals = totals + jnp.sum(weights, axis=1, keepdims=True)
        summed = summed + jnp.dot(
            weights.astype(jnp.bfloat16), value_refs[at][...], preferred_element_type=jnp.float32
        )
    result = (summed / totals).astype(jnp.bfloat16)
    for h in range(heads):
        out_ref[:, h * HD : (h + 1) * HD] = result[h * rows : (h + 1) * rows]


def attend(layout, places, queries, pieces, groups):
    rows, query_width = queries.shape
    width = pieces[0].shape[0]
    per_group = query_width // groups

    def spec(offset):
        return pl.BlockSpec((width, HD), lambda g: (0, offset + g))

    tokens = width * len(pieces)
    return pl.pallas_call(
        functools.partial(attend_kernel, layout, places, rows),
        grid=(groups,),
        in_specs=[pl.BlockSpec((rows, per_group), lambda g: (0, g))]
        + [spec(0) for _ in pieces]
        + [spec(groups) for _ in pieces],
        out_specs=pl.BlockSpec((rows, per_group), lambda g: (0, g)),
        out_shape=jax.ShapeDtypeStruct((rows, query_width), jnp.bfloat16),
        scratch_shapes=[pltpu.VMEM((rows * per_group // HD, tokens), jnp.float32)],
        compiler_params=pltpu.CompilerParams(vmem_limit_bytes=32 * 1024 * 1024),
        cost_estimate=pl.CostEstimate(
            flops=4 * rows * query_width * tokens, bytes_accessed=4 * tokens * groups * HD, transcendentals=0
        ),
    )(queries, *pieces, *pieces)


def solution(mesh):
    layout = Layout(dict(mesh.shape))

    def per_device(queries, keys, values):
        block = jnp.concatenate([keys, values], axis=1)
        places, pieces = gather_pieces(layout, block)
        return attend(layout, places, queries, pieces, keys.shape[1] // HD)

    placed = P(AXES, None)
    return jax.shard_map(
        per_device, mesh=mesh, in_specs=(placed, placed, placed), out_specs=placed, check_vma=False
    )
```

time: 133 us -> 37.4 us (0.28)
  blocking collectives: 73.7 us -> 0 us
  local copies, waits for them, and re-layouts: 9.02 us -> 0.78 us
  waiting for transfers between devices: 22.3 us -> 15.4 us
  Pallas kernels: 0 us -> 6.41 us
  matrix products: 4.17 us -> 0 us
  other arithmetic: 3.83 us -> 0.02 us
  starting transfers between devices: 17.9 us -> 14.4 us
    all_gather x2 -> x0, blocking collectives: 39.1 us -> none  [the longest x1 20.2 us: per_device(): lax.all_gather(value_local, 'ctx', axis=0, tiled=True)]
    all_to_all x3 -> x0, blocking collectives: 34.6 us -> none  [the longest x1 16.3 us: mirror_forward(): lax.all_to_all(pieces, 'ctx', split_axis=1, concat_axis=1, tiled=True)]
    all_to_all x5 -> x0, waiting for transfers between devices: 22.3 us -> none  [the longest x1 8.78 us: mirror_forward(): lax.all_to_all(flipped, 'ctx', split_axis=1, concat_axis=1, tiled=True)]
    all_to_all x5 -> x0, starting transfers between devices: 17.9 us -> none  [the longest x1 4.21 us: per_device(): lax.all_to_all(values, 'kvh', split_axis=1, concat_axis=0, tiled=True)]
    ppermute x0 -> x10, waiting for transfers between devices: none -> 15.4 us  [the longest x1 6.17 us: gather_pieces(): held[first, 0] = lax.ppermute(column, AXES, on(first, 0))]
    ppermute x0 -> x10, starting transfers between devices: none -> 14.4 us  [the longest x3 10.9 us: gather_pieces(): lax.ppermute(block, AXES, up(steps))]
    pallas_call x0 -> x1, Pallas kernels: none -> 6.41 us  [attend(): pl.pallas_call(functools.partial(attend_kernel, layout, places, rows), gr...]
    all_to_all x6 -> x0, local copies, waits for them, and re-layouts: 4.71 us -> none  [the longest x1 1.67 us: per_device(): lax.all_to_all(queries, 'kvh', split_axis=1, concat_axis=0, tiled=True)]
  transfers between devices with their start and end apart: 5 -> 10, of which waited for: 5 -> 4; matrix products, arithmetic and copies ran while one was open for 6% -> 0% of each run, Pallas kernels for 0% -> 0%
where the time goes in v1:
time: 37.4 us; the launch traced here: 37.1 us
  waiting for transfers between devices  15.4 us (41%)
  starting transfers between devices  14.4 us (39%)
  Pallas kernels  6.41 us (17%)
  local copies, waits for them, and re-layouts  0.78 us (2%)
    ppermute x3, starting transfers between devices, gather_pieces(): lax.ppermute(block, AXES, up(steps))  10.9 us
    pallas_call x1, Pallas kernels, attend(): pl.pallas_call(functools.partial(attend_kernel, layout, places, rows), gr...  6.41 us
    ppermute x1, waiting for transfers between devices, gather_pieces(): held[first, 0] = lax.ppermute(column, AXES, on(first, 0))  6.17 us
    ppermute x1, waiting for transfers between devices, gather_pieces(): held[first, second] = lax.ppermute(held[first, 0], AXES, on(0, second))  5.85 us
    ppermute x3, waiting for transfers between devices, gather_pieces(): lax.ppermute(block, AXES, up(steps))  1.87 us
    ppermute x1, starting transfers between devices, gather_pieces(): held[first, 0] = lax.ppermute(column, AXES, on(first, 0))  1.56 us
    ppermute x4, waiting for transfers between devices, gather_pieces(): swapped = [lax.ppermute(piece, AXES, other) for piece in own]  1.52 us
    ppermute x1, starting transfers between devices, gather_pieces(): held[0, second] = lax.ppermute(column, AXES, on(0, second))  1.52 us
  transfers between devices with their start and end apart: 10, of which 4 were waited for; matrix products, arithmetic and copies ran while one was open for 0% of the time, Pallas kernels for 0%

profile of v1, /device:TPU:0, one launch (start us, length us, event | category | flops | bytes accessed | tf_op | source)
XLA Modules:
  0.0 37.1 jit_solution(9644447178596361812)
XLA Ops:
  0.0 0.0 copy-start.1
  0.0 0.8 %constant_dynamic-update-slice_fusion.1 = bf16[64,512]{1,0:T(8,128)(2,1)S(1)} fusion(bf16[64,256]{1,0:T(8,128)(2,1)} %param.4), kind=kLoop, calls=%fused_computation.2 | loop fusion | bytes 65536
  0.8 0.0 copy-done.1
  0.8 0.0 copy-start
  0.8 7.1 %collective-permute-start.2 = (bf16[64,512]{1,0:T(8,128)(2,1)S(1)}, bf16[64,512]{1,0:T(8,128)(2,1)S(1)}, u32[]{:S(2)}, u32[]{:S(2)}) collective-permute-start(bf16[64,512]{1,0:T(8,128)(2,1)S(1)} %constant_dynamic-update-slice_fusion), channel_id=1, source_target_pairs={{0,24},{1,25},{2,26},{3,27},{4,28},{5,29},{6,30},{7,31}} | collective-permute-start | bytes 196616 | tf_op jit(solution)/shard_map/ppermute | solution.py:71
  7.9 1.3 %collective-permute-start.1 = (bf16[64,512]{1,0:T(8,128)(2,1)S(1)}, bf16[64,512]{1,0:T(8,128)(2,1)S(1)}, u32[]{:S(2)}, u32[]{:S(2)}) collective-permute-start(bf16[64,512]{1,0:T(8,128)(2,1)S(1)} %constant_dynamic-update-slice_fusion), channel_id=1, source_target_pairs={{0,16},{1,17},{2,18},{3,19},{4,20},{5,21},{6,22},{7,23},{8,24},{9,... | collective-permute-start | bytes 196616 | tf_op jit(solution)/shard_map/ppermute | solution.py:71
  9.2 2.5 %collective-permute-start = (bf16[64,512]{1,0:T(8,128)(2,1)S(1)}, bf16[64,512]{1,0:T(8,128)(2,1)S(1)}, u32[]{:S(2)}, u32[]{:S(2)}) collective-permute-start(bf16[64,512]{1,0:T(8,128)(2,1)S(1)} %constant_dynamic-update-slice_fusion), channel_id=1, source_target_pairs={{0,8},{1,9},{2,10},{3,11},{4,12},{5,13},{6,14},{7,15},{8,16},{9,17... | collective-permute-start | bytes 196616 | tf_op jit(solution)/shard_map/ppermute | solution.py:71
  11.7 0.0 collective-permute-done.2
  11.7 0.0 collective-permute-done.1
  11.7 1.9 %collective-permute-done = bf16[64,512]{1,0:T(8,128)(2,1)S(1)} collective-permute-done((bf16[64,512]{1,0:T(8,128)(2,1)S(1)}, bf16[64,512]{1,0:T(8,128)(2,1)S(1)}, u32[]{:S(2)}, u32[]{:S(2)}) %collective-permute-start) | collective-permute-done | bytes 65568 | tf_op jit(solution)/shard_map/ppermute | solution.py:71
  13.6 1.6 %collective-permute-start.4 = (bf16[256,512]{1,0:T(8,128)(2,1)S(1)}, bf16[256,512]{1,0:T(8,128)(2,1)S(1)}, u32[]{:S(2)}, u32[]{:S(2)}) collective-permute-start(bf16[256,512]{1,0:T(8,128)(2,1)S(1)} %pad_maximum_fusion.refs_1_.refs_9_), channel_id=1, source_target_pairs={{0,1},{1,0},{2,6},{3,7},{4,5},{5,4},{6,2},{7,3},{8,9},{9,8},{10,14... | collective-permute-start | bytes 786440 | tf_op jit(solution)/shard_map/ppermute | solution.py:75
  15.1 1.5 %collective-permute-start.3 = (bf16[256,512]{1,0:T(8,128)(2,1)S(1)}, bf16[256,512]{1,0:T(8,128)(2,1)S(1)}, u32[]{:S(2)}, u32[]{:S(2)}) collective-permute-start(bf16[256,512]{1,0:T(8,128)(2,1)S(1)} %pad_maximum_fusion.refs_1_.refs_9_), channel_id=1, source_target_pairs={{0,4},{1,5},{2,3},{3,2},{4,0},{5,1},{6,7},{7,6},{8,12},{9,13},{10,... | collective-permute-start | bytes 786440 | tf_op jit(solution)/shard_map/ppermute | solution.py:77
  16.6 6.2 %collective-permute-done.4.refs_3_.refs_11_ = bf16[256,512]{1,0:T(8,128)(2,1)S(1)} collective-permute-done((bf16[256,512]{1,0:T(8,128)(2,1)S(1)}, bf16[256,512]{1,0:T(8,128)(2,1)S(1)}, u32[]{:S(2)}, u32[]{:S(2)}) %collective-permute-start.4) | collective-permute-done | bytes 262176 | tf_op jit(solution)/shard_map/ppermute | solution.py:75
  22.8 0.0 collective-permute-start.5
  22.8 0.0 collective-permute-start.6
  22.8 0.5 %collective-permute-start.8 = (bf16[256,512]{1,0:T(8,128)(2,1)S(1)}, bf16[256,512]{1,0:T(8,128)(2,1)S(1)}, u32[]{:S(2)}, u32[]{:S(2)}) collective-permute-start(bf16[256,512]{1,0:T(8,128)(2,1)S(1)} %collective-permute-done.4.refs_3_.refs_11_), channel_id=1, source_target_pairs={{0,2},{1,3},{2,0},{3,1},{4,6},{5,7},{6,4},{7,5},{8,10},{9,11},{10,... | collective-permute-start | bytes 786440 | tf_op jit(solution)/shard_map/ppermute | solution.py:83
  23.3 0.0 collective-permute-done.3.refs_2_.refs_10_
  23.3 0.0 collective-permute-start.7
  23.3 5.8 %collective-permute-done.5.refs_4_.refs_12_ = bf16[256,512]{1,0:T(8,128)(2,1)S(1)} collective-permute-done((bf16[256,512]{1,0:T(8,128)(2,1)S(1)}, bf16[256,512]{1,0:T(8,128)(2,1)S(1)}, u32[]{:S(2)}, u32[]{:S(2)}) %collective-permute-start.5) | collective-permute-done | bytes 262176 | tf_op jit(solution)/shard_map/ppermute | solution.py:80
  29.2 0.0 collective-permute-start.9
  29.2 0.0 collective-permute-done.6.refs_5_.refs_13_
  29.2 0.0 collective-permute-done.8.refs_7_.refs_15_
  29.2 0.0 collective-permute-done.7.refs_6_.refs_14_
  29.2 1.5 %collective-permute-done.9.refs_8_.refs_16_ = bf16[256,512]{1,0:T(8,128)(2,1)S(1)} collective-permute-done((bf16[256,512]{1,0:T(8,128)(2,1)S(1)}, bf16[256,512]{1,0:T(8,128)(2,1)S(1)}, u32[]{:S(2)}, u32[]{:S(2)}) %collective-permute-start.9) | collective-permute-done | bytes 262176 | tf_op jit(solution)/shard_map/ppermute | solution.py:83
  30.7 0.0 copy-done
  30.7 6.4 %shard_map.37 = bf16[64,2048]{1,0:T(8,128)(2,1)} custom-call(bf16[64,2048]{1,0:T(8,128)(2,1)S(1)} %copy-done, bf16[256,512]{1,0:T(8,128)(2,1)S(1)} %pad_maximum_fusion.refs_1_.refs_9_, bf16[256,512]{1,0:T(8,128)(2,1)S(1)} %collective-permute-done.3.refs_2_.refs_10_, bf16[256,512]{1,0:T(8,128)(2,1)S(1)} %collective-permute-done.4.refs_3_.refs_11_, ...), custom_call_target="tpu_custom_call" | custom-call | flops 1073741824 | bytes 2097152 | tf_op jit(solution)/shard_map/pallas_call | solution.py:141
  (2 shorter events, 0.0 us)
Async XLA Ops:
  0.0 0.8 %copy-start.1 = (bf16[64,256]{1,0:T(8,128)(2,1)S(1)}, bf16[64,256]{1,0:T(8,128)(2,1)}, u32[]{:S(2)}) copy-start(bf16[64,256]{1,0:T(8,128)(2,1)} %param.5) | copy-start | bytes 98308
  0.8 29.9 %copy-start = (bf16[64,2048]{1,0:T(8,128)(2,1)S(1)}, bf16[64,2048]{1,0:T(8,128)(2,1)}, u32[]{:S(2)}) copy-start(bf16[64,2048]{1,0:T(8,128)(2,1)} %refs_0_.1) | copy-start | bytes 786436
  0.8 10.9 %collective-permute-start.2 = (bf16[64,512]{1,0:T(8,128)(2,1)S(1)}, bf16[64,512]{1,0:T(8,128)(2,1)S(1)}, u32[]{:S(2)}, u32[]{:S(2)}) collective-permute-start(bf16[64,512]{1,0:T(8,128)(2,1)S(1)} %constant_dynamic-update-slice_fusion), channel_id=1, source_target_pairs={{0,24},{1,25},{2,26},{3,27},{4,28},{5,29},{6,30},{7,31}} | collective-permute-start | bytes 196616 | tf_op jit(solution)/shard_map/ppermute | solution.py:71
  7.9 3.8 %collective-permute-start.1 = (bf16[64,512]{1,0:T(8,128)(2,1)S(1)}, bf16[64,512]{1,0:T(8,128)(2,1)S(1)}, u32[]{:S(2)}, u32[]{:S(2)}) collective-permute-start(bf16[64,512]{1,0:T(8,128)(2,1)S(1)} %constant_dynamic-update-slice_fusion), channel_id=1, source_target_pairs={{0,16},{1,17},{2,18},{3,19},{4,20},{5,21},{6,22},{7,23},{8,24},{9,... | collective-permute-start | bytes 196616 | tf_op jit(solution)/shard_map/ppermute | solution.py:71
  9.2 4.4 %collective-permute-start = (bf16[64,512]{1,0:T(8,128)(2,1)S(1)}, bf16[64,512]{1,0:T(8,128)(2,1)S(1)}, u32[]{:S(2)}, u32[]{:S(2)}) collective-permute-start(bf16[64,512]{1,0:T(8,128)(2,1)S(1)} %constant_dynamic-update-slice_fusion), channel_id=1, source_target_pairs={{0,8},{1,9},{2,10},{3,11},{4,12},{5,13},{6,14},{7,15},{8,16},{9,17... | collective-permute-start | bytes 196616 | tf_op jit(solution)/shard_map/ppermute | solution.py:71
  13.6 9.2 %collective-permute-start.4 = (bf16[256,512]{1,0:T(8,128)(2,1)S(1)}, bf16[256,512]{1,0:T(8,128)(2,1)S(1)}, u32[]{:S(2)}, u32[]{:S(2)}) collective-permute-start(bf16[256,512]{1,0:T(8,128)(2,1)S(1)} %pad_maximum_fusion.refs_1_.refs_9_), channel_id=1, source_target_pairs={{0,1},{1,0},{2,6},{3,7},{4,5},{5,4},{6,2},{7,3},{8,9},{9,8},{10,14... | collective-permute-start | bytes 786440 | tf_op jit(solution)/shard_map/ppermute | solution.py:75
  15.1 8.2 %collective-permute-start.3 = (bf16[256,512]{1,0:T(8,128)(2,1)S(1)}, bf16[256,512]{1,0:T(8,128)(2,1)S(1)}, u32[]{:S(2)}, u32[]{:S(2)}) collective-permute-start(bf16[256,512]{1,0:T(8,128)(2,1)S(1)} %pad_maximum_fusion.refs_1_.refs_9_), channel_id=1, source_target_pairs={{0,4},{1,5},{2,3},{3,2},{4,0},{5,1},{6,7},{7,6},{8,12},{9,13},{10,... | collective-permute-start | bytes 786440 | tf_op jit(solution)/shard_map/ppermute | solution.py:77
  22.8 6.4 %collective-permute-start.5 = (bf16[256,512]{1,0:T(8,128)(2,1)S(1)}, bf16[256,512]{1,0:T(8,128)(2,1)S(1)}, u32[]{:S(2)}, u32[]{:S(2)}) collective-permute-start(bf16[256,512]{1,0:T(8,128)(2,1)S(1)} %collective-permute-done.4.refs_3_.refs_11_), channel_id=1, source_target_pairs={{0,4},{1,5},{2,3},{3,2},{4,0},{5,1},{6,7},{7,6},{8,12},{9,13},{10,... | collective-permute-start | bytes 786440 | tf_op jit(solution)/shard_map/ppermute | solution.py:80
  22.8 6.4 %collective-permute-start.6 = (bf16[256,512]{1,0:T(8,128)(2,1)S(1)}, bf16[256,512]{1,0:T(8,128)(2,1)S(1)}, u32[]{:S(2)}, u32[]{:S(2)}) collective-permute-start(bf16[256,512]{1,0:T(8,128)(2,1)S(1)} %pad_maximum_fusion.refs_1_.refs_9_), channel_id=1, source_target_pairs={{0,2},{1,3},{2,0},{3,1},{4,6},{5,7},{6,4},{7,5},{8,10},{9,11},{10,... | collective-permute-start | bytes 786440 | tf_op jit(solution)/shard_map/ppermute | solution.py:83
  22.8 6.4 %collective-permute-start.8 = (bf16[256,512]{1,0:T(8,128)(2,1)S(1)}, bf16[256,512]{1,0:T(8,128)(2,1)S(1)}, u32[]{:S(2)}, u32[]{:S(2)}) collective-permute-start(bf16[256,512]{1,0:T(8,128)(2,1)S(1)} %collective-permute-done.4.refs_3_.refs_11_), channel_id=1, source_target_pairs={{0,2},{1,3},{2,0},{3,1},{4,6},{5,7},{6,4},{7,5},{8,10},{9,11},{10,... | collective-permute-start | bytes 786440 | tf_op jit(solution)/shard_map/ppermute | solution.py:83
  23.3 5.9 %collective-permute-start.7 = (bf16[256,512]{1,0:T(8,128)(2,1)S(1)}, bf16[256,512]{1,0:T(8,128)(2,1)S(1)}, u32[]{:S(2)}, u32[]{:S(2)}) collective-permute-start(bf16[256,512]{1,0:T(8,128)(2,1)S(1)} %collective-permute-done.3.refs_2_.refs_10_), channel_id=1, source_target_pairs={{0,2},{1,3},{2,0},{3,1},{4,6},{5,7},{6,4},{7,5},{8,10},{9,11},{10,... | collective-permute-start | bytes 786440 | tf_op jit(solution)/shard_map/ppermute | solution.py:83
  29.2 1.5 %collective-permute-start.9 = (bf16[256,512]{1,0:T(8,128)(2,1)S(1)}, bf16[256,512]{1,0:T(8,128)(2,1)S(1)}, u32[]{:S(2)}, u32[]{:S(2)}) collective-permute-start(bf16[256,512]{1,0:T(8,128)(2,1)S(1)} %collective-permute-done.5.refs_4_.refs_12_), channel_id=1, source_target_pairs={{0,2},{1,3},{2,0},{3,1},{4,6},{5,7},{6,4},{7,5},{8,10},{9,11},{10,... | collective-permute-start | bytes 786440 | tf_op jit(solution)/shard_map/ppermute | solution.py:83

commit v2 on v1

v2 whole, which is shorter than its diff:
```python
import functools
import math

import jax
import jax.numpy as jnp
from jax import lax
from jax.experimental import pallas as pl
from jax.experimental.pallas import tpu as pltpu
from jax.sharding import PartitionSpec as P

HD = 128
AXES = ("ctx", "kvh")
CORES = 2
HIDDEN = -1e30


class Layout:
    def __init__(self, mesh_shape):
        ctx, self.across = mesh_shape["ctx"], mesh_shape["kvh"]
        self.lines = 2
        self.planes = ctx // (CORES * self.lines)
        self.size = ctx * self.across
        self.mixed = self.lines == self.across

    def split(self, rank):
        column = rank % self.across
        core = rank // self.across % CORES
        line = rank // (self.across * CORES) % self.lines
        plane = rank // (self.across * CORES * self.lines)
        return plane, line, core, column

    def join(self, plane, line, core, column):
        return ((plane * self.lines + line) * CORES + core) * self.across + column

    def partner(self, place, up=0, first=0, second=0, swap=0):
        plane, line, core, column = place
        if self.mixed:
            by_line = core * first + (1 - core) * second
            by_column = core * second + (1 - core) * first
        else:
            by_line, by_column = second, first
        return plane ^ up, line ^ by_line, core ^ swap, column ^ by_column

    def exchange(self, array, **steps):
        pairs = [(rank, self.join(*self.partner(self.split(rank), **steps))) for rank in range(self.size)]
        return lax.ppermute(array, AXES, pairs)

    def here(self):
        return lax.axis_index("ctx") * self.across + lax.axis_index("kvh")


def fold_kernel(layout, sources, rows, carried, last, *refs):
    refs = list(refs)
    query_ref = refs.pop(0)
    state_refs = [refs.pop(0) for _ in range(2)] if carried else None
    count = len(sources)
    key_refs, value_refs = refs[:count], refs[count : 2 * count]
    out_refs, score_ref = refs[2 * count : -1], refs[-1]
    rank = layout.here()
    place = layout.split(rank)
    heads = query_ref.shape[1] // HD
    query = jnp.concatenate([query_ref[:, h * HD : (h + 1) * HD] for h in range(heads)], axis=0)
    begin = 0
    spans = []
    for blocks, key_ref in zip(sources, key_refs, strict=True):
        width = key_ref.shape[0]
        along = lax.broadcasted_iota(jnp.int32, (1, width), 1)
        bias = jnp.zeros((1, width), jnp.float32)
        scores = lax.dot_general(
            query, key_ref[...], (((1,), (1,)), ((), ())), preferred_element_type=jnp.float32
        )
        for at, (up, first, second, swap) in enumerate(blocks):
            plane, line, core, column = place
            there = layout.partner((plane, line, core ^ swap, column), up=up, first=first, second=second)
            source = layout.join(*there)
            level = jnp.where(source > rank, jnp.float32(HIDDEN), jnp.float32(0.0))
            bias = jnp.where(along // rows == at, level, bias)
        scores = scores + bias
        for at, steps in enumerate(blocks):
            if steps == (0, 0, 0, 0):
                token = lax.broadcasted_iota(jnp.int32, scores.shape, 0) % rows
                key_at = lax.broadcasted_iota(jnp.int32, scores.shape, 1) - at * rows
                later = jnp.logical_and(key_at < rows, key_at > token)
                scores = jnp.where(jnp.logical_and(key_at >= 0, later), HIDDEN, scores)
        score_ref[:, begin : begin + width] = scores
        spans.append((begin, begin + width))
        begin += width
    scale = math.log2(math.e) / math.sqrt(HD)
    largest = jnp.max(score_ref[...], axis=1, keepdims=True) * scale
    if carried:
        summed_ref, stat_ref = state_refs
        largest_old = stat_ref[0, :, 0:1]
        largest = jnp.maximum(largest, largest_old)
        decay = jnp.exp2(largest_old - largest)
        totals = stat_ref[0, :, 1:2] * decay
        summed = summed_ref[0] * decay
    else:
        totals = jnp.zeros((heads * rows, 1), jnp.float32)
        summed = jnp.zeros((heads * rows, HD), jnp.float32)
    for (start, end), value_ref in zip(spans, value_refs, strict=True):
        weights = jnp.exp2(score_ref[:, start:end] * scale - largest)
        totals = totals + jnp.sum(weights, axis=1, keepdims=True)
        summed = summed + jnp.dot(
            weights.astype(jnp.bfloat16), value_ref[...], preferred_element_type=jnp.float32
        )
    if last:
        result = (summed / totals).astype(jnp.bfloat16)
        for h in range(heads):
            out_refs[0][:, h * HD : (h + 1) * HD] = result[h * rows : (h + 1) * rows]
    else:
        out_refs[0][0] = summed
        lane = lax.broadcasted_iota(jnp.int32, (heads * rows, HD), 1)
        out_refs[1][0] = jnp.where(lane == 0, largest, totals)


def fold(layout, queries, state, pieces, groups, last=False):
    rows, query_width = queries.shape
    per_group = query_width // groups
    tall = rows * per_group // HD
    arrays = [array for array, _ in pieces]
    tokens = sum(array.shape[0] for array in arrays)

    def spec(array, offset):
        return pl.BlockSpec((array.shape[0], HD), lambda g: (0, offset + g))

    row_spec = pl.BlockSpec((rows, per_group), lambda g: (0, g))
    state_spec = pl.BlockSpec((1, tall, HD), lambda g: (g, 0, 0))
    state_type = jax.ShapeDtypeStruct((groups, tall, HD), jnp.float32)
    carried = state is not None
    return pl.pallas_call(
        functools.partial(fold_kernel, layout, [blocks for _, blocks in pieces], rows, carried, last),
        grid=(groups,),
        in_specs=[row_spec]
        + [state_spec] * (2 if carried else 0)
        + [spec(array, 0) for array in arrays]
        + [spec(array, groups) for array in arrays],
        out_specs=row_spec if last else [state_spec] * 2,
        out_shape=jax.ShapeDtypeStruct(queries.shape, jnp.bfloat16) if last else [state_type] * 2,
        scratch_shapes=[pltpu.VMEM((tall, tokens), jnp.float32)],
        compiler_params=pltpu.CompilerParams(vmem_limit_bytes=32 * 1024 * 1024),
        cost_estimate=pl.CostEstimate(flops=0, bytes_accessed=0, transcendentals=0),
    )(queries, *(state or ()), *arrays, *arrays)


def solution(mesh):
    layout = Layout(dict(mesh.shape))

    def per_device(queries, keys, values):
        groups = keys.shape[1] // HD
        exchange = layout.exchange
        block = jnp.concatenate([keys, values], axis=1)
        ups = range(1, layout.planes)
        firsts = range(1, layout.lines if layout.mixed else layout.across)
        seconds = range(1, layout.lines)
        above_steps = [(up, 0, 0) for up in reversed(ups)]
        flat_steps = [(0, f, 0) for f in firsts] + [(0, 0, s) for s in seconds]
        flat_steps += [(0, f, s) for f in firsts for s in seconds]
        above, flat = lax.optimization_barrier(
            (
                [exchange(block, up=up) for up, _, _ in above_steps],
                [exchange(block, first=f, second=s) for _, f, s in flat_steps],
            )
        )
        above = jnp.concatenate(above, axis=0)
        flat_steps = [(0, 0, 0)] + flat_steps
        flat = jnp.concatenate([block] + flat, axis=0)

        def both(array, steps):
            return [
                (array, [(*at, 0) for at in steps]),
                (exchange(array, swap=1), [(*at, 1) for at in steps]),
            ]

        def shifted(f, s):
            return [(up, f, s) for up, _, _ in above_steps]

        by_first = {f: exchange(above, first=f) for f in firsts}
        by_second = {s: exchange(above, second=s) for s in seconds}
        state = fold(layout, queries, None, both(flat, flat_steps), groups)
        state = fold(layout, queries, state, both(above, above_steps), groups)
        by_first, state = lax.optimization_barrier((by_first, state))
        by_second, state = lax.optimization_barrier((by_second, state))
        corners = {(f, s): exchange(by_first[f], second=s) for f in firsts for s in seconds}
        sides = []
        for f in firsts:
            sides += both(by_first[f], shifted(f, 0))
        for s in seconds:
            sides += both(by_second[s], shifted(0, s))
        state = fold(layout, queries, state, sides, groups)
        corners, state = lax.optimization_barrier((corners, state))
        ends = []
        for (f, s), array in corners.items():
            ends += both(array, shifted(f, s))
        return fold(layout, queries, state, ends, groups, last=True)

    placed = P(AXES, None)
    return jax.shard_map(
        per_device, mesh=mesh, in_specs=(placed, placed, placed), out_specs=placed, check_vma=False
    )
```

time: 37.4 us -> 43.9 us (1.17)
  Pallas kernels: 6.41 us -> 20.7 us
  waiting for transfers between devices: 15.4 us -> 6.25 us
  starting transfers between devices: 14.4 us -> 15.9 us
    pallas_call x1 -> x4, Pallas kernels: 6.41 us -> 20.7 us  [fold(): pl.pallas_call(functools.partial(fold_kernel, layout, [blocks for _, bloc...]
    ppermute x10 -> x14, waiting for transfers between devices: 15.4 us -> 6.25 us  [exchange(): return lax.ppermute(array, AXES, pairs)]
    ppermute x10 -> x14, starting transfers between devices: 14.4 us -> 15.9 us  [exchange(): return lax.ppermute(array, AXES, pairs)]
  transfers between devices with their start and end apart: 10 -> 14, of which waited for: 4 -> 5; matrix products, arithmetic and copies ran while one was open for 0% -> 0% of each run, Pallas kernels for 0% -> 33%
where the time goes in v2:
time: 43.9 us; the launch traced here: 43.8 us
  Pallas kernels  20.7 us (47%)
  starting transfers between devices  15.9 us (36%)
  waiting for transfers between devices  6.25 us (14%)
  local copies, waits for them, and re-layouts  0.8 us (2%)
    pallas_call x4, Pallas kernels, fold(): pl.pallas_call(functools.partial(fold_kernel, layout, [blocks for _, bloc...  20.7 us
    ppermute x14, starting transfers between devices, exchange(): return lax.ppermute(array, AXES, pairs)  15.9 us
    ppermute x14, waiting for transfers between devices, exchange(): return lax.ppermute(array, AXES, pairs)  6.25 us
  transfers between devices with their start and end apart: 14, of which 5 were waited for; matrix products, arithmetic and copies ran while one was open for 0% of the time, Pallas kernels for 33%

profile of v2, /device:TPU:0, one launch (start us, length us, event | category | flops | bytes accessed | tf_op | source)
XLA Modules:
  0.0 43.8 jit_solution(231093455618235112)
XLA Ops:
  0.0 0.0 copy-start.1
  0.0 0.8 %constant_dynamic-update-slice_fusion.1 = bf16[64,512]{1,0:T(8,128)(2,1)S(1)} fusion(bf16[64,256]{1,0:T(8,128)(2,1)} %param.4), kind=kLoop, calls=%fused_computation.2 | loop fusion | bytes 65536
  0.8 0.0 copy-done.1
  0.8 4.0 %collective-permute-start.5 = (bf16[64,512]{1,0:T(8,128)(2,1)S(1)}, bf16[64,512]{1,0:T(8,128)(2,1)S(1)}, u32[]{:S(2)}, u32[]{:S(2)}) collective-permute-start(bf16[64,512]{1,0:T(8,128)(2,1)S(1)} %constant_dynamic-update-slice_fusion), channel_id=1, source_target_pairs={{0,5},{1,4},{2,7},{3,6},{4,1},{5,0},{6,3},{7,2},{8,13},{9,12},{10,... | collective-permute-start | bytes 196616 | tf_op jit(solution)/shard_map/ppermute | solution.py:46
  4.7 0.5 %collective-permute-start.4 = (bf16[64,512]{1,0:T(8,128)(2,1)S(1)}, bf16[64,512]{1,0:T(8,128)(2,1)S(1)}, u32[]{:S(2)}, u32[]{:S(2)}) collective-permute-start(bf16[64,512]{1,0:T(8,128)(2,1)S(1)} %constant_dynamic-update-slice_fusion), channel_id=1, source_target_pairs={{0,4},{1,5},{2,3},{3,2},{4,0},{5,1},{6,7},{7,6},{8,12},{9,13},{10,... | collective-permute-start | bytes 196616 | tf_op jit(solution)/shard_map/ppermute | solution.py:46
  5.2 0.1 collective-permute-start.3
  5.4 2.0 %collective-permute-start.2 = (bf16[64,512]{1,0:T(8,128)(2,1)S(1)}, bf16[64,512]{1,0:T(8,128)(2,1)S(1)}, u32[]{:S(2)}, u32[]{:S(2)}) collective-permute-start(bf16[64,512]{1,0:T(8,128)(2,1)S(1)} %constant_dynamic-update-slice_fusion), channel_id=1, source_target_pairs={{0,8},{1,9},{2,10},{3,11},{4,12},{5,13},{6,14},{7,15},{8,0},{9,1},... | collective-permute-start | bytes 196616 | tf_op jit(solution)/shard_map/ppermute | solution.py:46
  7.4 2.6 %collective-permute-start.1 = (bf16[64,512]{1,0:T(8,128)(2,1)S(1)}, bf16[64,512]{1,0:T(8,128)(2,1)S(1)}, u32[]{:S(2)}, u32[]{:S(2)}) collective-permute-start(bf16[64,512]{1,0:T(8,128)(2,1)S(1)} %constant_dynamic-update-slice_fusion), channel_id=1, source_target_pairs={{0,16},{1,17},{2,18},{3,19},{4,20},{5,21},{6,22},{7,23},{8,24},{9,... | collective-permute-start | bytes 196616 | tf_op jit(solution)/shard_map/ppermute | solution.py:46
  9.9 0.0 collective-permute-done.5
  10.0 1.7 %collective-permute-start = (bf16[64,512]{1,0:T(8,128)(2,1)S(1)}, bf16[64,512]{1,0:T(8,128)(2,1)S(1)}, u32[]{:S(2)}, u32[]{:S(2)}) collective-permute-start(bf16[64,512]{1,0:T(8,128)(2,1)S(1)} %constant_dynamic-update-slice_fusion), channel_id=1, source_target_pairs={{0,24},{1,25},{2,26},{3,27},{4,28},{5,29},{6,30},{7,31},{8,16},{9,... | collective-permute-start | bytes 196616 | tf_op jit(solution)/shard_map/ppermute | solution.py:46
  11.7 0.0 collective-permute-done.4
  11.7 0.0 collective-permute-done.3
  11.7 0.0 collective-permute-done.2
  11.7 2.2 %collective-permute-done.1 = bf16[64,512]{1,0:T(8,128)(2,1)S(1)} collective-permute-done((bf16[64,512]{1,0:T(8,128)(2,1)S(1)}, bf16[64,512]{1,0:T(8,128)(2,1)S(1)}, u32[]{:S(2)}, u32[]{:S(2)}) %collective-permute-start.1) | collective-permute-done | bytes 65568 | tf_op jit(solution)/shard_map/ppermute | solution.py:46
  13.9 2.1 %collective-permute-done = bf16[64,512]{1,0:T(8,128)(2,1)S(1)} collective-permute-done((bf16[64,512]{1,0:T(8,128)(2,1)S(1)}, bf16[64,512]{1,0:T(8,128)(2,1)S(1)}, u32[]{:S(2)}, u32[]{:S(2)}) %collective-permute-start) | collective-permute-done | bytes 65568 | tf_op jit(solution)/shard_map/ppermute | solution.py:46
  16.0 0.0 copy-start
  16.1 0.1 collective-permute-start.7
  16.2 0.5 %collective-permute-start.8 = (bf16[192,512]{1,0:T(8,128)(2,1)S(1)}, bf16[192,512]{1,0:T(8,128)(2,1)S(1)}, u32[]{:S(2)}, u32[]{:S(2)}) collective-permute-start(bf16[192,512]{1,0:T(8,128)(2,1)S(1)} %constant_dynamic-update-slice_fusion.2.refs_3_.refs_5_), channel_id=1, source_target_pairs={{0,2},{1,3},{2,0},{3,1},{4,6},{5,7},{6,4},{7,5},{8,10},{9,11},{10,... | collective-permute-start | bytes 589832 | tf_op jit(solution)/shard_map/ppermute | solution.py:46
  16.7 1.5 %collective-permute-start.6 = (bf16[192,512]{1,0:T(8,128)(2,1)S(1)}, bf16[192,512]{1,0:T(8,128)(2,1)S(1)}, u32[]{:S(2)}, u32[]{:S(2)}) collective-permute-start(bf16[192,512]{1,0:T(8,128)(2,1)S(1)} %constant_dynamic-update-slice_fusion.2.refs_3_.refs_5_), channel_id=1, source_target_pairs={{0,1},{1,0},{2,6},{3,7},{4,5},{5,4},{6,2},{7,3},{8,9},{9,8},{10,14... | collective-permute-start | bytes 589832 | tf_op jit(solution)/shard_map/ppermute | solution.py:46
  18.2 1.5 %collective-permute-start.10 = (bf16[192,512]{1,0:T(8,128)(2,1)S(1)}, bf16[192,512]{1,0:T(8,128)(2,1)S(1)}, u32[]{:S(2)}, u32[]{:S(2)}) collective-permute-start(bf16[192,512]{1,0:T(8,128)(2,1)S(1)} %constant_dynamic-update-slice_fusion.2.refs_3_.refs_5_), channel_id=1, source_target_pairs={{0,4},{1,5},{2,3},{3,2},{4,0},{5,1},{6,7},{7,6},{8,12},{9,13},{10,... | collective-permute-start | bytes 589832 | tf_op jit(solution)/shard_map/ppermute | solution.py:46
  19.7 0.0 collective-permute-done.7.refs_2_.refs_4_
  19.7 0.0 copy-done
  19.7 1.8 %shard_map.37 = (f32[2,512,128]{2,1,0:T(8,128)S(1)}, f32[2,512,128]{2,1,0:T(8,128)S(1)}) custom-call(bf16[64,2048]{1,0:T(8,128)(2,1)S(1)} %copy-done, bf16[256,512]{1,0:T(8,128)(2,1)S(1)} %pad_maximum_fusion.refs_1_.refs_3_, bf16[256,512]{1,0:T(8,128)(2,1)S(1)} %collective-permute-done.7.refs_2_.refs_4_, ...), custom_call_target="tpu_custom_call" | custom-call | tf_op jit(solution)/shard_map/pallas_call | solution.py:130
  21.5 0.0 collective-permute-done.8.refs_4_.refs_6_
  21.5 5.6 %shard_map.38 = (f32[2,512,128]{2,1,0:T(8,128)S(1)}, f32[2,512,128]{2,1,0:T(8,128)S(1)}) custom-call(bf16[64,2048]{1,0:T(8,128)(2,1)S(1)} %copy-done, f32[2,512,128]{2,1,0:T(8,128)S(1)} %get-tuple-element.32.refs_1_, f32[2,512,128]{2,1,0:T(8,128)S(1)} %get-tuple-element.33.refs_2_, bf16[192,512]{1,0:T(8,128)(2,1)S(1)} %constant_dynamic-update-slice_fusion.2.refs_3_.refs_5_, ...), custom_call_target="tpu_custom_call" | custom-call | tf_op jit(solution)/shard_map/pallas_call | solution.py:130
  27.2 0.0 collective-permute-done.6.refs_3_.refs_7_
  27.2 0.0 collective-permute-done.10.refs_5_.refs_9_
  27.2 0.1 collective-permute-start.12
  27.3 0.5 %collective-permute-start.11 = (bf16[192,512]{1,0:T(8,128)(2,1)S(1)}, bf16[192,512]{1,0:T(8,128)(2,1)S(1)}, u32[]{:S(2)}, u32[]{:S(2)}) collective-permute-start(bf16[192,512]{1,0:T(8,128)(2,1)S(1)} %collective-permute-done.6.refs_3_.refs_7_), channel_id=1, source_target_pairs={{0,2},{1,3},{2,0},{3,1},{4,6},{5,7},{6,4},{7,5},{8,10},{9,11},{10,... | collective-permute-start | bytes 589832 | tf_op jit(solution)/shard_map/ppermute | solution.py:46
  27.8 0.5 %collective-permute-start.9 = (bf16[192,512]{1,0:T(8,128)(2,1)S(1)}, bf16[192,512]{1,0:T(8,128)(2,1)S(1)}, u32[]{:S(2)}, u32[]{:S(2)}) collective-permute-start(bf16[192,512]{1,0:T(8,128)(2,1)S(1)} %collective-permute-done.6.refs_3_.refs_7_), channel_id=1, source_target_pairs={{0,4},{1,5},{2,3},{3,2},{4,0},{5,1},{6,7},{7,6},{8,12},{9,13},{10,... | collective-permute-start | bytes 589832 | tf_op jit(solution)/shard_map/ppermute | solution.py:46
  28.3 0.4 collective-permute-done.12.refs_6_.refs_10_
  28.7 0.3 collective-permute-done.11.refs_4_.refs_8_
  29.0 7.0 %shard_map.39 = (f32[2,512,128]{2,1,0:T(8,128)S(1)}, f32[2,512,128]{2,1,0:T(8,128)S(1)}) custom-call(bf16[64,2048]{1,0:T(8,128)(2,1)S(1)} %copy-done, f32[2,512,128]{2,1,0:T(8,128)S(1)} %get-tuple-element.39.refs_1_, f32[2,512,128]{2,1,0:T(8,128)S(1)} %get-tuple-element.40.refs_2_, bf16[192,512]{1,0:T(8,128)(2,1)S(1)} %collective-permute-done.6.refs_3_.refs_7_, ...), custom_call_target="tpu_custom_call" | custom-call | tf_op jit(solution)/shard_map/pallas_call | solution.py:130
  36.0 0.0 collective-permute-done.9.refs_3_.refs_5_
  36.0 0.3 collective-permute-start.13
  36.3 1.2 %collective-permute-done.13.refs_4_.refs_6_ = bf16[192,512]{1,0:T(8,128)(2,1)S(1)} collective-permute-done((bf16[192,512]{1,0:T(8,128)(2,1)S(1)}, bf16[192,512]{1,0:T(8,128)(2,1)S(1)}, u32[]{:S(2)}, u32[]{:S(2)}) %collective-permute-start.13) | collective-permute-done | bytes 196640 | tf_op jit(solution)/shard_map/ppermute | solution.py:46
  37.5 6.2 %shard_map.40 = bf16[64,2048]{1,0:T(8,128)(2,1)} custom-call(bf16[64,2048]{1,0:T(8,128)(2,1)S(1)} %copy-done, f32[2,512,128]{2,1,0:T(8,128)S(1)} %get-tuple-element.44.refs_1_, f32[2,512,128]{2,1,0:T(8,128)S(1)} %get-tuple-element.45.refs_2_, bf16[192,512]{1,0:T(8,128)(2,1)S(1)} %collective-permute-done.9.refs_3_.refs_5_, ...), custom_call_target="tpu_custom_call" | custom-call | tf_op jit(solution)/shard_map/pallas_call | solution.py:130
  (5 shorter events, 0.0 us)
Async XLA Ops:
  0.0 0.8 %copy-start.1 = (bf16[64,256]{1,0:T(8,128)(2,1)S(1)}, bf16[64,256]{1,0:T(8,128)(2,1)}, u32[]{:S(2)}) copy-start(bf16[64,256]{1,0:T(8,128)(2,1)} %param.5) | copy-start | bytes 98308
  0.8 9.2 %collective-permute-start.5 = (bf16[64,512]{1,0:T(8,128)(2,1)S(1)}, bf16[64,512]{1,0:T(8,128)(2,1)S(1)}, u32[]{:S(2)}, u32[]{:S(2)}) collective-permute-start(bf16[64,512]{1,0:T(8,128)(2,1)S(1)} %constant_dynamic-update-slice_fusion), channel_id=1, source_target_pairs={{0,5},{1,4},{2,7},{3,6},{4,1},{5,0},{6,3},{7,2},{8,13},{9,12},{10,... | collective-permute-start | bytes 196616 | tf_op jit(solution)/shard_map/ppermute | solution.py:46
  4.7 7.0 %collective-permute-start.4 = (bf16[64,512]{1,0:T(8,128)(2,1)S(1)}, bf16[64,512]{1,0:T(8,128)(2,1)S(1)}, u32[]{:S(2)}, u32[]{:S(2)}) collective-permute-start(bf16[64,512]{1,0:T(8,128)(2,1)S(1)} %constant_dynamic-update-slice_fusion), channel_id=1, source_target_pairs={{0,4},{1,5},{2,3},{3,2},{4,0},{5,1},{6,7},{7,6},{8,12},{9,13},{10,... | collective-permute-start | bytes 196616 | tf_op jit(solution)/shard_map/ppermute | solution.py:46
  5.2 6.4 %collective-permute-start.3 = (bf16[64,512]{1,0:T(8,128)(2,1)S(1)}, bf16[64,512]{1,0:T(8,128)(2,1)S(1)}, u32[]{:S(2)}, u32[]{:S(2)}) collective-permute-start(bf16[64,512]{1,0:T(8,128)(2,1)S(1)} %constant_dynamic-update-slice_fusion), channel_id=1, source_target_pairs={{0,1},{1,0},{2,6},{3,7},{4,5},{5,4},{6,2},{7,3},{8,9},{9,8},{10,14... | collective-permute-start | bytes 196616 | tf_op jit(solution)/shard_map/ppermute | solution.py:46
  5.4 6.3 %collective-permute-start.2 = (bf16[64,512]{1,0:T(8,128)(2,1)S(1)}, bf16[64,512]{1,0:T(8,128)(2,1)S(1)}, u32[]{:S(2)}, u32[]{:S(2)}) collective-permute-start(bf16[64,512]{1,0:T(8,128)(2,1)S(1)} %constant_dynamic-update-slice_fusion), channel_id=1, source_target_pairs={{0,8},{1,9},{2,10},{3,11},{4,12},{5,13},{6,14},{7,15},{8,0},{9,1},... | collective-permute-start | bytes 196616 | tf_op jit(solution)/shard_map/ppermute | solution.py:46
  7.4 6.6 %collective-permute-start.1 = (bf16[64,512]{1,0:T(8,128)(2,1)S(1)}, bf16[64,512]{1,0:T(8,128)(2,1)S(1)}, u32[]{:S(2)}, u32[]{:S(2)}) collective-permute-start(bf16[64,512]{1,0:T(8,128)(2,1)S(1)} %constant_dynamic-update-slice_fusion), channel_id=1, source_target_pairs={{0,16},{1,17},{2,18},{3,19},{4,20},{5,21},{6,22},{7,23},{8,24},{9,... | collective-permute-start | bytes 196616 | tf_op jit(solution)/shard_map/ppermute | solution.py:46
  10.0 6.1 %collective-permute-start = (bf16[64,512]{1,0:T(8,128)(2,1)S(1)}, bf16[64,512]{1,0:T(8,128)(2,1)S(1)}, u32[]{:S(2)}, u32[]{:S(2)}) collective-permute-start(bf16[64,512]{1,0:T(8,128)(2,1)S(1)} %constant_dynamic-update-slice_fusion), channel_id=1, source_target_pairs={{0,24},{1,25},{2,26},{3,27},{4,28},{5,29},{6,30},{7,31},{8,16},{9,... | collective-permute-start | bytes 196616 | tf_op jit(solution)/shard_map/ppermute | solution.py:46
  16.0 3.7 %copy-start = (bf16[64,2048]{1,0:T(8,128)(2,1)S(1)}, bf16[64,2048]{1,0:T(8,128)(2,1)}, u32[]{:S(2)}) copy-start(bf16[64,2048]{1,0:T(8,128)(2,1)} %refs_0_.7) | copy-start | bytes 786436
  16.1 3.7 %collective-permute-start.7 = (bf16[256,512]{1,0:T(8,128)(2,1)S(1)}, bf16[256,512]{1,0:T(8,128)(2,1)S(1)}, u32[]{:S(2)}, u32[]{:S(2)}) collective-permute-start(bf16[256,512]{1,0:T(8,128)(2,1)S(1)} %pad_maximum_fusion.refs_1_.refs_3_), channel_id=1, source_target_pairs={{0,2},{1,3},{2,0},{3,1},{4,6},{5,7},{6,4},{7,5},{8,10},{9,11},{10,... | collective-permute-start | bytes 786440 | tf_op jit(solution)/shard_map/ppermute | solution.py:46
  16.2 5.4 %collective-permute-start.8 = (bf16[192,512]{1,0:T(8,128)(2,1)S(1)}, bf16[192,512]{1,0:T(8,128)(2,1)S(1)}, u32[]{:S(2)}, u32[]{:S(2)}) collective-permute-start(bf16[192,512]{1,0:T(8,128)(2,1)S(1)} %constant_dynamic-update-slice_fusion.2.refs_3_.refs_5_), channel_id=1, source_target_pairs={{0,2},{1,3},{2,0},{3,1},{4,6},{5,7},{6,4},{7,5},{8,10},{9,11},{10,... | collective-permute-start | bytes 589832 | tf_op jit(solution)/shard_map/ppermute | solution.py:46
  16.7 10.4 %collective-permute-start.6 = (bf16[192,512]{1,0:T(8,128)(2,1)S(1)}, bf16[192,512]{1,0:T(8,128)(2,1)S(1)}, u32[]{:S(2)}, u32[]{:S(2)}) collective-permute-start(bf16[192,512]{1,0:T(8,128)(2,1)S(1)} %constant_dynamic-update-slice_fusion.2.refs_3_.refs_5_), channel_id=1, source_target_pairs={{0,1},{1,0},{2,6},{3,7},{4,5},{5,4},{6,2},{7,3},{8,9},{9,8},{10,14... | collective-permute-start | bytes 589832 | tf_op jit(solution)/shard_map/ppermute | solution.py:46
  18.2 9.0 %collective-permute-start.10 = (bf16[192,512]{1,0:T(8,128)(2,1)S(1)}, bf16[192,512]{1,0:T(8,128)(2,1)S(1)}, u32[]{:S(2)}, u32[]{:S(2)}) collective-permute-start(bf16[192,512]{1,0:T(8,128)(2,1)S(1)} %constant_dynamic-update-slice_fusion.2.refs_3_.refs_5_), channel_id=1, source_target_pairs={{0,4},{1,5},{2,3},{3,2},{4,0},{5,1},{6,7},{7,6},{8,12},{9,13},{10,... | collective-permute-start | bytes 589832 | tf_op jit(solution)/shard_map/ppermute | solution.py:46
  27.2 1.5 %collective-permute-start.12 = (bf16[192,512]{1,0:T(8,128)(2,1)S(1)}, bf16[192,512]{1,0:T(8,128)(2,1)S(1)}, u32[]{:S(2)}, u32[]{:S(2)}) collective-permute-start(bf16[192,512]{1,0:T(8,128)(2,1)S(1)} %collective-permute-done.10.refs_5_.refs_9_), channel_id=1, source_target_pairs={{0,2},{1,3},{2,0},{3,1},{4,6},{5,7},{6,4},{7,5},{8,10},{9,11},{10,... | collective-permute-start | bytes 589832 | tf_op jit(solution)/shard_map/ppermute | solution.py:46
  27.3 1.7 %collective-permute-start.11 = (bf16[192,512]{1,0:T(8,128)(2,1)S(1)}, bf16[192,512]{1,0:T(8,128)(2,1)S(1)}, u32[]{:S(2)}, u32[]{:S(2)}) collective-permute-start(bf16[192,512]{1,0:T(8,128)(2,1)S(1)} %collective-permute-done.6.refs_3_.refs_7_), channel_id=1, source_target_pairs={{0,2},{1,3},{2,0},{3,1},{4,6},{5,7},{6,4},{7,5},{8,10},{9,11},{10,... | collective-permute-start | bytes 589832 | tf_op jit(solution)/shard_map/ppermute | solution.py:46
  27.8 8.3 %collective-permute-start.9 = (bf16[192,512]{1,0:T(8,128)(2,1)S(1)}, bf16[192,512]{1,0:T(8,128)(2,1)S(1)}, u32[]{:S(2)}, u32[]{:S(2)}) collective-permute-start(bf16[192,512]{1,0:T(8,128)(2,1)S(1)} %collective-permute-done.6.refs_3_.refs_7_), channel_id=1, source_target_pairs={{0,4},{1,5},{2,3},{3,2},{4,0},{5,1},{6,7},{7,6},{8,12},{9,13},{10,... | collective-permute-start | bytes 589832 | tf_op jit(solution)/shard_map/ppermute | solution.py:46
  36.0 1.5 %collective-permute-start.13 = (bf16[192,512]{1,0:T(8,128)(2,1)S(1)}, bf16[192,512]{1,0:T(8,128)(2,1)S(1)}, u32[]{:S(2)}, u32[]{:S(2)}) collective-permute-start(bf16[192,512]{1,0:T(8,128)(2,1)S(1)} %collective-permute-done.9.refs_3_.refs_5_), channel_id=1, source_target_pairs={{0,2},{1,3},{2,0},{3,1},{4,6},{5,7},{6,4},{7,5},{8,10},{9,11},{10,... | collective-permute-start | bytes 589832 | tf_op jit(solution)/shard_map/ppermute | solution.py:46

commit v3 on v1

v3 whole, which is shorter than its diff:
```python
import functools
import math

import jax
import jax.numpy as jnp
from jax import lax
from jax.experimental import pallas as pl
from jax.experimental.pallas import tpu as pltpu
from jax.sharding import PartitionSpec as P

HD = 128
AXES = ("ctx", "kvh")
CORES = 2
HIDDEN = -1e30


class Layout:
    def __init__(self, mesh_shape):
        ctx, self.across = mesh_shape["ctx"], mesh_shape["kvh"]
        self.lines = 2
        self.planes = ctx // (CORES * self.lines)
        self.size = ctx * self.across

    def split(self, rank):
        column = rank % self.across
        core = rank // self.across % CORES
        line = rank // (self.across * CORES) % self.lines
        plane = rank // (self.across * CORES * self.lines)
        return plane, line, core, column

    def join(self, plane, line, core, column):
        return ((plane * self.lines + line) * CORES + core) * self.across + column

    def partner(self, rank, up=0, line=0, swap=0, column=0):
        place = self.split(rank)
        return self.join(place[0] ^ up, place[1] ^ line, place[2] ^ swap, place[3] ^ column)

    def exchange(self, array, **steps):
        return lax.ppermute(array, AXES, [(rank, self.partner(rank, **steps)) for rank in range(self.size)])

    def here(self):
        return lax.axis_index("ctx") * self.across + lax.axis_index("kvh")


def fold_kernel(layout, sources, rows, groups, carried, last, *refs):
    refs = list(refs)
    query_ref = refs.pop(0)
    state_refs = [refs.pop(0) for _ in range(3)] if carried else None
    piece_refs, refs = refs[: len(sources)], refs[len(sources) :]
    out_refs, (score_ref, weight_ref) = refs[:-2], refs[-2:]
    blocks = [steps for piece in sources for steps in piece]
    width = len(blocks) * rows
    heads = query_ref.shape[1] // (groups * HD)
    tall = heads * rows
    scale = math.log2(math.e) / math.sqrt(HD)

    rank = layout.here()
    along = lax.broadcasted_iota(jnp.int32, (1, width), 1)
    bias = jnp.zeros((1, width), jnp.float32)
    for at, (up, line, swap, column) in enumerate(blocks):
        hidden = layout.partner(rank, up, line, swap, column) > rank
        bias = jnp.where(along // rows == at, jnp.where(hidden, HIDDEN, 0.0).astype(jnp.float32), bias)
    own = blocks.index((0, 0, 0, 0)) * rows if (0, 0, 0, 0) in blocks else None
    if own is not None:
        token = lax.broadcasted_iota(jnp.int32, (rows, width), 0)
        place = lax.broadcasted_iota(jnp.int32, (rows, width), 1) - own
        later = jnp.logical_and(place < rows, place > token)
        bias = jnp.where(jnp.logical_and(place >= 0, later), HIDDEN, bias)

    for group in range(groups):
        first = group * heads * HD
        query = jnp.concatenate([query_ref[:, first + h * HD : first + (h + 1) * HD] for h in range(heads)], axis=0)
        at = group * HD
        key = jnp.concatenate([ref[:, at : at + HD] for ref in piece_refs], axis=0)
        at = (groups + group) * HD
        value = jnp.concatenate([ref[:, at : at + HD] for ref in piece_refs], axis=0)
        score_ref[...] = lax.dot_general(
            query, key, (((1,), (1,)), ((), ())), preferred_element_type=jnp.float32
        )
        tops, sums = [], []
        for begin in range(0, tall, rows):
            scores = score_ref[begin : begin + rows, :] * scale + bias
            top = jnp.broadcast_to(jnp.max(scores, axis=1, keepdims=True), (rows, HD))
            if carried:
                top = jnp.maximum(top, state_refs[0][group, begin : begin + rows])
            total = jnp.zeros((rows, HD), jnp.float32)
            rest = jnp.zeros((rows, 1), jnp.float32)
            for left in range(0, width, HD):
                part = min(HD, width - left)
                weights = jnp.exp2(scores[:, left : left + part] - top[:, :part])
                if part == HD:
                    total = total + weights
                else:
                    rest = jnp.sum(weights, axis=1, keepdims=True)
                weight_ref[begin : begin + rows, left : left + part] = weights.astype(jnp.bfloat16)
            tops.append(top)
            sums.append(jnp.broadcast_to(jnp.sum(total, axis=1, keepdims=True) + rest, (rows, HD)))
        largest, totals = jnp.concatenate(tops, axis=0), jnp.concatenate(sums, axis=0)
        summed = jnp.dot(weight_ref[...], value, preferred_element_type=jnp.float32)
        if carried:
            decay = jnp.exp2(state_refs[0][group] - largest)
            totals = totals + state_refs[1][group] * decay
            summed = summed + state_refs[2][group] * decay
        if last:
            result = (summed / totals).astype(jnp.bfloat16)
            for h in range(heads):
                out_refs[0][:, first + h * HD : first + (h + 1) * HD] = result[h * rows : (h + 1) * rows]
        else:
            for ref, array in zip(out_refs, (largest, totals, summed), strict=True):
                ref[group] = array


def fold(layout, queries, state, pieces, groups, last=False):
    rows, query_width = queries.shape
    tall = rows * query_width // (groups * HD)
    arrays = [array for array, _ in pieces]
    tokens = sum(array.shape[0] for array in arrays)
    carried = state is not None
    state_type = jax.ShapeDtypeStruct((groups, tall, HD), jnp.float32)
    whole = pl.BlockSpec(memory_space=pltpu.VMEM)
    return pl.pallas_call(
        functools.partial(
            fold_kernel, layout, [blocks for _, blocks in pieces], rows, groups, carried, last
        ),
        in_specs=[whole] * (1 + 3 * carried + len(arrays)),
        out_specs=whole if last else [whole] * 3,
        out_shape=jax.ShapeDtypeStruct(queries.shape, jnp.bfloat16) if last else [state_type] * 3,
        scratch_shapes=[pltpu.VMEM((tall, tokens), jnp.float32), pltpu.VMEM((tall, tokens), jnp.bfloat16)],
        compiler_params=pltpu.CompilerParams(vmem_limit_bytes=24 * 1024 * 1024),
        cost_estimate=pl.CostEstimate(flops=0, bytes_accessed=0, transcendentals=0),
    )(queries, *(state or ()), *arrays)


def solution(mesh):
    layout = Layout(dict(mesh.shape))

    def per_device(queries, keys, values):
        groups = keys.shape[1] // HD
        exchange = layout.exchange
        block = jnp.concatenate([keys, values], axis=1)
        ups = range(1, layout.planes)
        lines = range(1, layout.lines)
        columns = range(1, layout.across)
        corners = [(0, l, 0, c) for l in lines for c in columns]

        def go(array, steps):
            return exchange(array, up=steps[0], line=steps[1], swap=steps[2], column=steps[3])

        def join(arrays):
            return jnp.concatenate(arrays, axis=0) if len(arrays) > 1 else arrays[0]

        def moved(steps, by):
            return [tuple(a ^ b for a, b in zip(one, by, strict=True)) for one in steps]

        def swapped(pieces):
            return [(exchange(array, swap=1), moved(steps, (0, 0, 1, 0))) for array, steps in pieces]

        corner = join([go(block, steps) for steps in corners])
        above_steps = [(up, 0, 0, 0) for up in reversed(ups)]
        above = join([go(block, steps) for steps in above_steps])
        side_steps = [(0, l, 0, 0) for l in lines] + [(0, 0, 0, c) for c in columns]
        flat = join([block] + [go(block, steps) for steps in side_steps] + [corner])
        flat_steps = [(0, 0, 0, 0)] + side_steps + corners
        far = [go(corner, steps) for steps in above_steps]
        sides = [go(above, steps) for steps in side_steps]

        near = [(flat, flat_steps), (above, above_steps)]
        state = fold(layout, queries, None, near + swapped(near), groups)
        (far, sides), state = lax.optimization_barrier(((far, sides), state))
        later = [(array, moved(above_steps, steps)) for array, steps in zip(sides, side_steps, strict=True)]
        later.append((join(far), [step for steps in above_steps for step in moved(corners, steps)]))
        others = swapped(later)
        state = fold(layout, queries, state, later, groups)
        return fold(layout, queries, state, others, groups, last=True)

    placed = P(AXES, None)
    return jax.shard_map(
        per_device, mesh=mesh, in_specs=(placed, placed, placed), out_specs=placed, check_vma=False
    )
```

time: 37.4 us -> 32.5 us (0.87)
  waiting for transfers between devices: 15.4 us -> 7.65 us
  starting transfers between devices: 14.4 us -> 17.6 us
  Pallas kernels: 6.41 us -> 6.02 us
    ppermute x10 -> x16, waiting for transfers between devices: 15.4 us -> 7.65 us  [exchange(): lax.ppermute(array, AXES, [(rank, self.partner(rank, **steps)) for rank i...]
    ppermute x10 -> x16, starting transfers between devices: 14.4 us -> 17.6 us  [exchange(): lax.ppermute(array, AXES, [(rank, self.partner(rank, **steps)) for rank i...]
    pallas_call x1 -> x3, Pallas kernels: 6.41 us -> 6.02 us  [fold(): pl.pallas_call(functools.partial(fold_kernel, layout, [blocks for _, bloc...]
    unnamed x5 -> x9, local copies, waits for them, and re-layouts: 0.78 us -> 0.8 us
  transfers between devices with their start and end apart: 10 -> 16, of which waited for: 4 -> 3; matrix products, arithmetic and copies ran while one was open for 0% -> 0% of each run, Pallas kernels for 0% -> 11%
where the time goes in v3:
time: 32.5 us; the launch traced here: 32.3 us
  starting transfers between devices  17.6 us (54%)
  waiting for transfers between devices  7.65 us (24%)
  Pallas kernels  6.02 us (19%)
  local copies, waits for them, and re-layouts  0.82 us (3%)
    ppermute x16, starting transfers between devices, exchange(): lax.ppermute(array, AXES, [(rank, self.partner(rank, **steps)) for rank i...  17.6 us
    ppermute x16, waiting for transfers between devices, exchange(): lax.ppermute(array, AXES, [(rank, self.partner(rank, **steps)) for rank i...  7.65 us
    pallas_call x3, Pallas kernels, fold(): pl.pallas_call(functools.partial(fold_kernel, layout, [blocks for _, bloc...  6.02 us
    unnamed x9, local copies, waits for them, and re-layouts  0.8 us
  transfers between devices with their start and end apart: 16, of which 3 were waited for; matrix products, arithmetic and copies ran while one was open for 0% of the time, Pallas kernels for 11%

profile of v3, /device:TPU:0, one launch (start us, length us, event | category | flops | bytes accessed | tf_op | source)
XLA Modules:
  0.0 32.3 jit_solution(382545339506065148)
XLA Ops:
  0.0 0.0 copy-start.1
  0.0 0.8 %constant_dynamic-update-slice_fusion.1 = bf16[64,512]{1,0:T(8,128)(2,1)S(1)} fusion(bf16[64,256]{1,0:T(8,128)(2,1)} %param.4), kind=kLoop, calls=%fused_computation.2 | loop fusion | bytes 65536
  0.8 0.0 copy-done.1
  0.8 3.0 %collective-permute-start.10 = (bf16[64,512]{1,0:T(8,128)(2,1)S(1)}, bf16[64,512]{1,0:T(8,128)(2,1)S(1)}, u32[]{:S(2)}, u32[]{:S(2)}) collective-permute-start(bf16[64,512]{1,0:T(8,128)(2,1)S(1)} %constant_dynamic-update-slice_fusion), channel_id=1, source_target_pairs={{0,1},{1,0},{2,3},{3,2},{4,5},{5,4},{6,7},{7,6},{8,9},{9,8},{10,11... | collective-permute-start | bytes 196616 | tf_op jit(solution)/shard_map/ppermute | solution.py:39
  3.8 1.5 %collective-permute-start.9 = (bf16[64,512]{1,0:T(8,128)(2,1)S(1)}, bf16[64,512]{1,0:T(8,128)(2,1)S(1)}, u32[]{:S(2)}, u32[]{:S(2)}) collective-permute-start(bf16[64,512]{1,0:T(8,128)(2,1)S(1)} %constant_dynamic-update-slice_fusion), channel_id=1, source_target_pairs={{0,4},{1,5},{2,6},{3,7},{4,0},{5,1},{6,2},{7,3},{8,12},{9,13},{10,... | collective-permute-start | bytes 196616 | tf_op jit(solution)/shard_map/ppermute | solution.py:39
  5.3 0.0 collective-permute-start
  5.3 2.0 %collective-permute-start.6 = (bf16[64,512]{1,0:T(8,128)(2,1)S(1)}, bf16[64,512]{1,0:T(8,128)(2,1)S(1)}, u32[]{:S(2)}, u32[]{:S(2)}) collective-permute-start(bf16[64,512]{1,0:T(8,128)(2,1)S(1)} %constant_dynamic-update-slice_fusion), channel_id=1, source_target_pairs={{0,8},{1,9},{2,10},{3,11},{4,12},{5,13},{6,14},{7,15},{8,0},{9,1},... | collective-permute-start | bytes 196616 | tf_op jit(solution)/shard_map/ppermute | solution.py:39
  7.4 2.6 %collective-permute-start.5 = (bf16[64,512]{1,0:T(8,128)(2,1)S(1)}, bf16[64,512]{1,0:T(8,128)(2,1)S(1)}, u32[]{:S(2)}, u32[]{:S(2)}) collective-permute-start(bf16[64,512]{1,0:T(8,128)(2,1)S(1)} %constant_dynamic-update-slice_fusion), channel_id=1, source_target_pairs={{0,16},{1,17},{2,18},{3,19},{4,20},{5,21},{6,22},{7,23},{8,24},{9,... | collective-permute-start | bytes 196616 | tf_op jit(solution)/shard_map/ppermute | solution.py:39
  9.9 0.0 collective-permute-done.10
  10.0 0.2 collective-permute-start.4
  10.2 0.0 collective-permute-done.9
  10.2 0.3 collective-permute-done
  10.5 0.0 copy-start
  10.5 0.1 collective-permute-start.11
  10.6 5.4 %collective-permute-done.4 = bf16[64,512]{1,0:T(8,128)(2,1)S(1)} collective-permute-done((bf16[64,512]{1,0:T(8,128)(2,1)S(1)}, bf16[64,512]{1,0:T(8,128)(2,1)S(1)}, u32[]{:S(2)}, u32[]{:S(2)}) %collective-permute-start.4) | collective-permute-done | bytes 65568 | tf_op jit(solution)/shard_map/ppermute | solution.py:39
  16.0 0.0 collective-permute-done.5
  16.0 0.0 collective-permute-done.6
  16.1 0.1 collective-permute-start.12
  16.1 1.6 %collective-permute-start.8 = (bf16[192,512]{1,0:T(8,128)(2,1)S(1)}, bf16[192,512]{1,0:T(8,128)(2,1)S(1)}, u32[]{:S(2)}, u32[]{:S(2)}) collective-permute-start(bf16[192,512]{1,0:T(8,128)(2,1)S(1)} %constant_dynamic-update-slice_fusion.2.refs_2_), channel_id=1, source_target_pairs={{0,1},{1,0},{2,3},{3,2},{4,5},{5,4},{6,7},{7,6},{8,9},{9,8},{10,11... | collective-permute-start | bytes 589832 | tf_op jit(solution)/shard_map/ppermute | solution.py:39
  17.7 1.5 %collective-permute-start.7 = (bf16[192,512]{1,0:T(8,128)(2,1)S(1)}, bf16[192,512]{1,0:T(8,128)(2,1)S(1)}, u32[]{:S(2)}, u32[]{:S(2)}) collective-permute-start(bf16[192,512]{1,0:T(8,128)(2,1)S(1)} %constant_dynamic-update-slice_fusion.2.refs_2_), channel_id=1, source_target_pairs={{0,4},{1,5},{2,6},{3,7},{4,0},{5,1},{6,2},{7,3},{8,12},{9,13},{10,... | collective-permute-start | bytes 589832 | tf_op jit(solution)/shard_map/ppermute | solution.py:39
  19.2 0.0 collective-permute-start.3
  19.2 0.0 collective-permute-done.12.refs_4_
  19.2 1.5 %collective-permute-start.2 = (bf16[64,512]{1,0:T(8,128)(2,1)S(1)}, bf16[64,512]{1,0:T(8,128)(2,1)S(1)}, u32[]{:S(2)}, u32[]{:S(2)}) collective-permute-start(bf16[64,512]{1,0:T(8,128)(2,1)S(1)} %collective-permute-done), channel_id=1, source_target_pairs={{0,16},{1,17},{2,18},{3,19},{4,20},{5,21},{6,22},{7,23},{8,24},{9,... | collective-permute-start | bytes 196616 | tf_op jit(solution)/shard_map/ppermute | solution.py:39
  20.7 0.0 collective-permute-done.11.refs_3_
  20.7 2.9 %collective-permute-start.1 = (bf16[64,512]{1,0:T(8,128)(2,1)S(1)}, bf16[64,512]{1,0:T(8,128)(2,1)S(1)}, u32[]{:S(2)}, u32[]{:S(2)}) collective-permute-start(bf16[64,512]{1,0:T(8,128)(2,1)S(1)} %collective-permute-done), channel_id=1, source_target_pairs={{0,24},{1,25},{2,26},{3,27},{4,28},{5,29},{6,30},{7,31},{8,16},{9,... | collective-permute-start | bytes 196616 | tf_op jit(solution)/shard_map/ppermute | solution.py:39
  23.6 0.0 copy-done
  23.6 2.1 %shard_map.37 = (f32[2,512,128]{2,1,0:T(8,128)S(1)}, f32[2,512,128]{2,1,0:T(8,128)S(1)}, f32[2,512,128]{2,1,0:T(8,128)S(1)}) custom-call(bf16[64,2048]{1,0:T(8,128)(2,1)S(1)} %copy-done, bf16[256,512]{1,0:T(8,128)(2,1)S(1)} %pad_maximum_fusion.refs_1_, bf16[192,512]{1,0:T(8,128)(2,1)S(1)} %constant_dynamic-update-slice_fusion.2.refs_2_, ...), custom_call_target="tpu_custom_call" | custom-call | tf_op jit(solution)/shard_map/pallas_call | solution.py:121
  25.7 0.0 collective-permute-done.3
  25.7 1.9 %collective-permute-done.2 = bf16[64,512]{1,0:T(8,128)(2,1)S(1)} collective-permute-done((bf16[64,512]{1,0:T(8,128)(2,1)S(1)}, bf16[64,512]{1,0:T(8,128)(2,1)S(1)}, u32[]{:S(2)}, u32[]{:S(2)}) %collective-permute-start.2) | collective-permute-done | bytes 65568 | tf_op jit(solution)/shard_map/ppermute | solution.py:39
  27.6 0.0 collective-permute-done.1
  27.6 0.0 collective-permute-done.8.refs_5_
  27.6 0.0 collective-permute-done.7.refs_4_
  27.6 0.1 collective-permute-start.15
  27.7 0.5 %collective-permute-start.13 = (bf16[192,512]{1,0:T(8,128)(2,1)S(1)}, bf16[192,512]{1,0:T(8,128)(2,1)S(1)}, u32[]{:S(2)}, u32[]{:S(2)}) collective-permute-start(bf16[192,512]{1,0:T(8,128)(2,1)S(1)} %collective-permute-done.7.refs_4_), channel_id=1, source_target_pairs={{0,2},{1,3},{2,0},{3,1},{4,6},{5,7},{6,4},{7,5},{8,10},{9,11},{10,... | collective-permute-start | bytes 589832 | tf_op jit(solution)/shard_map/ppermute | solution.py:39
  28.2 0.1 collective-permute-start.14
  28.3 1.6 %shard_map.38 = (f32[2,512,128]{2,1,0:T(8,128)S(1)}, f32[2,512,128]{2,1,0:T(8,128)S(1)}, f32[2,512,128]{2,1,0:T(8,128)S(1)}) custom-call(bf16[64,2048]{1,0:T(8,128)(2,1)S(1)} %copy-done, f32[2,512,128]{2,1,0:T(8,128)S(1)} %get-tuple-element.22.refs_1_, f32[2,512,128]{2,1,0:T(8,128)S(1)} %get-tuple-element.23.refs_2_, ...), custom_call_target="tpu_custom_call" | custom-call | tf_op jit(solution)/shard_map/pallas_call | solution.py:121
  29.9 0.0 collective-permute-done.15.refs_6_
  29.9 0.0 collective-permute-done.13.refs_4_
  29.9 0.0 collective-permute-done.14.refs_5_
  30.0 2.3 %shard_map.39 = bf16[64,2048]{1,0:T(8,128)(2,1)} custom-call(bf16[64,2048]{1,0:T(8,128)(2,1)S(1)} %copy-done, f32[2,512,128]{2,1,0:T(8,128)S(1)} %get-tuple-element.30.refs_1_, f32[2,512,128]{2,1,0:T(8,128)S(1)} %get-tuple-element.31.refs_2_, f32[2,512,128]{2,1,0:T(8,128)S(1)} %get-tuple-element.32.refs_3_, ...), custom_call_target="tpu_custom_call" | custom-call | tf_op jit(solution)/shard_map/pallas_call | solution.py:121
  (8 shorter events, 0.1 us)
Async XLA Ops:
  0.0 0.8 %copy-start.1 = (bf16[64,256]{1,0:T(8,128)(2,1)S(1)}, bf16[64,256]{1,0:T(8,128)(2,1)}, u32[]{:S(2)}) copy-start(bf16[64,256]{1,0:T(8,128)(2,1)} %param.5) | copy-start | bytes 98308
  0.8 9.2 %collective-permute-start.10 = (bf16[64,512]{1,0:T(8,128)(2,1)S(1)}, bf16[64,512]{1,0:T(8,128)(2,1)S(1)}, u32[]{:S(2)}, u32[]{:S(2)}) collective-permute-start(bf16[64,512]{1,0:T(8,128)(2,1)S(1)} %constant_dynamic-update-slice_fusion), channel_id=1, source_target_pairs={{0,1},{1,0},{2,3},{3,2},{4,5},{5,4},{6,7},{7,6},{8,9},{9,8},{10,11... | collective-permute-start | bytes 196616 | tf_op jit(solution)/shard_map/ppermute | solution.py:39
  3.8 6.4 %collective-permute-start.9 = (bf16[64,512]{1,0:T(8,128)(2,1)S(1)}, bf16[64,512]{1,0:T(8,128)(2,1)S(1)}, u32[]{:S(2)}, u32[]{:S(2)}) collective-permute-start(bf16[64,512]{1,0:T(8,128)(2,1)S(1)} %constant_dynamic-update-slice_fusion), channel_id=1, source_target_pairs={{0,4},{1,5},{2,6},{3,7},{4,0},{5,1},{6,2},{7,3},{8,12},{9,13},{10,... | collective-permute-start | bytes 196616 | tf_op jit(solution)/shard_map/ppermute | solution.py:39
  5.3 5.2 %collective-permute-start = (bf16[64,512]{1,0:T(8,128)(2,1)S(1)}, bf16[64,512]{1,0:T(8,128)(2,1)S(1)}, u32[]{:S(2)}, u32[]{:S(2)}) collective-permute-start(bf16[64,512]{1,0:T(8,128)(2,1)S(1)} %constant_dynamic-update-slice_fusion), channel_id=1, source_target_pairs={{0,5},{1,4},{2,7},{3,6},{4,1},{5,0},{6,3},{7,2},{8,13},{9,12},{10,... | collective-permute-start | bytes 196616 | tf_op jit(solution)/shard_map/ppermute | solution.py:39
  5.3 10.7 %collective-permute-start.6 = (bf16[64,512]{1,0:T(8,128)(2,1)S(1)}, bf16[64,512]{1,0:T(8,128)(2,1)S(1)}, u32[]{:S(2)}, u32[]{:S(2)}) collective-permute-start(bf16[64,512]{1,0:T(8,128)(2,1)S(1)} %constant_dynamic-update-slice_fusion), channel_id=1, source_target_pairs={{0,8},{1,9},{2,10},{3,11},{4,12},{5,13},{6,14},{7,15},{8,0},{9,1},... | collective-permute-start | bytes 196616 | tf_op jit(solution)/shard_map/ppermute | solution.py:39
  7.4 8.7 %collective-permute-start.5 = (bf16[64,512]{1,0:T(8,128)(2,1)S(1)}, bf16[64,512]{1,0:T(8,128)(2,1)S(1)}, u32[]{:S(2)}, u32[]{:S(2)}) collective-permute-start(bf16[64,512]{1,0:T(8,128)(2,1)S(1)} %constant_dynamic-update-slice_fusion), channel_id=1, source_target_pairs={{0,16},{1,17},{2,18},{3,19},{4,20},{5,21},{6,22},{7,23},{8,24},{9,... | collective-permute-start | bytes 196616 | tf_op jit(solution)/shard_map/ppermute | solution.py:39
  10.0 6.1 %collective-permute-start.4 = (bf16[64,512]{1,0:T(8,128)(2,1)S(1)}, bf16[64,512]{1,0:T(8,128)(2,1)S(1)}, u32[]{:S(2)}, u32[]{:S(2)}) collective-permute-start(bf16[64,512]{1,0:T(8,128)(2,1)S(1)} %constant_dynamic-update-slice_fusion), channel_id=1, source_target_pairs={{0,24},{1,25},{2,26},{3,27},{4,28},{5,29},{6,30},{7,31},{8,16},{9,... | collective-permute-start | bytes 196616 | tf_op jit(solution)/shard_map/ppermute | solution.py:39
  10.5 13.1 %copy-start = (bf16[64,2048]{1,0:T(8,128)(2,1)S(1)}, bf16[64,2048]{1,0:T(8,128)(2,1)}, u32[]{:S(2)}) copy-start(bf16[64,2048]{1,0:T(8,128)(2,1)} %refs_0_.5) | copy-start | bytes 786436
  10.5 10.2 %collective-permute-start.11 = (bf16[256,512]{1,0:T(8,128)(2,1)S(1)}, bf16[256,512]{1,0:T(8,128)(2,1)S(1)}, u32[]{:S(2)}, u32[]{:S(2)}) collective-permute-start(bf16[256,512]{1,0:T(8,128)(2,1)S(1)} %pad_maximum_fusion.refs_1_), channel_id=1, source_target_pairs={{0,2},{1,3},{2,0},{3,1},{4,6},{5,7},{6,4},{7,5},{8,10},{9,11},{10,... | collective-permute-start | bytes 786440 | tf_op jit(solution)/shard_map/ppermute | solution.py:39
  16.1 3.2 %collective-permute-start.12 = (bf16[192,512]{1,0:T(8,128)(2,1)S(1)}, bf16[192,512]{1,0:T(8,128)(2,1)S(1)}, u32[]{:S(2)}, u32[]{:S(2)}) collective-permute-start(bf16[192,512]{1,0:T(8,128)(2,1)S(1)} %constant_dynamic-update-slice_fusion.2.refs_2_), channel_id=1, source_target_pairs={{0,2},{1,3},{2,0},{3,1},{4,6},{5,7},{6,4},{7,5},{8,10},{9,11},{10,... | collective-permute-start | bytes 589832 | tf_op jit(solution)/shard_map/ppermute | solution.py:39
  16.1 11.4 %collective-permute-start.8 = (bf16[192,512]{1,0:T(8,128)(2,1)S(1)}, bf16[192,512]{1,0:T(8,128)(2,1)S(1)}, u32[]{:S(2)}, u32[]{:S(2)}) collective-permute-start(bf16[192,512]{1,0:T(8,128)(2,1)S(1)} %constant_dynamic-update-slice_fusion.2.refs_2_), channel_id=1, source_target_pairs={{0,1},{1,0},{2,3},{3,2},{4,5},{5,4},{6,7},{7,6},{8,9},{9,8},{10,11... | collective-permute-start | bytes 589832 | tf_op jit(solution)/shard_map/ppermute | solution.py:39
  17.7 9.9 %collective-permute-start.7 = (bf16[192,512]{1,0:T(8,128)(2,1)S(1)}, bf16[192,512]{1,0:T(8,128)(2,1)S(1)}, u32[]{:S(2)}, u32[]{:S(2)}) collective-permute-start(bf16[192,512]{1,0:T(8,128)(2,1)S(1)} %constant_dynamic-update-slice_fusion.2.refs_2_), channel_id=1, source_target_pairs={{0,4},{1,5},{2,6},{3,7},{4,0},{5,1},{6,2},{7,3},{8,12},{9,13},{10,... | collective-permute-start | bytes 589832 | tf_op jit(solution)/shard_map/ppermute | solution.py:39
  19.2 6.5 %collective-permute-start.3 = (bf16[64,512]{1,0:T(8,128)(2,1)S(1)}, bf16[64,512]{1,0:T(8,128)(2,1)S(1)}, u32[]{:S(2)}, u32[]{:S(2)}) collective-permute-start(bf16[64,512]{1,0:T(8,128)(2,1)S(1)} %collective-permute-done), channel_id=1, source_target_pairs={{0,8},{1,9},{2,10},{3,11},{4,12},{5,13},{6,14},{7,15},{8,0},{9,1},... | collective-permute-start | bytes 196616 | tf_op jit(solution)/shard_map/ppermute | solution.py:39
  19.2 8.3 %collective-permute-start.2 = (bf16[64,512]{1,0:T(8,128)(2,1)S(1)}, bf16[64,512]{1,0:T(8,128)(2,1)S(1)}, u32[]{:S(2)}, u32[]{:S(2)}) collective-permute-start(bf16[64,512]{1,0:T(8,128)(2,1)S(1)} %collective-permute-done), channel_id=1, source_target_pairs={{0,16},{1,17},{2,18},{3,19},{4,20},{5,21},{6,22},{7,23},{8,24},{9,... | collective-permute-start | bytes 196616 | tf_op jit(solution)/shard_map/ppermute | solution.py:39
  20.7 6.9 %collective-permute-start.1 = (bf16[64,512]{1,0:T(8,128)(2,1)S(1)}, bf16[64,512]{1,0:T(8,128)(2,1)S(1)}, u32[]{:S(2)}, u32[]{:S(2)}) collective-permute-start(bf16[64,512]{1,0:T(8,128)(2,1)S(1)} %collective-permute-done), channel_id=1, source_target_pairs={{0,24},{1,25},{2,26},{3,27},{4,28},{5,29},{6,30},{7,31},{8,16},{9,... | collective-permute-start | bytes 196616 | tf_op jit(solution)/shard_map/ppermute | solution.py:39
  27.6 2.3 %collective-permute-start.15 = (bf16[192,512]{1,0:T(8,128)(2,1)S(1)}, bf16[192,512]{1,0:T(8,128)(2,1)S(1)}, u32[]{:S(2)}, u32[]{:S(2)}) collective-permute-start(bf16[192,512]{1,0:T(8,128)(2,1)S(1)} %constant_dynamic-update-slice_fusion.5.refs_6_), channel_id=1, source_target_pairs={{0,2},{1,3},{2,0},{3,1},{4,6},{5,7},{6,4},{7,5},{8,10},{9,11},{10,... | collective-permute-start | bytes 589832 | tf_op jit(solution)/shard_map/ppermute | solution.py:39
  27.7 2.2 %collective-permute-start.13 = (bf16[192,512]{1,0:T(8,128)(2,1)S(1)}, bf16[192,512]{1,0:T(8,128)(2,1)S(1)}, u32[]{:S(2)}, u32[]{:S(2)}) collective-permute-start(bf16[192,512]{1,0:T(8,128)(2,1)S(1)} %collective-permute-done.7.refs_4_), channel_id=1, source_target_pairs={{0,2},{1,3},{2,0},{3,1},{4,6},{5,7},{6,4},{7,5},{8,10},{9,11},{10,... | collective-permute-start | bytes 589832 | tf_op jit(solution)/shard_map/ppermute | solution.py:39
  28.2 1.7 %collective-permute-start.14 = (bf16[192,512]{1,0:T(8,128)(2,1)S(1)}, bf16[192,512]{1,0:T(8,128)(2,1)S(1)}, u32[]{:S(2)}, u32[]{:S(2)}) collective-permute-start(bf16[192,512]{1,0:T(8,128)(2,1)S(1)} %collective-permute-done.8.refs_5_), channel_id=1, source_target_pairs={{0,2},{1,3},{2,0},{3,1},{4,6},{5,7},{6,4},{7,5},{8,10},{9,11},{10,... | collective-permute-start | bytes 589832 | tf_op jit(solution)/shard_map/ppermute | solution.py:39

commit v4 on v3

--- a/solution.py
+++ b/solution.py
@@ -141,13 +141,12 @@
         ups = range(1, layout.planes)
         lines = range(1, layout.lines)
         columns = range(1, layout.across)
-        corners = [(0, l, 0, c) for l in lines for c in columns]
+        side_steps = [(0, l, 0, 0) for l in lines] + [(0, 0, 0, c) for c in columns]
+        corner_steps = [(0, l, 0, c) for l in lines for c in columns]
+        above_steps = [(up, 0, 0, 0) for up in reversed(ups)]
 
         def go(array, steps):
             return exchange(array, up=steps[0], line=steps[1], swap=steps[2], column=steps[3])
-
-        def join(arrays):
-            return jnp.concatenate(arrays, axis=0) if len(arrays) > 1 else arrays[0]
 
         def moved(steps, by):
             return [tuple(a ^ b for a, b in zip(one, by, strict=True)) for one in steps]
@@ -155,23 +154,28 @@
         def swapped(pieces):
             return [(exchange(array, swap=1), moved(steps, (0, 0, 1, 0))) for array, steps in pieces]
 
-        corner = join([go(block, steps) for steps in corners])
-        above_steps = [(up, 0, 0, 0) for up in reversed(ups)]
-        above = join([go(block, steps) for steps in above_steps])
-        side_steps = [(0, l, 0, 0) for l in lines] + [(0, 0, 0, c) for c in columns]
-        flat = join([block] + [go(block, steps) for steps in side_steps] + [corner])
-        flat_steps = [(0, 0, 0, 0)] + side_steps + corners
-        far = [go(corner, steps) for steps in above_steps]
-        sides = [go(above, steps) for steps in side_steps]
+        corner = [go(block, steps) for steps in corner_steps]
+        corner = jnp.concatenate(corner, axis=0) if len(corner) > 1 else corner[0]
+        tower_steps = [(0, 0, 0, 0)] + above_steps
+        corner, above = lax.optimization_barrier((corner, [go(block, steps) for steps in above_steps]))
+        near = [(jnp.concatenate([block] + above, axis=0), tower_steps)]
+        far = [(corner, corner_steps)]
+        far += [(go(corner, steps), moved(corner_steps, steps)) for steps in above_steps]
+        sides = [(go(near[0][0], steps), moved(tower_steps, steps)) for steps in side_steps]
 
-        near = [(flat, flat_steps), (above, above_steps)]
-        state = fold(layout, queries, None, near + swapped(near), groups)
-        (far, sides), state = lax.optimization_barrier(((far, sides), state))
-        later = [(array, moved(above_steps, steps)) for array, steps in zip(sides, side_steps, strict=True)]
-        later.append((join(far), [step for steps in above_steps for step in moved(corners, steps)]))
-        others = swapped(later)
-        state = fold(layout, queries, state, later, groups)
-        return fold(layout, queries, state, others, groups, last=True)
+        def after(pieces, state):
+            arrays, state = lax.optimization_barrier(([array for array, _ in pieces], state))
+            return [(array, steps) for array, (_, steps) in zip(arrays, pieces, strict=True)], state
+
+        state = fold(layout, queries, None, near, groups)
+        near_others = swapped(near)
+        state = fold(layout, queries, state, near_others, groups)
+        far, state = after(far, state)
+        far = [(jnp.concatenate([x for x, _ in far], axis=0), [one for _, steps in far for one in steps])]
+        far_others = swapped(far)
+        sides, state = after(sides, state)
+        state = fold(layout, queries, state, far + sides, groups)
+        return fold(layout, queries, state, swapped(sides) + far_others, groups, last=True)
 
     placed = P(AXES, None)
     return jax.shard_map(

time: 32.5 us -> 29.1 us (0.90)
  starting transfers between devices: 17.6 us -> 14.5 us
    ppermute x16 -> x13, starting transfers between devices: 17.6 us -> 14.5 us  [exchange(): lax.ppermute(array, AXES, [(rank, self.partner(rank, **steps)) for rank i...]
    pallas_call x3 -> x4, Pallas kernels: 6.02 us -> 5.71 us  [fold(): pl.pallas_call(functools.partial(fold_kernel, layout, [blocks for _, bloc...]
    ppermute x16 -> x13, waiting for transfers between devices: 7.65 us -> 7.77 us  [exchange(): lax.ppermute(array, AXES, [(rank, self.partner(rank, **steps)) for rank i...]
    unnamed x9 -> x8, local copies, waits for them, and re-layouts: 0.8 us -> 0.8 us
  transfers between devices with their start and end apart: 16 -> 13, of which waited for: 3 -> 5; matrix products, arithmetic and copies ran while one was open for 0% -> 0% of each run, Pallas kernels for 11% -> 11%
where the time goes in v4:
time: 29.1 us; the launch traced here: 28.9 us
  starting transfers between devices  14.5 us (50%)
  waiting for transfers between devices  7.77 us (27%)
  Pallas kernels  5.71 us (20%)
  local copies, waits for them, and re-layouts  0.81 us (3%)
    ppermute x13, starting transfers between devices, exchange(): lax.ppermute(array, AXES, [(rank, self.partner(rank, **steps)) for rank i...  14.5 us
    ppermute x13, waiting for transfers between devices, exchange(): lax.ppermute(array, AXES, [(rank, self.partner(rank, **steps)) for rank i...  7.77 us
    pallas_call x4, Pallas kernels, fold(): pl.pallas_call(functools.partial(fold_kernel, layout, [blocks for _, bloc...  5.71 us
    unnamed x8, local copies, waits for them, and re-layouts  0.8 us
  transfers between devices with their start and end apart: 13, of which 5 were waited for; matrix products, arithmetic and copies ran while one was open for 0% of the time, Pallas kernels for 11%

profile of v4, /device:TPU:0, one launch (start us, length us, event | category | flops | bytes accessed | tf_op | source)
XLA Modules:
  0.0 28.9 jit_solution(7165411447293912991)
XLA Ops:
  0.0 0.0 copy-start.1
  0.0 0.8 %constant_dynamic-update-slice_fusion.1 = bf16[64,512]{1,0:T(8,128)(2,1)S(1)} fusion(bf16[64,256]{1,0:T(8,128)(2,1)} %param.4), kind=kLoop, calls=%fused_computation.2 | loop fusion | bytes 65536
  0.8 0.0 copy-done.1
  0.8 0.0 copy-start
  0.8 4.0 %collective-permute-start = (bf16[64,512]{1,0:T(8,128)(2,1)S(1)}, bf16[64,512]{1,0:T(8,128)(2,1)S(1)}, u32[]{:S(2)}, u32[]{:S(2)}) collective-permute-start(bf16[64,512]{1,0:T(8,128)(2,1)S(1)} %constant_dynamic-update-slice_fusion), channel_id=1, source_target_pairs={{0,5},{1,4},{2,7},{3,6},{4,1},{5,0},{6,3},{7,2},{8,13},{9,12},{10,... | collective-permute-start | bytes 196616 | tf_op jit(solution)/shard_map/ppermute | solution.py:39
  4.8 3.6 %collective-permute-start.1 = (bf16[64,512]{1,0:T(8,128)(2,1)S(1)}, bf16[64,512]{1,0:T(8,128)(2,1)S(1)}, u32[]{:S(2)}, u32[]{:S(2)}) collective-permute-start(bf16[64,512]{1,0:T(8,128)(2,1)S(1)} %constant_dynamic-update-slice_fusion), channel_id=1, source_target_pairs={{0,24},{1,25},{2,26},{3,27},{4,28},{5,29},{6,30},{7,31},{8,16},{9,... | collective-permute-start | bytes 196616 | tf_op jit(solution)/shard_map/ppermute | solution.py:39
  8.4 0.0 collective-permute-start.2
  8.4 0.8 %collective-permute-start.3 = (bf16[64,512]{1,0:T(8,128)(2,1)S(1)}, bf16[64,512]{1,0:T(8,128)(2,1)S(1)}, u32[]{:S(2)}, u32[]{:S(2)}) collective-permute-start(bf16[64,512]{1,0:T(8,128)(2,1)S(1)} %constant_dynamic-update-slice_fusion), channel_id=1, source_target_pairs={{0,8},{1,9},{2,10},{3,11},{4,12},{5,13},{6,14},{7,15},{8,0},{9,1},... | collective-permute-start | bytes 196616 | tf_op jit(solution)/shard_map/ppermute | solution.py:39
  9.1 0.0 collective-permute-done
  9.1 2.5 %collective-permute-done.1 = bf16[64,512]{1,0:T(8,128)(2,1)S(1)} collective-permute-done((bf16[64,512]{1,0:T(8,128)(2,1)S(1)}, bf16[64,512]{1,0:T(8,128)(2,1)S(1)}, u32[]{:S(2)}, u32[]{:S(2)}) %collective-permute-start.1) | collective-permute-done | bytes 65568 | tf_op jit(solution)/shard_map/ppermute | solution.py:39
  11.6 2.1 %collective-permute-done.2 = bf16[64,512]{1,0:T(8,128)(2,1)S(1)} collective-permute-done((bf16[64,512]{1,0:T(8,128)(2,1)S(1)}, bf16[64,512]{1,0:T(8,128)(2,1)S(1)}, u32[]{:S(2)}, u32[]{:S(2)}) %collective-permute-start.2) | collective-permute-done | bytes 65568 | tf_op jit(solution)/shard_map/ppermute | solution.py:39
  13.7 0.1 collective-permute-done.3
  13.8 0.1 collective-permute-start.9
  13.9 0.6 %collective-permute-start.4 = (bf16[256,512]{1,0:T(8,128)(2,1)S(1)}, bf16[256,512]{1,0:T(8,128)(2,1)S(1)}, u32[]{:S(2)}, u32[]{:S(2)}) collective-permute-start(bf16[256,512]{1,0:T(8,128)(2,1)S(1)} %pad_maximum_fusion.refs_1_), channel_id=1, source_target_pairs={{0,4},{1,5},{2,6},{3,7},{4,0},{5,1},{6,2},{7,3},{8,12},{9,13},{10,... | collective-permute-start | bytes 786440 | tf_op jit(solution)/shard_map/ppermute | solution.py:39
  14.5 0.4 %collective-permute-start.5 = (bf16[256,512]{1,0:T(8,128)(2,1)S(1)}, bf16[256,512]{1,0:T(8,128)(2,1)S(1)}, u32[]{:S(2)}, u32[]{:S(2)}) collective-permute-start(bf16[256,512]{1,0:T(8,128)(2,1)S(1)} %pad_maximum_fusion.refs_1_), channel_id=1, source_target_pairs={{0,1},{1,0},{2,3},{3,2},{4,5},{5,4},{6,7},{7,6},{8,9},{9,8},{10,11... | collective-permute-start | bytes 786440 | tf_op jit(solution)/shard_map/ppermute | solution.py:39
  14.9 2.6 %collective-permute-start.6 = (bf16[64,512]{1,0:T(8,128)(2,1)S(1)}, bf16[64,512]{1,0:T(8,128)(2,1)S(1)}, u32[]{:S(2)}, u32[]{:S(2)}) collective-permute-start(bf16[64,512]{1,0:T(8,128)(2,1)S(1)} %collective-permute-done), channel_id=1, source_target_pairs={{0,24},{1,25},{2,26},{3,27},{4,28},{5,29},{6,30},{7,31},{8,16},{9,... | collective-permute-start | bytes 196616 | tf_op jit(solution)/shard_map/ppermute | solution.py:39
  17.5 0.0 collective-permute-start.7
  17.5 0.0 collective-permute-done.9.refs_4_
  17.5 1.8 %collective-permute-start.8 = (bf16[64,512]{1,0:T(8,128)(2,1)S(1)}, bf16[64,512]{1,0:T(8,128)(2,1)S(1)}, u32[]{:S(2)}, u32[]{:S(2)}) collective-permute-start(bf16[64,512]{1,0:T(8,128)(2,1)S(1)} %collective-permute-done), channel_id=1, source_target_pairs={{0,8},{1,9},{2,10},{3,11},{4,12},{5,13},{6,14},{7,15},{8,0},{9,1},... | collective-permute-start | bytes 196616 | tf_op jit(solution)/shard_map/ppermute | solution.py:39
  19.3 0.0 copy-done
  19.3 0.7 %shard_map.37 = (f32[2,512,128]{2,1,0:T(8,128)S(1)}, f32[2,512,128]{2,1,0:T(8,128)S(1)}, f32[2,512,128]{2,1,0:T(8,128)S(1)}) custom-call(bf16[64,2048]{1,0:T(8,128)(2,1)S(1)} %copy-done, bf16[256,512]{1,0:T(8,128)(2,1)S(1)} %pad_maximum_fusion.refs_1_), custom_call_target="tpu_custom_call" | custom-call | tf_op jit(solution)/shard_map/pallas_call | solution.py:121
  20.0 0.7 %shard_map.38 = (f32[2,512,128]{2,1,0:T(8,128)S(1)}, f32[2,512,128]{2,1,0:T(8,128)S(1)}, f32[2,512,128]{2,1,0:T(8,128)S(1)}) custom-call(bf16[64,2048]{1,0:T(8,128)(2,1)S(1)} %copy-done, f32[2,512,128]{2,1,0:T(8,128)S(1)} %get-tuple-element.34.refs_1_, f32[2,512,128]{2,1,0:T(8,128)S(1)} %get-tuple-element.35.refs_2_, ...), custom_call_target="tpu_custom_call" | custom-call | tf_op jit(solution)/shard_map/pallas_call | solution.py:121
  20.8 0.6 %collective-permute-done.6 = bf16[64,512]{1,0:T(8,128)(2,1)S(1)} collective-permute-done((bf16[64,512]{1,0:T(8,128)(2,1)S(1)}, bf16[64,512]{1,0:T(8,128)(2,1)S(1)}, u32[]{:S(2)}, u32[]{:S(2)}) %collective-permute-start.6) | collective-permute-done | bytes 65568 | tf_op jit(solution)/shard_map/ppermute | solution.py:39
  21.4 2.5 %collective-permute-done.7 = bf16[64,512]{1,0:T(8,128)(2,1)S(1)} collective-permute-done((bf16[64,512]{1,0:T(8,128)(2,1)S(1)}, bf16[64,512]{1,0:T(8,128)(2,1)S(1)}, u32[]{:S(2)}, u32[]{:S(2)}) %collective-permute-start.7) | collective-permute-done | bytes 65568 | tf_op jit(solution)/shard_map/ppermute | solution.py:39
  23.9 0.0 collective-permute-done.8
  23.9 0.0 collective-permute-done.4.refs_5_
  23.9 0.0 collective-permute-done.5.refs_6_
  24.0 0.1 collective-permute-start.12
  24.0 0.5 %collective-permute-start.10 = (bf16[256,512]{1,0:T(8,128)(2,1)S(1)}, bf16[256,512]{1,0:T(8,128)(2,1)S(1)}, u32[]{:S(2)}, u32[]{:S(2)}) collective-permute-start(bf16[256,512]{1,0:T(8,128)(2,1)S(1)} %collective-permute-done.4.refs_5_), channel_id=1, source_target_pairs={{0,2},{1,3},{2,0},{3,1},{4,6},{5,7},{6,4},{7,5},{8,10},{9,11},{10,... | collective-permute-start | bytes 786440 | tf_op jit(solution)/shard_map/ppermute | solution.py:39
  24.5 0.1 collective-permute-start.11
  24.6 1.8 %shard_map.39 = (f32[2,512,128]{2,1,0:T(8,128)S(1)}, f32[2,512,128]{2,1,0:T(8,128)S(1)}, f32[2,512,128]{2,1,0:T(8,128)S(1)}) custom-call(bf16[64,2048]{1,0:T(8,128)(2,1)S(1)} %copy-done, f32[2,512,128]{2,1,0:T(8,128)S(1)} %get-tuple-element.43.refs_1_, f32[2,512,128]{2,1,0:T(8,128)S(1)} %get-tuple-element.44.refs_2_, ...), custom_call_target="tpu_custom_call" | custom-call | tf_op jit(solution)/shard_map/pallas_call | solution.py:121
  26.4 0.0 collective-permute-done.12.refs_6_
  26.4 0.0 collective-permute-done.10.refs_4_
  26.4 0.0 collective-permute-done.11.refs_5_
  26.4 2.5 %shard_map.40 = bf16[64,2048]{1,0:T(8,128)(2,1)} custom-call(bf16[64,2048]{1,0:T(8,128)(2,1)S(1)} %copy-done, f32[2,512,128]{2,1,0:T(8,128)S(1)} %get-tuple-element.52.refs_1_, f32[2,512,128]{2,1,0:T(8,128)S(1)} %get-tuple-element.53.refs_2_, f32[2,512,128]{2,1,0:T(8,128)S(1)} %get-tuple-element.54.refs_3_, ...), custom_call_target="tpu_custom_call" | custom-call | tf_op jit(solution)/shard_map/pallas_call | solution.py:121
  (6 shorter events, 0.0 us)
Async XLA Ops:
  0.0 0.8 %copy-start.1 = (bf16[64,256]{1,0:T(8,128)(2,1)S(1)}, bf16[64,256]{1,0:T(8,128)(2,1)}, u32[]{:S(2)}) copy-start(bf16[64,256]{1,0:T(8,128)(2,1)} %param.5) | copy-start | bytes 98308
  0.8 18.5 %copy-start = (bf16[64,2048]{1,0:T(8,128)(2,1)S(1)}, bf16[64,2048]{1,0:T(8,128)(2,1)}, u32[]{:S(2)}) copy-start(bf16[64,2048]{1,0:T(8,128)(2,1)} %refs_0_.7) | copy-start | bytes 786436
  0.8 8.4 %collective-permute-start = (bf16[64,512]{1,0:T(8,128)(2,1)S(1)}, bf16[64,512]{1,0:T(8,128)(2,1)S(1)}, u32[]{:S(2)}, u32[]{:S(2)}) collective-permute-start(bf16[64,512]{1,0:T(8,128)(2,1)S(1)} %constant_dynamic-update-slice_fusion), channel_id=1, source_target_pairs={{0,5},{1,4},{2,7},{3,6},{4,1},{5,0},{6,3},{7,2},{8,13},{9,12},{10,... | collective-permute-start | bytes 196616 | tf_op jit(solution)/shard_map/ppermute | solution.py:39
  4.8 6.9 %collective-permute-start.1 = (bf16[64,512]{1,0:T(8,128)(2,1)S(1)}, bf16[64,512]{1,0:T(8,128)(2,1)S(1)}, u32[]{:S(2)}, u32[]{:S(2)}) collective-permute-start(bf16[64,512]{1,0:T(8,128)(2,1)S(1)} %constant_dynamic-update-slice_fusion), channel_id=1, source_target_pairs={{0,24},{1,25},{2,26},{3,27},{4,28},{5,29},{6,30},{7,31},{8,16},{9,... | collective-permute-start | bytes 196616 | tf_op jit(solution)/shard_map/ppermute | solution.py:39
  8.4 5.4 %collective-permute-start.2 = (bf16[64,512]{1,0:T(8,128)(2,1)S(1)}, bf16[64,512]{1,0:T(8,128)(2,1)S(1)}, u32[]{:S(2)}, u32[]{:S(2)}) collective-permute-start(bf16[64,512]{1,0:T(8,128)(2,1)S(1)} %constant_dynamic-update-slice_fusion), channel_id=1, source_target_pairs={{0,16},{1,17},{2,18},{3,19},{4,20},{5,21},{6,22},{7,23},{8,24},{9,... | collective-permute-start | bytes 196616 | tf_op jit(solution)/shard_map/ppermute | solution.py:39
  8.4 5.4 %collective-permute-start.3 = (bf16[64,512]{1,0:T(8,128)(2,1)S(1)}, bf16[64,512]{1,0:T(8,128)(2,1)S(1)}, u32[]{:S(2)}, u32[]{:S(2)}) collective-permute-start(bf16[64,512]{1,0:T(8,128)(2,1)S(1)} %constant_dynamic-update-slice_fusion), channel_id=1, source_target_pairs={{0,8},{1,9},{2,10},{3,11},{4,12},{5,13},{6,14},{7,15},{8,0},{9,1},... | collective-permute-start | bytes 196616 | tf_op jit(solution)/shard_map/ppermute | solution.py:39
  13.8 3.7 %collective-permute-start.9 = (bf16[256,512]{1,0:T(8,128)(2,1)S(1)}, bf16[256,512]{1,0:T(8,128)(2,1)S(1)}, u32[]{:S(2)}, u32[]{:S(2)}) collective-permute-start(bf16[256,512]{1,0:T(8,128)(2,1)S(1)} %pad_maximum_fusion.refs_1_), channel_id=1, source_target_pairs={{0,2},{1,3},{2,0},{3,1},{4,6},{5,7},{6,4},{7,5},{8,10},{9,11},{10,... | collective-permute-start | bytes 786440 | tf_op jit(solution)/shard_map/ppermute | solution.py:39
  13.9 10.0 %collective-permute-start.4 = (bf16[256,512]{1,0:T(8,128)(2,1)S(1)}, bf16[256,512]{1,0:T(8,128)(2,1)S(1)}, u32[]{:S(2)}, u32[]{:S(2)}) collective-permute-start(bf16[256,512]{1,0:T(8,128)(2,1)S(1)} %pad_maximum_fusion.refs_1_), channel_id=1, source_target_pairs={{0,4},{1,5},{2,6},{3,7},{4,0},{5,1},{6,2},{7,3},{8,12},{9,13},{10,... | collective-permute-start | bytes 786440 | tf_op jit(solution)/shard_map/ppermute | solution.py:39
  14.5 9.5 %collective-permute-start.5 = (bf16[256,512]{1,0:T(8,128)(2,1)S(1)}, bf16[256,512]{1,0:T(8,128)(2,1)S(1)}, u32[]{:S(2)}, u32[]{:S(2)}) collective-permute-start(bf16[256,512]{1,0:T(8,128)(2,1)S(1)} %pad_maximum_fusion.refs_1_), channel_id=1, source_target_pairs={{0,1},{1,0},{2,3},{3,2},{4,5},{5,4},{6,7},{7,6},{8,9},{9,8},{10,11... | collective-permute-start | bytes 786440 | tf_op jit(solution)/shard_map/ppermute | solution.py:39
  14.9 6.5 %collective-permute-start.6 = (bf16[64,512]{1,0:T(8,128)(2,1)S(1)}, bf16[64,512]{1,0:T(8,128)(2,1)S(1)}, u32[]{:S(2)}, u32[]{:S(2)}) collective-permute-start(bf16[64,512]{1,0:T(8,128)(2,1)S(1)} %collective-permute-done), channel_id=1, source_target_pairs={{0,24},{1,25},{2,26},{3,27},{4,28},{5,29},{6,30},{7,31},{8,16},{9,... | collective-permute-start | bytes 196616 | tf_op jit(solution)/shard_map/ppermute | solution.py:39
  17.5 6.4 %collective-permute-start.7 = (bf16[64,512]{1,0:T(8,128)(2,1)S(1)}, bf16[64,512]{1,0:T(8,128)(2,1)S(1)}, u32[]{:S(2)}, u32[]{:S(2)}) collective-permute-start(bf16[64,512]{1,0:T(8,128)(2,1)S(1)} %collective-permute-done), channel_id=1, source_target_pairs={{0,16},{1,17},{2,18},{3,19},{4,20},{5,21},{6,22},{7,23},{8,24},{9,... | collective-permute-start | bytes 196616 | tf_op jit(solution)/shard_map/ppermute | solution.py:39
  17.5 6.3 %collective-permute-start.8 = (bf16[64,512]{1,0:T(8,128)(2,1)S(1)}, bf16[64,512]{1,0:T(8,128)(2,1)S(1)}, u32[]{:S(2)}, u32[]{:S(2)}) collective-permute-start(bf16[64,512]{1,0:T(8,128)(2,1)S(1)} %collective-permute-done), channel_id=1, source_target_pairs={{0,8},{1,9},{2,10},{3,11},{4,12},{5,13},{6,14},{7,15},{8,0},{9,1},... | collective-permute-start | bytes 196616 | tf_op jit(solution)/shard_map/ppermute | solution.py:39
  24.0 2.4 %collective-permute-start.12 = (bf16[256,512]{1,0:T(8,128)(2,1)S(1)}, bf16[256,512]{1,0:T(8,128)(2,1)S(1)}, u32[]{:S(2)}, u32[]{:S(2)}) collective-permute-start(bf16[256,512]{1,0:T(8,128)(2,1)S(1)} %constant_dynamic-update-slice_fusion.2.refs_4_), channel_id=1, source_target_pairs={{0,2},{1,3},{2,0},{3,1},{4,6},{5,7},{6,4},{7,5},{8,10},{9,11},{10,... | collective-permute-start | bytes 786440 | tf_op jit(solution)/shard_map/ppermute | solution.py:39
  24.0 2.3 %collective-permute-start.10 = (bf16[256,512]{1,0:T(8,128)(2,1)S(1)}, bf16[256,512]{1,0:T(8,128)(2,1)S(1)}, u32[]{:S(2)}, u32[]{:S(2)}) collective-permute-start(bf16[256,512]{1,0:T(8,128)(2,1)S(1)} %collective-permute-done.4.refs_5_), channel_id=1, source_target_pairs={{0,2},{1,3},{2,0},{3,1},{4,6},{5,7},{6,4},{7,5},{8,10},{9,11},{10,... | collective-permute-start | bytes 786440 | tf_op jit(solution)/shard_map/ppermute | solution.py:39
  24.5 1.9 %collective-permute-start.11 = (bf16[256,512]{1,0:T(8,128)(2,1)S(1)}, bf16[256,512]{1,0:T(8,128)(2,1)S(1)}, u32[]{:S(2)}, u32[]{:S(2)}) collective-permute-start(bf16[256,512]{1,0:T(8,128)(2,1)S(1)} %collective-permute-done.5.refs_6_), channel_id=1, source_target_pairs={{0,2},{1,3},{2,0},{3,1},{4,6},{5,7},{6,4},{7,5},{8,10},{9,11},{10,... | collective-permute-start | bytes 786440 | tf_op jit(solution)/shard_map/ppermute | solution.py:39

commit v5 on v4

--- a/solution.py
+++ b/solution.py
@@ -43,12 +43,30 @@
 
 
 def fold_kernel(layout, sources, rows, groups, carried, last, *refs):
+    plane = layout.split(layout.here())[0]
+    level = [[steps for steps in piece if steps[0] == 0] for piece in sources]
+    assert all(piece[: len(flat)] == flat for piece, flat in zip(sources, level, strict=True))
+    if level == sources:
+        fold_blocks(layout, sources, rows, groups, carried, last, *refs)
+        return
+
+    @pl.when(plane == 0)
+    def _():
+        fold_blocks(layout, level, rows, groups, carried, last, *refs)
+
+    @pl.when(plane > 0)
+    def _():
+        fold_blocks(layout, sources, rows, groups, carried, last, *refs)
+
+
+def fold_blocks(layout, sources, rows, groups, carried, last, *refs):
     refs = list(refs)
     query_ref = refs.pop(0)
     state_refs = [refs.pop(0) for _ in range(3)] if carried else None
     piece_refs, refs = refs[: len(sources)], refs[len(sources) :]
     out_refs, (score_ref, weight_ref) = refs[:-2], refs[-2:]
     blocks = [steps for piece in sources for steps in piece]
+    taken = [(ref, len(piece) * rows) for ref, piece in zip(piece_refs, sources, strict=True) if piece]
     width = len(blocks) * rows
     heads = query_ref.shape[1] // (groups * HD)
     tall = heads * rows
@@ -67,19 +85,20 @@
         later = jnp.logical_and(place < rows, place > token)
         bias = jnp.where(jnp.logical_and(place >= 0, later), HIDDEN, bias)
 
-    for group in range(groups):
+    def score(group):
         first = group * heads * HD
         query = jnp.concatenate([query_ref[:, first + h * HD : first + (h + 1) * HD] for h in range(heads)], axis=0)
         at = group * HD
-        key = jnp.concatenate([ref[:, at : at + HD] for ref in piece_refs], axis=0)
-        at = (groups + group) * HD
-        value = jnp.concatenate([ref[:, at : at + HD] for ref in piece_refs], axis=0)
-        score_ref[...] = lax.dot_general(
+        key = jnp.concatenate([ref[:size, at : at + HD] for ref, size in taken], axis=0)
+        score_ref[group % 2, :, :width] = lax.dot_general(
             query, key, (((1,), (1,)), ((), ())), preferred_element_type=jnp.float32
         )
+
+    def mix(group):
+        slot = group % 2
         tops, sums = [], []
         for begin in range(0, tall, rows):
-            scores = score_ref[begin : begin + rows, :] * scale + bias
+            scores = score_ref[slot, begin : begin + rows, :width] * scale + bias
             top = jnp.broadcast_to(jnp.max(scores, axis=1, keepdims=True), (rows, HD))
             if carried:
                 top = jnp.maximum(top, state_refs[0][group, begin : begin + rows])
@@ -92,16 +111,19 @@
                     total = total + weights
                 else:
                     rest = jnp.sum(weights, axis=1, keepdims=True)
-                weight_ref[begin : begin + rows, left : left + part] = weights.astype(jnp.bfloat16)
+                weight_ref[slot, begin : begin + rows, left : left + part] = weights.astype(jnp.bfloat16)
             tops.append(top)
             sums.append(jnp.broadcast_to(jnp.sum(total, axis=1, keepdims=True) + rest, (rows, HD)))
         largest, totals = jnp.concatenate(tops, axis=0), jnp.concatenate(sums, axis=0)
-        summed = jnp.dot(weight_ref[...], value, preferred_element_type=jnp.float32)
+        at = (groups + group) * HD
+        value = jnp.concatenate([ref[:size, at : at + HD] for ref, size in taken], axis=0)
+        summed = jnp.dot(weight_ref[slot, :, :width], value, preferred_element_type=jnp.float32)
         if carried:
             decay = jnp.exp2(state_refs[0][group] - largest)
             totals = totals + state_refs[1][group] * decay
             summed = summed + state_refs[2][group] * decay
         if last:
+            first = group * heads * HD
             result = (summed / totals).astype(jnp.bfloat16)
             for h in range(heads):
                 out_refs[0][:, first + h * HD : first + (h + 1) * HD] = result[h * rows : (h + 1) * rows]
@@ -109,12 +131,19 @@
             for ref, array in zip(out_refs, (largest, totals, summed), strict=True):
                 ref[group] = array
 
+    for begin in range(0, groups, 2):
+        both = range(begin, min(begin + 2, groups))
+        for group in both:
+            score(group)
+        for group in both:
+            mix(group)
+
 
 def fold(layout, queries, state, pieces, groups, last=False):
     rows, query_width = queries.shape
     tall = rows * query_width // (groups * HD)
     arrays = [array for array, _ in pieces]
-    tokens = sum(array.shape[0] for array in arrays)
+    tokens = -(-sum(array.shape[0] for array in arrays) // HD) * HD
     carried = state is not None
     state_type = jax.ShapeDtypeStruct((groups, tall, HD), jnp.float32)
     whole = pl.BlockSpec(memory_space=pltpu.VMEM)
@@ -125,7 +154,7 @@
         in_specs=[whole] * (1 + 3 * carried + len(arrays)),
         out_specs=whole if last else [whole] * 3,
         out_shape=jax.ShapeDtypeStruct(queries.shape, jnp.bfloat16) if last else [state_type] * 3,
-        scratch_shapes=[pltpu.VMEM((tall, tokens), jnp.float32), pltpu.VMEM((tall, tokens), jnp.bfloat16)],
+        scratch_shapes=[pltpu.VMEM((2, tall, tokens), jnp.float32), pltpu.VMEM((2, tall, tokens), jnp.bfloat16)],
         compiler_params=pltpu.CompilerParams(vmem_limit_bytes=24 * 1024 * 1024),
         cost_estimate=pl.CostEstimate(flops=0, bytes_accessed=0, transcendentals=0),
     )(queries, *(state or ()), *arrays)
@@ -168,14 +197,14 @@
             return [(array, steps) for array, (_, steps) in zip(arrays, pieces, strict=True)], state
 
         state = fold(layout, queries, None, near, groups)
-        near_others = swapped(near)
-        state = fold(layout, queries, state, near_others, groups)
+        sides, state = after(sides, state)
+        others = swapped(near) + swapped(sides)
+        state = fold(layout, queries, state, sides, groups)
         far, state = after(far, state)
         far = [(jnp.concatenate([x for x, _ in far], axis=0), [one for _, steps in far for one in steps])]
         far_others = swapped(far)
-        sides, state = after(sides, state)
-        state = fold(layout, queries, state, far + sides, groups)
-        return fold(layout, queries, state, swapped(sides) + far_others, groups, last=True)
+        state = fold(layout, queries, state, others, groups)
+        return fold(layout, queries, state, far + far_others, groups, last=True)
 
     placed = P(AXES, None)
     return jax.shard_map(

time: 29.1 us -> 26.6 us (0.914)
  Pallas kernels: 5.71 us -> 3.32 us
    pallas_call x4, Pallas kernels: 5.71 us -> 3.32 us  [fold(): pl.pallas_call(functools.partial(fold_kernel, layout, [blocks for _, bloc...]
  transfers between devices with their start and end apart: 13 -> 13, of which waited for: 5 -> 7; matrix products, arithmetic and copies ran while one was open for 0% -> 0% of each run, Pallas kernels for 11% -> 8%
where the time goes in v5:
time: 26.6 us; the launch traced here: 26.4 us
  starting transfers between devices  14.7 us (55%)
  waiting for transfers between devices  7.5 us (28%)
  Pallas kernels  3.32 us (12%)
  local copies, waits for them, and re-layouts  0.81 us (3%)
    ppermute x13, starting transfers between devices, exchange(): lax.ppermute(array, AXES, [(rank, self.partner(rank, **steps)) for rank i...  14.7 us
    ppermute x13, waiting for transfers between devices, exchange(): lax.ppermute(array, AXES, [(rank, self.partner(rank, **steps)) for rank i...  7.5 us
    pallas_call x4, Pallas kernels, fold(): pl.pallas_call(functools.partial(fold_kernel, layout, [blocks for _, bloc...  3.32 us
    unnamed x8, local copies, waits for them, and re-layouts  0.8 us
  transfers between devices with their start and end apart: 13, of which 7 were waited for; matrix products, arithmetic and copies ran while one was open for 0% of the time, Pallas kernels for 8%

profile of v5, /device:TPU:0, one launch (start us, length us, event | category | flops | bytes accessed | tf_op | source)
XLA Modules:
  0.0 26.4 jit_solution(17492148290073156736)
XLA Ops:
  0.0 0.0 copy-start.1
  0.0 0.8 %constant_dynamic-update-slice_fusion.1 = bf16[64,512]{1,0:T(8,128)(2,1)S(1)} fusion(bf16[64,256]{1,0:T(8,128)(2,1)} %param.4), kind=kLoop, calls=%fused_computation.2 | loop fusion | bytes 65536
  0.8 0.0 copy-done.1
  0.8 0.0 copy-start
  0.8 4.0 %collective-permute-start = (bf16[64,512]{1,0:T(8,128)(2,1)S(1)}, bf16[64,512]{1,0:T(8,128)(2,1)S(1)}, u32[]{:S(2)}, u32[]{:S(2)}) collective-permute-start(bf16[64,512]{1,0:T(8,128)(2,1)S(1)} %constant_dynamic-update-slice_fusion), channel_id=1, source_target_pairs={{0,5},{1,4},{2,7},{3,6},{4,1},{5,0},{6,3},{7,2},{8,13},{9,12},{10,... | collective-permute-start | bytes 196616 | tf_op jit(solution)/shard_map/ppermute | solution.py:39
  4.8 3.6 %collective-permute-start.1 = (bf16[64,512]{1,0:T(8,128)(2,1)S(1)}, bf16[64,512]{1,0:T(8,128)(2,1)S(1)}, u32[]{:S(2)}, u32[]{:S(2)}) collective-permute-start(bf16[64,512]{1,0:T(8,128)(2,1)S(1)} %constant_dynamic-update-slice_fusion), channel_id=1, source_target_pairs={{0,24},{1,25},{2,26},{3,27},{4,28},{5,29},{6,30},{7,31},{8,16},{9,... | collective-permute-start | bytes 196616 | tf_op jit(solution)/shard_map/ppermute | solution.py:39
  8.4 0.0 collective-permute-start.2
  8.4 0.8 %collective-permute-start.3 = (bf16[64,512]{1,0:T(8,128)(2,1)S(1)}, bf16[64,512]{1,0:T(8,128)(2,1)S(1)}, u32[]{:S(2)}, u32[]{:S(2)}) collective-permute-start(bf16[64,512]{1,0:T(8,128)(2,1)S(1)} %constant_dynamic-update-slice_fusion), channel_id=1, source_target_pairs={{0,8},{1,9},{2,10},{3,11},{4,12},{5,13},{6,14},{7,15},{8,0},{9,1},... | collective-permute-start | bytes 196616 | tf_op jit(solution)/shard_map/ppermute | solution.py:39
  9.1 0.0 collective-permute-done
  9.1 2.5 %collective-permute-done.1 = bf16[64,512]{1,0:T(8,128)(2,1)S(1)} collective-permute-done((bf16[64,512]{1,0:T(8,128)(2,1)S(1)}, bf16[64,512]{1,0:T(8,128)(2,1)S(1)}, u32[]{:S(2)}, u32[]{:S(2)}) %collective-permute-start.1) | collective-permute-done | bytes 65568 | tf_op jit(solution)/shard_map/ppermute | solution.py:39
  11.6 2.1 %collective-permute-done.2 = bf16[64,512]{1,0:T(8,128)(2,1)S(1)} collective-permute-done((bf16[64,512]{1,0:T(8,128)(2,1)S(1)}, bf16[64,512]{1,0:T(8,128)(2,1)S(1)}, u32[]{:S(2)}, u32[]{:S(2)}) %collective-permute-start.2) | collective-permute-done | bytes 65568 | tf_op jit(solution)/shard_map/ppermute | solution.py:39
  13.7 0.1 collective-permute-done.3
  13.8 0.6 %collective-permute-start.7 = (bf16[256,512]{1,0:T(8,128)(2,1)S(1)}, bf16[256,512]{1,0:T(8,128)(2,1)S(1)}, u32[]{:S(2)}, u32[]{:S(2)}) collective-permute-start(bf16[256,512]{1,0:T(8,128)(2,1)S(1)} %pad_maximum_fusion.refs_1_), channel_id=1, source_target_pairs={{0,4},{1,5},{2,6},{3,7},{4,0},{5,1},{6,2},{7,3},{8,12},{9,13},{10,... | collective-permute-start | bytes 786440 | tf_op jit(solution)/shard_map/ppermute | solution.py:39
  14.4 0.4 %collective-permute-start.8 = (bf16[256,512]{1,0:T(8,128)(2,1)S(1)}, bf16[256,512]{1,0:T(8,128)(2,1)S(1)}, u32[]{:S(2)}, u32[]{:S(2)}) collective-permute-start(bf16[256,512]{1,0:T(8,128)(2,1)S(1)} %pad_maximum_fusion.refs_1_), channel_id=1, source_target_pairs={{0,1},{1,0},{2,3},{3,2},{4,5},{5,4},{6,7},{7,6},{8,9},{9,8},{10,11... | collective-permute-start | bytes 786440 | tf_op jit(solution)/shard_map/ppermute | solution.py:39
  14.8 2.6 %collective-permute-start.4 = (bf16[64,512]{1,0:T(8,128)(2,1)S(1)}, bf16[64,512]{1,0:T(8,128)(2,1)S(1)}, u32[]{:S(2)}, u32[]{:S(2)}) collective-permute-start(bf16[64,512]{1,0:T(8,128)(2,1)S(1)} %collective-permute-done), channel_id=1, source_target_pairs={{0,24},{1,25},{2,26},{3,27},{4,28},{5,29},{6,30},{7,31},{8,16},{9,... | collective-permute-start | bytes 196616 | tf_op jit(solution)/shard_map/ppermute | solution.py:39
  17.5 0.0 collective-permute-start.5
  17.5 1.8 %collective-permute-start.6 = (bf16[64,512]{1,0:T(8,128)(2,1)S(1)}, bf16[64,512]{1,0:T(8,128)(2,1)S(1)}, u32[]{:S(2)}, u32[]{:S(2)}) collective-permute-start(bf16[64,512]{1,0:T(8,128)(2,1)S(1)} %collective-permute-done), channel_id=1, source_target_pairs={{0,8},{1,9},{2,10},{3,11},{4,12},{5,13},{6,14},{7,15},{8,0},{9,1},... | collective-permute-start | bytes 196616 | tf_op jit(solution)/shard_map/ppermute | solution.py:39
  19.2 0.0 copy-done
  19.2 0.5 %shard_map.37 = (f32[2,512,128]{2,1,0:T(8,128)S(1)}, f32[2,512,128]{2,1,0:T(8,128)S(1)}, f32[2,512,128]{2,1,0:T(8,128)S(1)}) custom-call(bf16[64,2048]{1,0:T(8,128)(2,1)S(1)} %copy-done, bf16[256,512]{1,0:T(8,128)(2,1)S(1)} %pad_maximum_fusion.refs_1_), custom_call_target="tpu_custom_call" | custom-call | tf_op jit(solution)/shard_map/pallas_call | solution.py:150
  19.8 1.7 %collective-permute-done.7.refs_4_ = bf16[256,512]{1,0:T(8,128)(2,1)S(1)} collective-permute-done((bf16[256,512]{1,0:T(8,128)(2,1)S(1)}, bf16[256,512]{1,0:T(8,128)(2,1)S(1)}, u32[]{:S(2)}, u32[]{:S(2)}) %collective-permute-start.7) | collective-permute-done | bytes 262176 | tf_op jit(solution)/shard_map/ppermute | solution.py:39
  21.5 0.0 collective-permute-start.9
  21.5 0.2 collective-permute-done.8.refs_5_
  21.7 0.3 %collective-permute-start.10 = (bf16[256,512]{1,0:T(8,128)(2,1)S(1)}, bf16[256,512]{1,0:T(8,128)(2,1)S(1)}, u32[]{:S(2)}, u32[]{:S(2)}) collective-permute-start(bf16[256,512]{1,0:T(8,128)(2,1)S(1)} %collective-permute-done.7.refs_4_), channel_id=1, source_target_pairs={{0,2},{1,3},{2,0},{3,1},{4,6},{5,7},{6,4},{7,5},{8,10},{9,11},{10,... | collective-permute-start | bytes 786440 | tf_op jit(solution)/shard_map/ppermute | solution.py:39
  22.0 0.6 %shard_map.38 = (f32[2,512,128]{2,1,0:T(8,128)S(1)}, f32[2,512,128]{2,1,0:T(8,128)S(1)}, f32[2,512,128]{2,1,0:T(8,128)S(1)}) custom-call(bf16[64,2048]{1,0:T(8,128)(2,1)S(1)} %copy-done, f32[2,512,128]{2,1,0:T(8,128)S(1)} %get-tuple-element.37.refs_1_, f32[2,512,128]{2,1,0:T(8,128)S(1)} %get-tuple-element.38.refs_2_, ...), custom_call_target="tpu_custom_call" | custom-call | tf_op jit(solution)/shard_map/pallas_call | solution.py:150
  22.6 0.0 collective-permute-done.4
  22.6 0.3 %collective-permute-start.11 = (bf16[256,512]{1,0:T(8,128)(2,1)S(1)}, bf16[256,512]{1,0:T(8,128)(2,1)S(1)}, u32[]{:S(2)}, u32[]{:S(2)}) collective-permute-start(bf16[256,512]{1,0:T(8,128)(2,1)S(1)} %collective-permute-done.8.refs_5_), channel_id=1, source_target_pairs={{0,2},{1,3},{2,0},{3,1},{4,6},{5,7},{6,4},{7,5},{8,10},{9,11},{10,... | collective-permute-start | bytes 786440 | tf_op jit(solution)/shard_map/ppermute | solution.py:39
  22.9 0.0 collective-permute-done.5
  22.9 0.0 collective-permute-done.6
  22.9 0.4 %collective-permute-start.12 = (bf16[256,512]{1,0:T(8,128)(2,1)S(1)}, bf16[256,512]{1,0:T(8,128)(2,1)S(1)}, u32[]{:S(2)}, u32[]{:S(2)}) collective-permute-start(bf16[256,512]{1,0:T(8,128)(2,1)S(1)} %constant_dynamic-update-slice_fusion.2.refs_4_), channel_id=1, source_target_pairs={{0,2},{1,3},{2,0},{3,1},{4,6},{5,7},{6,4},{7,5},{8,10},{9,11},{10,... | collective-permute-start | bytes 786440 | tf_op jit(solution)/shard_map/ppermute | solution.py:39
  23.3 0.0 collective-permute-done.9.refs_4_
  23.3 0.1 collective-permute-done.10.refs_5_
  23.4 0.8 %collective-permute-done.11.refs_6_ = bf16[256,512]{1,0:T(8,128)(2,1)S(1)} collective-permute-done((bf16[256,512]{1,0:T(8,128)(2,1)S(1)}, bf16[256,512]{1,0:T(8,128)(2,1)S(1)}, u32[]{:S(2)}, u32[]{:S(2)}) %collective-permute-start.11) | collective-permute-done | bytes 262176 | tf_op jit(solution)/shard_map/ppermute | solution.py:39
  24.2 0.9 %shard_map.39 = (f32[2,512,128]{2,1,0:T(8,128)S(1)}, f32[2,512,128]{2,1,0:T(8,128)S(1)}, f32[2,512,128]{2,1,0:T(8,128)S(1)}) custom-call(bf16[64,2048]{1,0:T(8,128)(2,1)S(1)} %copy-done, f32[2,512,128]{2,1,0:T(8,128)S(1)} %get-tuple-element.45.refs_1_, f32[2,512,128]{2,1,0:T(8,128)S(1)} %get-tuple-element.46.refs_2_, ...), custom_call_target="tpu_custom_call" | custom-call | tf_op jit(solution)/shard_map/pallas_call | solution.py:150
  25.1 0.0 collective-permute-done.12.refs_5_
  25.1 1.3 %shard_map.40 = bf16[64,2048]{1,0:T(8,128)(2,1)} custom-call(bf16[64,2048]{1,0:T(8,128)(2,1)S(1)} %copy-done, f32[2,512,128]{2,1,0:T(8,128)S(1)} %get-tuple-element.48.refs_1_, f32[2,512,128]{2,1,0:T(8,128)S(1)} %get-tuple-element.49.refs_2_, f32[2,512,128]{2,1,0:T(8,128)S(1)} %get-tuple-element.50.refs_3_, ...), custom_call_target="tpu_custom_call" | custom-call | tf_op jit(solution)/shard_map/pallas_call | solution.py:150
  (6 shorter events, 0.0 us)
Async XLA Ops:
  0.0 0.8 %copy-start.1 = (bf16[64,256]{1,0:T(8,128)(2,1)S(1)}, bf16[64,256]{1,0:T(8,128)(2,1)}, u32[]{:S(2)}) copy-start(bf16[64,256]{1,0:T(8,128)(2,1)} %param.5) | copy-start | bytes 98308
  0.8 18.4 %copy-start = (bf16[64,2048]{1,0:T(8,128)(2,1)S(1)}, bf16[64,2048]{1,0:T(8,128)(2,1)}, u32[]{:S(2)}) copy-start(bf16[64,2048]{1,0:T(8,128)(2,1)} %refs_0_.7) | copy-start | bytes 786436
  0.8 8.4 %collective-permute-start = (bf16[64,512]{1,0:T(8,128)(2,1)S(1)}, bf16[64,512]{1,0:T(8,128)(2,1)S(1)}, u32[]{:S(2)}, u32[]{:S(2)}) collective-permute-start(bf16[64,512]{1,0:T(8,128)(2,1)S(1)} %constant_dynamic-update-slice_fusion), channel_id=1, source_target_pairs={{0,5},{1,4},{2,7},{3,6},{4,1},{5,0},{6,3},{7,2},{8,13},{9,12},{10,... | collective-permute-start | bytes 196616 | tf_op jit(solution)/shard_map/ppermute | solution.py:39
  4.8 6.9 %collective-permute-start.1 = (bf16[64,512]{1,0:T(8,128)(2,1)S(1)}, bf16[64,512]{1,0:T(8,128)(2,1)S(1)}, u32[]{:S(2)}, u32[]{:S(2)}) collective-permute-start(bf16[64,512]{1,0:T(8,128)(2,1)S(1)} %constant_dynamic-update-slice_fusion), channel_id=1, source_target_pairs={{0,24},{1,25},{2,26},{3,27},{4,28},{5,29},{6,30},{7,31},{8,16},{9,... | collective-permute-start | bytes 196616 | tf_op jit(solution)/shard_map/ppermute | solution.py:39
  8.4 5.4 %collective-permute-start.2 = (bf16[64,512]{1,0:T(8,128)(2,1)S(1)}, bf16[64,512]{1,0:T(8,128)(2,1)S(1)}, u32[]{:S(2)}, u32[]{:S(2)}) collective-permute-start(bf16[64,512]{1,0:T(8,128)(2,1)S(1)} %constant_dynamic-update-slice_fusion), channel_id=1, source_target_pairs={{0,16},{1,17},{2,18},{3,19},{4,20},{5,21},{6,22},{7,23},{8,24},{9,... | collective-permute-start | bytes 196616 | tf_op jit(solution)/shard_map/ppermute | solution.py:39
  8.4 5.4 %collective-permute-start.3 = (bf16[64,512]{1,0:T(8,128)(2,1)S(1)}, bf16[64,512]{1,0:T(8,128)(2,1)S(1)}, u32[]{:S(2)}, u32[]{:S(2)}) collective-permute-start(bf16[64,512]{1,0:T(8,128)(2,1)S(1)} %constant_dynamic-update-slice_fusion), channel_id=1, source_target_pairs={{0,8},{1,9},{2,10},{3,11},{4,12},{5,13},{6,14},{7,15},{8,0},{9,1},... | collective-permute-start | bytes 196616 | tf_op jit(solution)/shard_map/ppermute | solution.py:39
  13.8 7.7 %collective-permute-start.7 = (bf16[256,512]{1,0:T(8,128)(2,1)S(1)}, bf16[256,512]{1,0:T(8,128)(2,1)S(1)}, u32[]{:S(2)}, u32[]{:S(2)}) collective-permute-start(bf16[256,512]{1,0:T(8,128)(2,1)S(1)} %pad_maximum_fusion.refs_1_), channel_id=1, source_target_pairs={{0,4},{1,5},{2,6},{3,7},{4,0},{5,1},{6,2},{7,3},{8,12},{9,13},{10,... | collective-permute-start | bytes 786440 | tf_op jit(solution)/shard_map/ppermute | solution.py:39
  14.4 7.3 %collective-permute-start.8 = (bf16[256,512]{1,0:T(8,128)(2,1)S(1)}, bf16[256,512]{1,0:T(8,128)(2,1)S(1)}, u32[]{:S(2)}, u32[]{:S(2)}) collective-permute-start(bf16[256,512]{1,0:T(8,128)(2,1)S(1)} %pad_maximum_fusion.refs_1_), channel_id=1, source_target_pairs={{0,1},{1,0},{2,3},{3,2},{4,5},{5,4},{6,7},{7,6},{8,9},{9,8},{10,11... | collective-permute-start | bytes 786440 | tf_op jit(solution)/shard_map/ppermute | solution.py:39
  14.8 7.8 %collective-permute-start.4 = (bf16[64,512]{1,0:T(8,128)(2,1)S(1)}, bf16[64,512]{1,0:T(8,128)(2,1)S(1)}, u32[]{:S(2)}, u32[]{:S(2)}) collective-permute-start(bf16[64,512]{1,0:T(8,128)(2,1)S(1)} %collective-permute-done), channel_id=1, source_target_pairs={{0,24},{1,25},{2,26},{3,27},{4,28},{5,29},{6,30},{7,31},{8,16},{9,... | collective-permute-start | bytes 196616 | tf_op jit(solution)/shard_map/ppermute | solution.py:39
  17.5 5.4 %collective-permute-start.5 = (bf16[64,512]{1,0:T(8,128)(2,1)S(1)}, bf16[64,512]{1,0:T(8,128)(2,1)S(1)}, u32[]{:S(2)}, u32[]{:S(2)}) collective-permute-start(bf16[64,512]{1,0:T(8,128)(2,1)S(1)} %collective-permute-done), channel_id=1, source_target_pairs={{0,16},{1,17},{2,18},{3,19},{4,20},{5,21},{6,22},{7,23},{8,24},{9,... | collective-permute-start | bytes 196616 | tf_op jit(solution)/shard_map/ppermute | solution.py:39
  17.5 5.4 %collective-permute-start.6 = (bf16[64,512]{1,0:T(8,128)(2,1)S(1)}, bf16[64,512]{1,0:T(8,128)(2,1)S(1)}, u32[]{:S(2)}, u32[]{:S(2)}) collective-permute-start(bf16[64,512]{1,0:T(8,128)(2,1)S(1)} %collective-permute-done), channel_id=1, source_target_pairs={{0,8},{1,9},{2,10},{3,11},{4,12},{5,13},{6,14},{7,15},{8,0},{9,1},... | collective-permute-start | bytes 196616 | tf_op jit(solution)/shard_map/ppermute | solution.py:39
  21.5 1.8 %collective-permute-start.9 = (bf16[256,512]{1,0:T(8,128)(2,1)S(1)}, bf16[256,512]{1,0:T(8,128)(2,1)S(1)}, u32[]{:S(2)}, u32[]{:S(2)}) collective-permute-start(bf16[256,512]{1,0:T(8,128)(2,1)S(1)} %pad_maximum_fusion.refs_1_), channel_id=1, source_target_pairs={{0,2},{1,3},{2,0},{3,1},{4,6},{5,7},{6,4},{7,5},{8,10},{9,11},{10,... | collective-permute-start | bytes 786440 | tf_op jit(solution)/shard_map/ppermute | solution.py:39
  21.7 1.7 %collective-permute-start.10 = (bf16[256,512]{1,0:T(8,128)(2,1)S(1)}, bf16[256,512]{1,0:T(8,128)(2,1)S(1)}, u32[]{:S(2)}, u32[]{:S(2)}) collective-permute-start(bf16[256,512]{1,0:T(8,128)(2,1)S(1)} %collective-permute-done.7.refs_4_), channel_id=1, source_target_pairs={{0,2},{1,3},{2,0},{3,1},{4,6},{5,7},{6,4},{7,5},{8,10},{9,11},{10,... | collective-permute-start | bytes 786440 | tf_op jit(solution)/shard_map/ppermute | solution.py:39
  22.6 1.6 %collective-permute-start.11 = (bf16[256,512]{1,0:T(8,128)(2,1)S(1)}, bf16[256,512]{1,0:T(8,128)(2,1)S(1)}, u32[]{:S(2)}, u32[]{:S(2)}) collective-permute-start(bf16[256,512]{1,0:T(8,128)(2,1)S(1)} %collective-permute-done.8.refs_5_), channel_id=1, source_target_pairs={{0,2},{1,3},{2,0},{3,1},{4,6},{5,7},{6,4},{7,5},{8,10},{9,11},{10,... | collective-permute-start | bytes 786440 | tf_op jit(solution)/shard_map/ppermute | solution.py:39
  22.9 2.2 %collective-permute-start.12 = (bf16[256,512]{1,0:T(8,128)(2,1)S(1)}, bf16[256,512]{1,0:T(8,128)(2,1)S(1)}, u32[]{:S(2)}, u32[]{:S(2)}) collective-permute-start(bf16[256,512]{1,0:T(8,128)(2,1)S(1)} %constant_dynamic-update-slice_fusion.2.refs_4_), channel_id=1, source_target_pairs={{0,2},{1,3},{2,0},{3,1},{4,6},{5,7},{6,4},{7,5},{8,10},{9,11},{10,... | collective-permute-start | bytes 786440 | tf_op jit(solution)/shard_map/ppermute | solution.py:39

commit v6 on v5

--- a/solution.py
+++ b/solution.py
@@ -12,6 +12,8 @@
 AXES = ("ctx", "kvh")
 CORES = 2
 HIDDEN = -1e30
+HERE = (0, 0)
+SELF = (HERE, 0, 0, 0)
 
 
 class Layout:
@@ -31,12 +33,14 @@
     def join(self, plane, line, core, column):
         return ((plane * self.lines + line) * CORES + core) * self.across + column
 
-    def partner(self, rank, up=0, line=0, swap=0, column=0):
+    def partner(self, rank, steps):
+        (even, odd), line, swap, column = steps
         place = self.split(rank)
+        up = even * (1 - place[2]) + odd * place[2]
         return self.join(place[0] ^ up, place[1] ^ line, place[2] ^ swap, place[3] ^ column)
 
-    def exchange(self, array, **steps):
-        return lax.ppermute(array, AXES, [(rank, self.partner(rank, **steps)) for rank in range(self.size)])
+    def exchange(self, array, steps):
+        return lax.ppermute(array, AXES, [(rank, self.partner(rank, steps)) for rank in range(self.size)])
 
     def here(self):
         return lax.axis_index("ctx") * self.across + lax.axis_index("kvh")
@@ -44,7 +48,7 @@
 
 def fold_kernel(layout, sources, rows, groups, carried, last, *refs):
     plane = layout.split(layout.here())[0]
-    level = [[steps for steps in piece if steps[0] == 0] for piece in sources]
+    level = [[steps for steps in piece if steps[0] == HERE] for piece in sources]
     assert all(piece[: len(flat)] == flat for piece, flat in zip(sources, level, strict=True))
     if level == sources:
         fold_blocks(layout, sources, rows, groups, carried, last, *refs)
@@ -75,15 +79,30 @@
     rank = layout.here()
     along = lax.broadcasted_iota(jnp.int32, (1, width), 1)
     bias = jnp.zeros((1, width), jnp.float32)
-    for at, (up, line, swap, column) in enumerate(blocks):
-        hidden = layout.partner(rank, up, line, swap, column) > rank
+    for at, steps in enumerate(blocks):
+        hidden = layout.partner(rank, steps) > rank
         bias = jnp.where(along // rows == at, jnp.where(hidden, HIDDEN, 0.0).astype(jnp.float32), bias)
-    own = blocks.index((0, 0, 0, 0)) * rows if (0, 0, 0, 0) in blocks else None
+    own = blocks.index(SELF) * rows if SELF in blocks else None
     if own is not None:
         token = lax.broadcasted_iota(jnp.int32, (rows, width), 0)
         place = lax.broadcasted_iota(jnp.int32, (rows, width), 1) - own
         later = jnp.logical_and(place < rows, place > token)
         bias = jnp.where(jnp.logical_and(place >= 0, later), HIDDEN, bias)
+
+    def write(group, largest, totals, summed):
+        if last:
+            first = group * heads * HD
+            result = (summed / totals).astype(jnp.bfloat16)
+            for h in range(heads):
+                out_refs[0][:, first + h * HD : first + (h + 1) * HD] = result[h * rows : (h + 1) * rows]
+        else:
+            for ref, array in zip(out_refs, (largest, totals, summed), strict=True):
+                ref[group] = array
+
+    if not blocks:
+        for group in range(groups):
+            write(group, *(ref[group] for ref in state_refs))
+        return
 
     def score(group):
         first = group * heads * HD
@@ -122,14 +141,7 @@
             decay = jnp.exp2(state_refs[0][group] - largest)
             totals = totals + state_refs[1][group] * decay
             summed = summed + state_refs[2][group] * decay
-        if last:
-            first = group * heads * HD
-            result = (summed / totals).astype(jnp.bfloat16)
-            for h in range(heads):
-                out_refs[0][:, first + h * HD : first + (h + 1) * HD] = result[h * rows : (h + 1) * rows]
-        else:
-            for ref, array in zip(out_refs, (largest, totals, summed), strict=True):
-                ref[group] = array
+        write(group, largest, totals, summed)
 
     for begin in range(0, groups, 2):
         both = range(begin, min(begin + 2, groups))
@@ -165,46 +177,56 @@
 
     def per_device(queries, keys, values):
         groups = keys.shape[1] // HD
-        exchange = layout.exchange
+        go = layout.exchange
         block = jnp.concatenate([keys, values], axis=1)
-        ups = range(1, layout.planes)
+        ups = list(range(layout.planes - 1, 0, -1))
         lines = range(1, layout.lines)
         columns = range(1, layout.across)
-        side_steps = [(0, l, 0, 0) for l in lines] + [(0, 0, 0, c) for c in columns]
-        corner_steps = [(0, l, 0, c) for l in lines for c in columns]
-        above_steps = [(up, 0, 0, 0) for up in reversed(ups)]
-
-        def go(array, steps):
-            return exchange(array, up=steps[0], line=steps[1], swap=steps[2], column=steps[3])
+        side_steps = [(HERE, l, 0, 0) for l in lines] + [(HERE, 0, 0, c) for c in columns]
+        corner_steps = [(HERE, l, 0, c) for l in lines for c in columns]
+        above_steps = [((up, up), 0, 0, 0) for up in ups]
+        if layout.planes == 4:
+            above_steps = [(pair, 0, 0, 0) for pair in [(3, 3), (2, 2), (1, 1)]]
+        far_above = [(pair, 0, 0, 0) for pair in [(3, 3), (2, 2), (1, 1)]] if layout.planes == 4 else above_steps
+        tower_steps = [SELF] + above_steps
 
         def moved(steps, by):
-            return [tuple(a ^ b for a, b in zip(one, by, strict=True)) for one in steps]
+            def add(one):
+                up = (one[0][0] ^ by[0][0], one[0][1] ^ by[0][1])
+                return up, one[1] ^ by[1], one[2] ^ by[2], one[3] ^ by[3]
+
+            return [add(one) for one in steps]
 
         def swapped(pieces):
-            return [(exchange(array, swap=1), moved(steps, (0, 0, 1, 0))) for array, steps in pieces]
-
-        corner = [go(block, steps) for steps in corner_steps]
-        corner = jnp.concatenate(corner, axis=0) if len(corner) > 1 else corner[0]
-        tower_steps = [(0, 0, 0, 0)] + above_steps
-        corner, above = lax.optimization_barrier((corner, [go(block, steps) for steps in above_steps]))
-        near = [(jnp.concatenate([block] + above, axis=0), tower_steps)]
-        far = [(corner, corner_steps)]
-        far += [(go(corner, steps), moved(corner_steps, steps)) for steps in above_steps]
-        sides = [(go(near[0][0], steps), moved(tower_steps, steps)) for steps in side_steps]
+            turned = [(go(array, (HERE, 0, 1, 0)), steps) for array, steps in pieces]
+            return [(array, [(up[::-1], l, 1 - swap, c) for up, l, swap, c in steps]) for array, steps in turned]
+
+        def join(pieces):
+            if len(pieces) == 1:
+                return pieces[0]
+            return jnp.concatenate([x for x, _ in pieces], axis=0), [one for _, steps in pieces for one in steps]
 
         def after(pieces, state):
             arrays, state = lax.optimization_barrier(([array for array, _ in pieces], state))
             return [(array, steps) for array, (_, steps) in zip(arrays, pieces, strict=True)], state
 
+        corner = join([(go(block, steps), [steps]) for steps in corner_steps])
+        corner_array, above = lax.optimization_barrier((corner[0], [go(block, steps) for steps in above_steps]))
+        corner = (corner_array, corner[1])
+        near = [(jnp.concatenate([block] + above, axis=0), tower_steps)]
+        sides = [(go(near[0][0], steps), moved(tower_steps, steps)) for steps in side_steps]
+        far = [corner] + [(go(corner[0], steps), moved(corner[1], steps)) for steps in far_above]
+
         state = fold(layout, queries, None, near, groups)
         sides, state = after(sides, state)
-        others = swapped(near) + swapped(sides)
+        side_others = swapped(sides)
         state = fold(layout, queries, state, sides, groups)
-        far, state = after(far, state)
-        far = [(jnp.concatenate([x for x, _ in far], axis=0), [one for _, steps in far for one in steps])]
-        far_others = swapped(far)
-        state = fold(layout, queries, state, others, groups)
-        return fold(layout, queries, state, far + far_others, groups, last=True)
+        rest, state = after(far + near, state)
+        far, near = rest[:-1], rest[-1:]
+        far = [join(far)]
+        others = swapped(far) + swapped(near)
+        state = fold(layout, queries, state, side_others + far, groups)
+        return fold(layout, queries, state, others, groups, last=True)
 
     placed = P(AXES, None)
     return jax.shard_map(

time: 26.6 us -> 26.3 us (0.989)
  waiting for transfers between devices: 7.5 us -> 7.12 us
    ppermute x13, waiting for transfers between devices: 7.5 us -> 7.12 us  [exchange(): lax.ppermute(array, AXES, [(rank, self.partner(rank, steps)) for rank in...]
where the time goes in v6:
time: 26.3 us; the launch traced here: 26.2 us
  starting transfers between devices  14.8 us (56%)
  waiting for transfers between devices  7.12 us (27%)
  Pallas kernels  3.3 us (13%)
  local copies, waits for them, and re-layouts  0.81 us (3%)
    ppermute x13, starting transfers between devices, exchange(): lax.ppermute(array, AXES, [(rank, self.partner(rank, steps)) for rank in...  14.8 us
    ppermute x13, waiting for transfers between devices, exchange(): lax.ppermute(array, AXES, [(rank, self.partner(rank, steps)) for rank in...  7.12 us
    pallas_call x4, Pallas kernels, fold(): pl.pallas_call(functools.partial(fold_kernel, layout, [blocks for _, bloc...  3.3 us
    unnamed x8, local copies, waits for them, and re-layouts  0.8 us
  transfers between devices with their start and end apart: 13, of which 7 were waited for; matrix products, arithmetic and copies ran while one was open for 0% of the time, Pallas kernels for 8%

profile of v6, /device:TPU:0, one launch (start us, length us, event | category | flops | bytes accessed | tf_op | source)
XLA Modules:
  0.0 26.2 jit_solution(1028884511602048751)
XLA Ops:
  0.0 0.0 copy-start.1
  0.0 0.8 %constant_dynamic-update-slice_fusion.1 = bf16[64,512]{1,0:T(8,128)(2,1)S(1)} fusion(bf16[64,256]{1,0:T(8,128)(2,1)} %param.4), kind=kLoop, calls=%fused_computation.2 | loop fusion | bytes 65536
  0.8 0.0 copy-done.1
  0.8 0.0 copy-start
  0.8 4.0 %collective-permute-start = (bf16[64,512]{1,0:T(8,128)(2,1)S(1)}, bf16[64,512]{1,0:T(8,128)(2,1)S(1)}, u32[]{:S(2)}, u32[]{:S(2)}) collective-permute-start(bf16[64,512]{1,0:T(8,128)(2,1)S(1)} %constant_dynamic-update-slice_fusion), channel_id=1, source_target_pairs={{0,5},{1,4},{2,7},{3,6},{4,1},{5,0},{6,3},{7,2},{8,13},{9,12},{10,... | collective-permute-start | bytes 196616 | tf_op jit(solution)/shard_map/ppermute | solution.py:43
  4.8 3.6 %collective-permute-start.1 = (bf16[64,512]{1,0:T(8,128)(2,1)S(1)}, bf16[64,512]{1,0:T(8,128)(2,1)S(1)}, u32[]{:S(2)}, u32[]{:S(2)}) collective-permute-start(bf16[64,512]{1,0:T(8,128)(2,1)S(1)} %constant_dynamic-update-slice_fusion), channel_id=1, source_target_pairs={{0,24},{1,25},{2,26},{3,27},{4,28},{5,29},{6,30},{7,31},{8,16},{9,... | collective-permute-start | bytes 196616 | tf_op jit(solution)/shard_map/ppermute | solution.py:43
  8.4 0.0 collective-permute-start.2
  8.4 0.8 %collective-permute-start.3 = (bf16[64,512]{1,0:T(8,128)(2,1)S(1)}, bf16[64,512]{1,0:T(8,128)(2,1)S(1)}, u32[]{:S(2)}, u32[]{:S(2)}) collective-permute-start(bf16[64,512]{1,0:T(8,128)(2,1)S(1)} %constant_dynamic-update-slice_fusion), channel_id=1, source_target_pairs={{0,8},{1,9},{2,10},{3,11},{4,12},{5,13},{6,14},{7,15},{8,0},{9,1},... | collective-permute-start | bytes 196616 | tf_op jit(solution)/shard_map/ppermute | solution.py:43
  9.1 0.0 collective-permute-done
  9.1 2.5 %collective-permute-done.1 = bf16[64,512]{1,0:T(8,128)(2,1)S(1)} collective-permute-done((bf16[64,512]{1,0:T(8,128)(2,1)S(1)}, bf16[64,512]{1,0:T(8,128)(2,1)S(1)}, u32[]{:S(2)}, u32[]{:S(2)}) %collective-permute-start.1) | collective-permute-done | bytes 65568 | tf_op jit(solution)/shard_map/ppermute | solution.py:43
  11.6 2.1 %collective-permute-done.2 = bf16[64,512]{1,0:T(8,128)(2,1)S(1)} collective-permute-done((bf16[64,512]{1,0:T(8,128)(2,1)S(1)}, bf16[64,512]{1,0:T(8,128)(2,1)S(1)}, u32[]{:S(2)}, u32[]{:S(2)}) %collective-permute-start.2) | collective-permute-done | bytes 65568 | tf_op jit(solution)/shard_map/ppermute | solution.py:43
  13.7 0.1 collective-permute-done.3
  13.8 0.6 %collective-permute-start.7 = (bf16[256,512]{1,0:T(8,128)(2,1)S(1)}, bf16[256,512]{1,0:T(8,128)(2,1)S(1)}, u32[]{:S(2)}, u32[]{:S(2)}) collective-permute-start(bf16[256,512]{1,0:T(8,128)(2,1)S(1)} %pad_maximum_fusion.refs_1_), channel_id=1, source_target_pairs={{0,4},{1,5},{2,6},{3,7},{4,0},{5,1},{6,2},{7,3},{8,12},{9,13},{10,... | collective-permute-start | bytes 786440 | tf_op jit(solution)/shard_map/ppermute | solution.py:43
  14.4 0.4 %collective-permute-start.8 = (bf16[256,512]{1,0:T(8,128)(2,1)S(1)}, bf16[256,512]{1,0:T(8,128)(2,1)S(1)}, u32[]{:S(2)}, u32[]{:S(2)}) collective-permute-start(bf16[256,512]{1,0:T(8,128)(2,1)S(1)} %pad_maximum_fusion.refs_1_), channel_id=1, source_target_pairs={{0,1},{1,0},{2,3},{3,2},{4,5},{5,4},{6,7},{7,6},{8,9},{9,8},{10,11... | collective-permute-start | bytes 786440 | tf_op jit(solution)/shard_map/ppermute | solution.py:43
  14.8 2.6 %collective-permute-start.4 = (bf16[64,512]{1,0:T(8,128)(2,1)S(1)}, bf16[64,512]{1,0:T(8,128)(2,1)S(1)}, u32[]{:S(2)}, u32[]{:S(2)}) collective-permute-start(bf16[64,512]{1,0:T(8,128)(2,1)S(1)} %collective-permute-done), channel_id=1, source_target_pairs={{0,24},{1,25},{2,26},{3,27},{4,28},{5,29},{6,30},{7,31},{8,16},{9,... | collective-permute-start | bytes 196616 | tf_op jit(solution)/shard_map/ppermute | solution.py:43
  17.5 0.0 collective-permute-start.5
  17.5 1.8 %collective-permute-start.6 = (bf16[64,512]{1,0:T(8,128)(2,1)S(1)}, bf16[64,512]{1,0:T(8,128)(2,1)S(1)}, u32[]{:S(2)}, u32[]{:S(2)}) collective-permute-start(bf16[64,512]{1,0:T(8,128)(2,1)S(1)} %collective-permute-done), channel_id=1, source_target_pairs={{0,8},{1,9},{2,10},{3,11},{4,12},{5,13},{6,14},{7,15},{8,0},{9,1},... | collective-permute-start | bytes 196616 | tf_op jit(solution)/shard_map/ppermute | solution.py:43
  19.2 0.0 copy-done
  19.2 0.5 %shard_map.37 = (f32[2,512,128]{2,1,0:T(8,128)S(1)}, f32[2,512,128]{2,1,0:T(8,128)S(1)}, f32[2,512,128]{2,1,0:T(8,128)S(1)}) custom-call(bf16[64,2048]{1,0:T(8,128)(2,1)S(1)} %copy-done, bf16[256,512]{1,0:T(8,128)(2,1)S(1)} %pad_maximum_fusion.refs_1_), custom_call_target="tpu_custom_call" | custom-call | tf_op jit(solution)/shard_map/pallas_call | solution.py:162
  19.8 1.7 %collective-permute-done.7.refs_4_ = bf16[256,512]{1,0:T(8,128)(2,1)S(1)} collective-permute-done((bf16[256,512]{1,0:T(8,128)(2,1)S(1)}, bf16[256,512]{1,0:T(8,128)(2,1)S(1)}, u32[]{:S(2)}, u32[]{:S(2)}) %collective-permute-start.7) | collective-permute-done | bytes 262176 | tf_op jit(solution)/shard_map/ppermute | solution.py:43
  21.5 0.2 collective-permute-done.8.refs_5_
  21.7 0.0 collective-permute-start.10
  21.7 0.5 %collective-permute-start.9 = (bf16[256,512]{1,0:T(8,128)(2,1)S(1)}, bf16[256,512]{1,0:T(8,128)(2,1)S(1)}, u32[]{:S(2)}, u32[]{:S(2)}) collective-permute-start(bf16[256,512]{1,0:T(8,128)(2,1)S(1)} %collective-permute-done.7.refs_4_), channel_id=1, source_target_pairs={{0,2},{1,3},{2,0},{3,1},{4,6},{5,7},{6,4},{7,5},{8,10},{9,11},{10,... | collective-permute-start | bytes 786440 | tf_op jit(solution)/shard_map/ppermute | solution.py:43
  22.2 0.6 %shard_map.38 = (f32[2,512,128]{2,1,0:T(8,128)S(1)}, f32[2,512,128]{2,1,0:T(8,128)S(1)}, f32[2,512,128]{2,1,0:T(8,128)S(1)}) custom-call(bf16[64,2048]{1,0:T(8,128)(2,1)S(1)} %copy-done, f32[2,512,128]{2,1,0:T(8,128)S(1)} %get-tuple-element.38.refs_1_, f32[2,512,128]{2,1,0:T(8,128)S(1)} %get-tuple-element.39.refs_2_, ...), custom_call_target="tpu_custom_call" | custom-call | tf_op jit(solution)/shard_map/pallas_call | solution.py:162
  22.8 0.0 collective-permute-done.4
  22.8 0.0 collective-permute-done.5
  22.8 0.0 collective-permute-done.6
  22.9 0.1 collective-permute-start.11
  23.0 0.5 %collective-permute-start.12 = (bf16[256,512]{1,0:T(8,128)(2,1)S(1)}, bf16[256,512]{1,0:T(8,128)(2,1)S(1)}, u32[]{:S(2)}, u32[]{:S(2)}) collective-permute-start(bf16[256,512]{1,0:T(8,128)(2,1)S(1)} %pad_maximum_fusion.refs_1_), channel_id=1, source_target_pairs={{0,2},{1,3},{2,0},{3,1},{4,6},{5,7},{6,4},{7,5},{8,10},{9,11},{10,... | collective-permute-start | bytes 786440 | tf_op jit(solution)/shard_map/ppermute | solution.py:43
  23.5 0.0 collective-permute-done.10.refs_5_
  23.5 0.1 collective-permute-done.9.refs_4_
  23.6 0.9 %shard_map.39 = (f32[2,512,128]{2,1,0:T(8,128)S(1)}, f32[2,512,128]{2,1,0:T(8,128)S(1)}, f32[2,512,128]{2,1,0:T(8,128)S(1)}) custom-call(bf16[64,2048]{1,0:T(8,128)(2,1)S(1)} %copy-done, f32[2,512,128]{2,1,0:T(8,128)S(1)} %get-tuple-element.46.refs_1_, f32[2,512,128]{2,1,0:T(8,128)S(1)} %get-tuple-element.47.refs_2_, ...), custom_call_target="tpu_custom_call" | custom-call | tf_op jit(solution)/shard_map/pallas_call | solution.py:162
  24.5 0.0 collective-permute-done.11.refs_4_
  24.5 0.3 %collective-permute-done.12.refs_5_ = bf16[256,512]{1,0:T(8,128)(2,1)S(1)} collective-permute-done((bf16[256,512]{1,0:T(8,128)(2,1)S(1)}, bf16[256,512]{1,0:T(8,128)(2,1)S(1)}, u32[]{:S(2)}, u32[]{:S(2)}) %collective-permute-start.12) | collective-permute-done | bytes 262176 | tf_op jit(solution)/shard_map/ppermute | solution.py:43
  24.9 1.3 %shard_map.40 = bf16[64,2048]{1,0:T(8,128)(2,1)} custom-call(bf16[64,2048]{1,0:T(8,128)(2,1)S(1)} %copy-done, f32[2,512,128]{2,1,0:T(8,128)S(1)} %get-tuple-element.53.refs_1_, f32[2,512,128]{2,1,0:T(8,128)S(1)} %get-tuple-element.54.refs_2_, f32[2,512,128]{2,1,0:T(8,128)S(1)} %get-tuple-element.55.refs_3_, ...), custom_call_target="tpu_custom_call" | custom-call | tf_op jit(solution)/shard_map/pallas_call | solution.py:162
  (6 shorter events, 0.0 us)
Async XLA Ops:
  0.0 0.8 %copy-start.1 = (bf16[64,256]{1,0:T(8,128)(2,1)S(1)}, bf16[64,256]{1,0:T(8,128)(2,1)}, u32[]{:S(2)}) copy-start(bf16[64,256]{1,0:T(8,128)(2,1)} %param.5) | copy-start | bytes 98308
  0.8 18.4 %copy-start = (bf16[64,2048]{1,0:T(8,128)(2,1)S(1)}, bf16[64,2048]{1,0:T(8,128)(2,1)}, u32[]{:S(2)}) copy-start(bf16[64,2048]{1,0:T(8,128)(2,1)} %refs_0_.7) | copy-start | bytes 786436
  0.8 8.4 %collective-permute-start = (bf16[64,512]{1,0:T(8,128)(2,1)S(1)}, bf16[64,512]{1,0:T(8,128)(2,1)S(1)}, u32[]{:S(2)}, u32[]{:S(2)}) collective-permute-start(bf16[64,512]{1,0:T(8,128)(2,1)S(1)} %constant_dynamic-update-slice_fusion), channel_id=1, source_target_pairs={{0,5},{1,4},{2,7},{3,6},{4,1},{5,0},{6,3},{7,2},{8,13},{9,12},{10,... | collective-permute-start | bytes 196616 | tf_op jit(solution)/shard_map/ppermute | solution.py:43
  4.8 6.9 %collective-permute-start.1 = (bf16[64,512]{1,0:T(8,128)(2,1)S(1)}, bf16[64,512]{1,0:T(8,128)(2,1)S(1)}, u32[]{:S(2)}, u32[]{:S(2)}) collective-permute-start(bf16[64,512]{1,0:T(8,128)(2,1)S(1)} %constant_dynamic-update-slice_fusion), channel_id=1, source_target_pairs={{0,24},{1,25},{2,26},{3,27},{4,28},{5,29},{6,30},{7,31},{8,16},{9,... | collective-permute-start | bytes 196616 | tf_op jit(solution)/shard_map/ppermute | solution.py:43
  8.4 5.4 %collective-permute-start.2 = (bf16[64,512]{1,0:T(8,128)(2,1)S(1)}, bf16[64,512]{1,0:T(8,128)(2,1)S(1)}, u32[]{:S(2)}, u32[]{:S(2)}) collective-permute-start(bf16[64,512]{1,0:T(8,128)(2,1)S(1)} %constant_dynamic-update-slice_fusion), channel_id=1, source_target_pairs={{0,16},{1,17},{2,18},{3,19},{4,20},{5,21},{6,22},{7,23},{8,24},{9,... | collective-permute-start | bytes 196616 | tf_op jit(solution)/shard_map/ppermute | solution.py:43
  8.4 5.4 %collective-permute-start.3 = (bf16[64,512]{1,0:T(8,128)(2,1)S(1)}, bf16[64,512]{1,0:T(8,128)(2,1)S(1)}, u32[]{:S(2)}, u32[]{:S(2)}) collective-permute-start(bf16[64,512]{1,0:T(8,128)(2,1)S(1)} %constant_dynamic-update-slice_fusion), channel_id=1, source_target_pairs={{0,8},{1,9},{2,10},{3,11},{4,12},{5,13},{6,14},{7,15},{8,0},{9,1},... | collective-permute-start | bytes 196616 | tf_op jit(solution)/shard_map/ppermute | solution.py:43
  13.8 7.7 %collective-permute-start.7 = (bf16[256,512]{1,0:T(8,128)(2,1)S(1)}, bf16[256,512]{1,0:T(8,128)(2,1)S(1)}, u32[]{:S(2)}, u32[]{:S(2)}) collective-permute-start(bf16[256,512]{1,0:T(8,128)(2,1)S(1)} %pad_maximum_fusion.refs_1_), channel_id=1, source_target_pairs={{0,4},{1,5},{2,6},{3,7},{4,0},{5,1},{6,2},{7,3},{8,12},{9,13},{10,... | collective-permute-start | bytes 786440 | tf_op jit(solution)/shard_map/ppermute | solution.py:43
  14.4 7.3 %collective-permute-start.8 = (bf16[256,512]{1,0:T(8,128)(2,1)S(1)}, bf16[256,512]{1,0:T(8,128)(2,1)S(1)}, u32[]{:S(2)}, u32[]{:S(2)}) collective-permute-start(bf16[256,512]{1,0:T(8,128)(2,1)S(1)} %pad_maximum_fusion.refs_1_), channel_id=1, source_target_pairs={{0,1},{1,0},{2,3},{3,2},{4,5},{5,4},{6,7},{7,6},{8,9},{9,8},{10,11... | collective-permute-start | bytes 786440 | tf_op jit(solution)/shard_map/ppermute | solution.py:43
  14.8 8.0 %collective-permute-start.4 = (bf16[64,512]{1,0:T(8,128)(2,1)S(1)}, bf16[64,512]{1,0:T(8,128)(2,1)S(1)}, u32[]{:S(2)}, u32[]{:S(2)}) collective-permute-start(bf16[64,512]{1,0:T(8,128)(2,1)S(1)} %collective-permute-done), channel_id=1, source_target_pairs={{0,24},{1,25},{2,26},{3,27},{4,28},{5,29},{6,30},{7,31},{8,16},{9,... | collective-permute-start | bytes 196616 | tf_op jit(solution)/shard_map/ppermute | solution.py:43
  17.5 5.4 %collective-permute-start.5 = (bf16[64,512]{1,0:T(8,128)(2,1)S(1)}, bf16[64,512]{1,0:T(8,128)(2,1)S(1)}, u32[]{:S(2)}, u32[]{:S(2)}) collective-permute-start(bf16[64,512]{1,0:T(8,128)(2,1)S(1)} %collective-permute-done), channel_id=1, source_target_pairs={{0,16},{1,17},{2,18},{3,19},{4,20},{5,21},{6,22},{7,23},{8,24},{9,... | collective-permute-start | bytes 196616 | tf_op jit(solution)/shard_map/ppermute | solution.py:43
  17.5 5.4 %collective-permute-start.6 = (bf16[64,512]{1,0:T(8,128)(2,1)S(1)}, bf16[64,512]{1,0:T(8,128)(2,1)S(1)}, u32[]{:S(2)}, u32[]{:S(2)}) collective-permute-start(bf16[64,512]{1,0:T(8,128)(2,1)S(1)} %collective-permute-done), channel_id=1, source_target_pairs={{0,8},{1,9},{2,10},{3,11},{4,12},{5,13},{6,14},{7,15},{8,0},{9,1},... | collective-permute-start | bytes 196616 | tf_op jit(solution)/shard_map/ppermute | solution.py:43
  21.7 1.8 %collective-permute-start.10 = (bf16[256,512]{1,0:T(8,128)(2,1)S(1)}, bf16[256,512]{1,0:T(8,128)(2,1)S(1)}, u32[]{:S(2)}, u32[]{:S(2)}) collective-permute-start(bf16[256,512]{1,0:T(8,128)(2,1)S(1)} %collective-permute-done.8.refs_5_), channel_id=1, source_target_pairs={{0,2},{1,3},{2,0},{3,1},{4,6},{5,7},{6,4},{7,5},{8,10},{9,11},{10,... | collective-permute-start | bytes 786440 | tf_op jit(solution)/shard_map/ppermute | solution.py:43
  21.7 1.9 %collective-permute-start.9 = (bf16[256,512]{1,0:T(8,128)(2,1)S(1)}, bf16[256,512]{1,0:T(8,128)(2,1)S(1)}, u32[]{:S(2)}, u32[]{:S(2)}) collective-permute-start(bf16[256,512]{1,0:T(8,128)(2,1)S(1)} %collective-permute-done.7.refs_4_), channel_id=1, source_target_pairs={{0,2},{1,3},{2,0},{3,1},{4,6},{5,7},{6,4},{7,5},{8,10},{9,11},{10,... | collective-permute-start | bytes 786440 | tf_op jit(solution)/shard_map/ppermute | solution.py:43
  22.9 1.6 %collective-permute-start.11 = (bf16[256,512]{1,0:T(8,128)(2,1)S(1)}, bf16[256,512]{1,0:T(8,128)(2,1)S(1)}, u32[]{:S(2)}, u32[]{:S(2)}) collective-permute-start(bf16[256,512]{1,0:T(8,128)(2,1)S(1)} %constant_dynamic-update-slice_fusion.2.refs_6_), channel_id=1, source_target_pairs={{0,2},{1,3},{2,0},{3,1},{4,6},{5,7},{6,4},{7,5},{8,10},{9,11},{10,... | collective-permute-start | bytes 786440 | tf_op jit(solution)/shard_map/ppermute | solution.py:43
  23.0 1.9 %collective-permute-start.12 = (bf16[256,512]{1,0:T(8,128)(2,1)S(1)}, bf16[256,512]{1,0:T(8,128)(2,1)S(1)}, u32[]{:S(2)}, u32[]{:S(2)}) collective-permute-start(bf16[256,512]{1,0:T(8,128)(2,1)S(1)} %pad_maximum_fusion.refs_1_), channel_id=1, source_target_pairs={{0,2},{1,3},{2,0},{3,1},{4,6},{5,7},{6,4},{7,5},{8,10},{9,11},{10,... | collective-permute-start | bytes 786440 | tf_op jit(solution)/shard_map/ppermute | solution.py:43

commit v7 on v6

--- a/solution.py
+++ b/solution.py
@@ -48,19 +48,23 @@
 
 def fold_kernel(layout, sources, rows, groups, carried, last, *refs):
     plane = layout.split(layout.here())[0]
-    level = [[steps for steps in piece if steps[0] == HERE] for piece in sources]
-    assert all(piece[: len(flat)] == flat for piece, flat in zip(sources, level, strict=True))
-    if level == sources:
-        fold_blocks(layout, sources, rows, groups, carried, last, *refs)
+    assert all(piece == sorted(piece, key=lambda steps: max(steps[0])) for piece in sources)
+
+    def upto(most):
+        return [[steps for steps in piece if max(steps[0]) <= most] for piece in sources]
+
+    def run(taken):
+        fold_blocks(layout, taken, rows, groups, carried, last, *refs)
+
+    if upto(0) == sources:
+        run(sources)
         return
-
-    @pl.when(plane == 0)
-    def _():
-        fold_blocks(layout, level, rows, groups, carried, last, *refs)
-
-    @pl.when(plane > 0)
-    def _():
-        fold_blocks(layout, sources, rows, groups, carried, last, *refs)
+    pl.when(plane == 0)(lambda: run(upto(0)))
+    if layout.planes > 2:
+        pl.when(plane == 1)(lambda: run(upto(1)))
+        pl.when(plane > 1)(lambda: run(sources))
+    else:
+        pl.when(plane == 1)(lambda: run(sources))
 
 
 def fold_blocks(layout, sources, rows, groups, carried, last, *refs):
@@ -179,16 +183,10 @@
         groups = keys.shape[1] // HD
         go = layout.exchange
         block = jnp.concatenate([keys, values], axis=1)
-        ups = list(range(layout.planes - 1, 0, -1))
-        lines = range(1, layout.lines)
-        columns = range(1, layout.across)
-        side_steps = [(HERE, l, 0, 0) for l in lines] + [(HERE, 0, 0, c) for c in columns]
-        corner_steps = [(HERE, l, 0, c) for l in lines for c in columns]
-        above_steps = [((up, up), 0, 0, 0) for up in ups]
-        if layout.planes == 4:
-            above_steps = [(pair, 0, 0, 0) for pair in [(3, 3), (2, 2), (1, 1)]]
-        far_above = [(pair, 0, 0, 0) for pair in [(3, 3), (2, 2), (1, 1)]] if layout.planes == 4 else above_steps
-        tower_steps = [SELF] + above_steps
+        above = [((up, up), 0, 0, 0) for up in range(layout.planes - 1, 0, -1)]
+        columns = [(HERE, 0, 0, c) for c in range(1, layout.across)]
+        lines = [(HERE, l, 0, 0) for l in range(1, layout.lines)]
+        corners = [(HERE, l, 0, c) for _, l, _, _ in lines for _, _, _, c in columns]
 
         def moved(steps, by):
             def add(one):
@@ -197,36 +195,40 @@
 
             return [add(one) for one in steps]
 
+        def sent(piece, by):
+            return go(piece[0], by), moved(piece[1], by)
+
         def swapped(pieces):
-            turned = [(go(array, (HERE, 0, 1, 0)), steps) for array, steps in pieces]
-            return [(array, [(up[::-1], l, 1 - swap, c) for up, l, swap, c in steps]) for array, steps in turned]
+            turned = [sent(piece, (HERE, 0, 1, 0)) for piece in pieces]
+            return [(array, [(up[::-1], l, swap, c) for up, l, swap, c in steps]) for array, steps in turned]
 
         def join(pieces):
             if len(pieces) == 1:
                 return pieces[0]
             return jnp.concatenate([x for x, _ in pieces], axis=0), [one for _, steps in pieces for one in steps]
 
-        def after(pieces, state):
+        def tied(pieces, state=None):
             arrays, state = lax.optimization_barrier(([array for array, _ in pieces], state))
             return [(array, steps) for array, (_, steps) in zip(arrays, pieces, strict=True)], state
 
-        corner = join([(go(block, steps), [steps]) for steps in corner_steps])
-        corner_array, above = lax.optimization_barrier((corner[0], [go(block, steps) for steps in above_steps]))
-        corner = (corner_array, corner[1])
-        near = [(jnp.concatenate([block] + above, axis=0), tower_steps)]
-        sides = [(go(near[0][0], steps), moved(tower_steps, steps)) for steps in side_steps]
-        far = [corner] + [(go(corner[0], steps), moved(corner[1], steps)) for steps in far_above]
-
-        state = fold(layout, queries, None, near, groups)
-        sides, state = after(sides, state)
-        side_others = swapped(sides)
+        own = (block, [SELF])
+        corner = join([sent(own, steps) for steps in corners])
+        column = [sent(own, steps) for steps in above]
+        (longest, corner, *column), _ = tied([column[0], corner, *column[1:]])
+        near = join([own, *column[::-1], longest])
+        (near, corner), _ = tied([near, corner])
+        far = [sent(corner, steps) for steps in above]
+        sides = [sent(near, steps) for steps in columns + lines]
+
+        state = fold(layout, queries, None, [near, corner], groups)
+        sides, state = tied(sides, state)
+        others = swapped(sides) + swapped([join([corner, near])])
         state = fold(layout, queries, state, sides, groups)
-        rest, state = after(far + near, state)
-        far, near = rest[:-1], rest[-1:]
-        far = [join(far)]
-        others = swapped(far) + swapped(near)
-        state = fold(layout, queries, state, side_others + far, groups)
-        return fold(layout, queries, state, others, groups, last=True)
+        far, state = tied(far, state)
+        far = [join(far[::-1])]
+        far_others = swapped(far)
+        state = fold(layout, queries, state, others, groups)
+        return fold(layout, queries, state, far + far_others, groups, last=True)
 
     placed = P(AXES, None)
     return jax.shard_map(

time: 26.3 us -> 25.4 us (0.966)
  Pallas kernels: 3.3 us -> 2.71 us
  starting transfers between devices: 14.8 us -> 14.5 us
    pallas_call x4, Pallas kernels: 3.3 us -> 2.71 us  [fold(): pl.pallas_call(functools.partial(fold_kernel, layout, [blocks for _, bloc...]
    ppermute x13, starting transfers between devices: 14.8 us -> 14.5 us  [exchange(): lax.ppermute(array, AXES, [(rank, self.partner(rank, steps)) for rank in...]
    unnamed x8 -> x7, local copies, waits for them, and re-layouts: 0.8 us -> 0.79 us
  transfers between devices with their start and end apart: 13 -> 13, of which waited for: 7 -> 6; matrix products, arithmetic and copies ran while one was open for 0% -> 0% of each run, Pallas kernels for 8% -> 8%
where the time goes in v7:
time: 25.4 us; the launch traced here: 25.2 us
  starting transfers between devices  14.5 us (57%)
  waiting for transfers between devices  7.02 us (28%)
  Pallas kernels  2.71 us (11%)
  local copies, waits for them, and re-layouts  0.8 us (3%)
    ppermute x13, starting transfers between devices, exchange(): lax.ppermute(array, AXES, [(rank, self.partner(rank, steps)) for rank in...  14.5 us
    ppermute x13, waiting for transfers between devices, exchange(): lax.ppermute(array, AXES, [(rank, self.partner(rank, steps)) for rank in...  7.02 us
    pallas_call x4, Pallas kernels, fold(): pl.pallas_call(functools.partial(fold_kernel, layout, [blocks for _, bloc...  2.71 us
    unnamed x7, local copies, waits for them, and re-layouts  0.79 us
  transfers between devices with their start and end apart: 13, of which 6 were waited for; matrix products, arithmetic and copies ran while one was open for 0% of the time, Pallas kernels for 8%

profile of v7, /device:TPU:0, one launch (start us, length us, event | category | flops | bytes accessed | tf_op | source)
XLA Modules:
  0.0 25.2 jit_solution(3138401113093684796)
XLA Ops:
  0.0 0.0 copy-start.1
  0.0 0.8 %constant_dynamic-update-slice_fusion.1 = bf16[64,512]{1,0:T(8,128)(2,1)S(1)} fusion(bf16[64,256]{1,0:T(8,128)(2,1)} %param.4), kind=kLoop, calls=%fused_computation.3 | loop fusion | bytes 65536
  0.8 0.0 copy-done.1
  0.8 0.0 copy-start
  0.8 5.1 %collective-permute-start = (bf16[64,512]{1,0:T(8,128)(2,1)S(1)}, bf16[64,512]{1,0:T(8,128)(2,1)S(1)}, u32[]{:S(2)}, u32[]{:S(2)}) collective-permute-start(bf16[64,512]{1,0:T(8,128)(2,1)S(1)} %constant_dynamic-update-slice_fusion), channel_id=1, source_target_pairs={{0,24},{1,25},{2,26},{3,27},{4,28},{5,29},{6,30},{7,31},{8,16},{9,... | collective-permute-start | bytes 196616 | tf_op jit(solution)/shard_map/ppermute | solution.py:43
  5.9 2.4 %collective-permute-start.1 = (bf16[64,512]{1,0:T(8,128)(2,1)S(1)}, bf16[64,512]{1,0:T(8,128)(2,1)S(1)}, u32[]{:S(2)}, u32[]{:S(2)}) collective-permute-start(bf16[64,512]{1,0:T(8,128)(2,1)S(1)} %constant_dynamic-update-slice_fusion), channel_id=1, source_target_pairs={{0,5},{1,4},{2,7},{3,6},{4,1},{5,0},{6,3},{7,2},{8,13},{9,12},{10,... | collective-permute-start | bytes 196616 | tf_op jit(solution)/shard_map/ppermute | solution.py:43
  8.4 0.0 collective-permute-start.2
  8.4 0.8 %collective-permute-start.3 = (bf16[64,512]{1,0:T(8,128)(2,1)S(1)}, bf16[64,512]{1,0:T(8,128)(2,1)S(1)}, u32[]{:S(2)}, u32[]{:S(2)}) collective-permute-start(bf16[64,512]{1,0:T(8,128)(2,1)S(1)} %constant_dynamic-update-slice_fusion), channel_id=1, source_target_pairs={{0,8},{1,9},{2,10},{3,11},{4,12},{5,13},{6,14},{7,15},{8,0},{9,1},... | collective-permute-start | bytes 196616 | tf_op jit(solution)/shard_map/ppermute | solution.py:43
  9.1 0.0 collective-permute-done
  9.1 1.9 %collective-permute-done.1.refs_2_ = bf16[64,512]{1,0:T(8,128)(2,1)S(1)} collective-permute-done((bf16[64,512]{1,0:T(8,128)(2,1)S(1)}, bf16[64,512]{1,0:T(8,128)(2,1)S(1)}, u32[]{:S(2)}, u32[]{:S(2)}) %collective-permute-start.1) | collective-permute-done | bytes 65568 | tf_op jit(solution)/shard_map/ppermute | solution.py:43
  11.1 2.4 %collective-permute-done.2 = bf16[64,512]{1,0:T(8,128)(2,1)S(1)} collective-permute-done((bf16[64,512]{1,0:T(8,128)(2,1)S(1)}, bf16[64,512]{1,0:T(8,128)(2,1)S(1)}, u32[]{:S(2)}, u32[]{:S(2)}) %collective-permute-start.2) | collective-permute-done | bytes 65568 | tf_op jit(solution)/shard_map/ppermute | solution.py:43
  13.5 0.0 collective-permute-done.3
  13.5 0.6 %collective-permute-start.7 = (bf16[256,512]{1,0:T(8,128)(2,1)S(1)}, bf16[256,512]{1,0:T(8,128)(2,1)S(1)}, u32[]{:S(2)}, u32[]{:S(2)}) collective-permute-start(bf16[256,512]{1,0:T(8,128)(2,1)S(1)} %pad_maximum_fusion.1.refs_1_), channel_id=1, source_target_pairs={{0,1},{1,0},{2,3},{3,2},{4,5},{5,4},{6,7},{7,6},{8,9},{9,8},{10,11... | collective-permute-start | bytes 786440 | tf_op jit(solution)/shard_map/ppermute | solution.py:43
  14.1 0.5 %collective-permute-start.8 = (bf16[256,512]{1,0:T(8,128)(2,1)S(1)}, bf16[256,512]{1,0:T(8,128)(2,1)S(1)}, u32[]{:S(2)}, u32[]{:S(2)}) collective-permute-start(bf16[256,512]{1,0:T(8,128)(2,1)S(1)} %pad_maximum_fusion.1.refs_1_), channel_id=1, source_target_pairs={{0,4},{1,5},{2,6},{3,7},{4,0},{5,1},{6,2},{7,3},{8,12},{9,13},{10,... | collective-permute-start | bytes 786440 | tf_op jit(solution)/shard_map/ppermute | solution.py:43
  14.7 2.7 %collective-permute-start.4 = (bf16[64,512]{1,0:T(8,128)(2,1)S(1)}, bf16[64,512]{1,0:T(8,128)(2,1)S(1)}, u32[]{:S(2)}, u32[]{:S(2)}) collective-permute-start(bf16[64,512]{1,0:T(8,128)(2,1)S(1)} %collective-permute-done.1.refs_2_), channel_id=1, source_target_pairs={{0,24},{1,25},{2,26},{3,27},{4,28},{5,29},{6,30},{7,31},{8,16},{9,... | collective-permute-start | bytes 196616 | tf_op jit(solution)/shard_map/ppermute | solution.py:43
  17.4 0.0 collective-permute-start.5
  17.4 1.7 %collective-permute-start.6 = (bf16[64,512]{1,0:T(8,128)(2,1)S(1)}, bf16[64,512]{1,0:T(8,128)(2,1)S(1)}, u32[]{:S(2)}, u32[]{:S(2)}) collective-permute-start(bf16[64,512]{1,0:T(8,128)(2,1)S(1)} %collective-permute-done.1.refs_2_), channel_id=1, source_target_pairs={{0,8},{1,9},{2,10},{3,11},{4,12},{5,13},{6,14},{7,15},{8,0},{9,1},... | collective-permute-start | bytes 196616 | tf_op jit(solution)/shard_map/ppermute | solution.py:43
  19.0 0.0 copy-done
  19.0 0.6 %shard_map.37 = (f32[2,512,128]{2,1,0:T(8,128)S(1)}, f32[2,512,128]{2,1,0:T(8,128)S(1)}, f32[2,512,128]{2,1,0:T(8,128)S(1)}) custom-call(bf16[64,2048]{1,0:T(8,128)(2,1)S(1)} %copy-done, bf16[256,512]{1,0:T(8,128)(2,1)S(1)} %pad_maximum_fusion.1.refs_1_, bf16[64,512]{1,0:T(8,128)(2,1)S(1)} %collective-permute-done.1.refs_2_), custom_call_target="tpu_custom_call" | custom-call | tf_op jit(solution)/shard_map/pallas_call | solution.py:166
  19.6 0.3 %collective-permute-done.7.refs_4_ = bf16[256,512]{1,0:T(8,128)(2,1)S(1)} collective-permute-done((bf16[256,512]{1,0:T(8,128)(2,1)S(1)}, bf16[256,512]{1,0:T(8,128)(2,1)S(1)}, u32[]{:S(2)}, u32[]{:S(2)}) %collective-permute-start.7) | collective-permute-done | bytes 262176 | tf_op jit(solution)/shard_map/ppermute | solution.py:43
  20.0 0.0 collective-permute-start.11
  20.0 0.5 %collective-permute-done.8.refs_5_ = bf16[256,512]{1,0:T(8,128)(2,1)S(1)} collective-permute-done((bf16[256,512]{1,0:T(8,128)(2,1)S(1)}, bf16[256,512]{1,0:T(8,128)(2,1)S(1)}, u32[]{:S(2)}, u32[]{:S(2)}) %collective-permute-start.8) | collective-permute-done | bytes 262176 | tf_op jit(solution)/shard_map/ppermute | solution.py:43
  20.5 0.0 collective-permute-start.9
  20.5 0.6 %shard_map.38 = (f32[2,512,128]{2,1,0:T(8,128)S(1)}, f32[2,512,128]{2,1,0:T(8,128)S(1)}, f32[2,512,128]{2,1,0:T(8,128)S(1)}) custom-call(bf16[64,2048]{1,0:T(8,128)(2,1)S(1)} %copy-done, f32[2,512,128]{2,1,0:T(8,128)S(1)} %get-tuple-element.40.refs_1_, f32[2,512,128]{2,1,0:T(8,128)S(1)} %get-tuple-element.41.refs_2_, ...), custom_call_target="tpu_custom_call" | custom-call | tf_op jit(solution)/shard_map/pallas_call | solution.py:166
  21.1 0.0 collective-permute-done.4
  21.1 0.6 %collective-permute-start.10 = (bf16[256,512]{1,0:T(8,128)(2,1)S(1)}, bf16[256,512]{1,0:T(8,128)(2,1)S(1)}, u32[]{:S(2)}, u32[]{:S(2)}) collective-permute-start(bf16[256,512]{1,0:T(8,128)(2,1)S(1)} %collective-permute-done.8.refs_5_), channel_id=1, source_target_pairs={{0,2},{1,3},{2,0},{3,1},{4,6},{5,7},{6,4},{7,5},{8,10},{9,11},{10,... | collective-permute-start | bytes 786440 | tf_op jit(solution)/shard_map/ppermute | solution.py:43
  21.7 1.1 %collective-permute-done.5 = bf16[64,512]{1,0:T(8,128)(2,1)S(1)} collective-permute-done((bf16[64,512]{1,0:T(8,128)(2,1)S(1)}, bf16[64,512]{1,0:T(8,128)(2,1)S(1)}, u32[]{:S(2)}, u32[]{:S(2)}) %collective-permute-start.5) | collective-permute-done | bytes 65568 | tf_op jit(solution)/shard_map/ppermute | solution.py:43
  22.8 0.0 collective-permute-done.6
  22.9 0.1 collective-permute-start.12
  23.0 0.0 collective-permute-done.11.refs_6_
  23.0 0.0 collective-permute-done.9.refs_4_
  23.0 0.0 collective-permute-done.10.refs_5_
  23.0 0.8 %shard_map.39 = (f32[2,512,128]{2,1,0:T(8,128)S(1)}, f32[2,512,128]{2,1,0:T(8,128)S(1)}, f32[2,512,128]{2,1,0:T(8,128)S(1)}) custom-call(bf16[64,2048]{1,0:T(8,128)(2,1)S(1)} %copy-done, f32[2,512,128]{2,1,0:T(8,128)S(1)} %get-tuple-element.48.refs_1_, f32[2,512,128]{2,1,0:T(8,128)S(1)} %get-tuple-element.49.refs_2_, ...), custom_call_target="tpu_custom_call" | custom-call | tf_op jit(solution)/shard_map/pallas_call | solution.py:166
  23.8 0.6 %collective-permute-done.12.refs_5_ = bf16[192,512]{1,0:T(8,128)(2,1)S(1)} collective-permute-done((bf16[192,512]{1,0:T(8,128)(2,1)S(1)}, bf16[192,512]{1,0:T(8,128)(2,1)S(1)}, u32[]{:S(2)}, u32[]{:S(2)}) %collective-permute-start.12) | collective-permute-done | bytes 196640 | tf_op jit(solution)/shard_map/ppermute | solution.py:43
  24.4 0.8 %shard_map.40 = bf16[64,2048]{1,0:T(8,128)(2,1)} custom-call(bf16[64,2048]{1,0:T(8,128)(2,1)S(1)} %copy-done, f32[2,512,128]{2,1,0:T(8,128)S(1)} %get-tuple-element.51.refs_1_, f32[2,512,128]{2,1,0:T(8,128)S(1)} %get-tuple-element.52.refs_2_, f32[2,512,128]{2,1,0:T(8,128)S(1)} %get-tuple-element.53.refs_3_, ...), custom_call_target="tpu_custom_call" | custom-call | tf_op jit(solution)/shard_map/pallas_call | solution.py:166
  (6 shorter events, 0.1 us)
Async XLA Ops:
  0.0 0.8 %copy-start.1 = (bf16[64,256]{1,0:T(8,128)(2,1)S(1)}, bf16[64,256]{1,0:T(8,128)(2,1)}, u32[]{:S(2)}) copy-start(bf16[64,256]{1,0:T(8,128)(2,1)} %param.5) | copy-start | bytes 98308
  0.8 18.3 %copy-start = (bf16[64,2048]{1,0:T(8,128)(2,1)S(1)}, bf16[64,2048]{1,0:T(8,128)(2,1)}, u32[]{:S(2)}) copy-start(bf16[64,2048]{1,0:T(8,128)(2,1)} %refs_0_.7) | copy-start | bytes 786436
  0.8 8.4 %collective-permute-start = (bf16[64,512]{1,0:T(8,128)(2,1)S(1)}, bf16[64,512]{1,0:T(8,128)(2,1)S(1)}, u32[]{:S(2)}, u32[]{:S(2)}) collective-permute-start(bf16[64,512]{1,0:T(8,128)(2,1)S(1)} %constant_dynamic-update-slice_fusion), channel_id=1, source_target_pairs={{0,24},{1,25},{2,26},{3,27},{4,28},{5,29},{6,30},{7,31},{8,16},{9,... | collective-permute-start | bytes 196616 | tf_op jit(solution)/shard_map/ppermute | solution.py:43
  5.9 5.2 %collective-permute-start.1 = (bf16[64,512]{1,0:T(8,128)(2,1)S(1)}, bf16[64,512]{1,0:T(8,128)(2,1)S(1)}, u32[]{:S(2)}, u32[]{:S(2)}) collective-permute-start(bf16[64,512]{1,0:T(8,128)(2,1)S(1)} %constant_dynamic-update-slice_fusion), channel_id=1, source_target_pairs={{0,5},{1,4},{2,7},{3,6},{4,1},{5,0},{6,3},{7,2},{8,13},{9,12},{10,... | collective-permute-start | bytes 196616 | tf_op jit(solution)/shard_map/ppermute | solution.py:43
  8.4 5.2 %collective-permute-start.2 = (bf16[64,512]{1,0:T(8,128)(2,1)S(1)}, bf16[64,512]{1,0:T(8,128)(2,1)S(1)}, u32[]{:S(2)}, u32[]{:S(2)}) collective-permute-start(bf16[64,512]{1,0:T(8,128)(2,1)S(1)} %constant_dynamic-update-slice_fusion), channel_id=1, source_target_pairs={{0,16},{1,17},{2,18},{3,19},{4,20},{5,21},{6,22},{7,23},{8,24},{9,... | collective-permute-start | bytes 196616 | tf_op jit(solution)/shard_map/ppermute | solution.py:43
  8.4 5.2 %collective-permute-start.3 = (bf16[64,512]{1,0:T(8,128)(2,1)S(1)}, bf16[64,512]{1,0:T(8,128)(2,1)S(1)}, u32[]{:S(2)}, u32[]{:S(2)}) collective-permute-start(bf16[64,512]{1,0:T(8,128)(2,1)S(1)} %constant_dynamic-update-slice_fusion), channel_id=1, source_target_pairs={{0,8},{1,9},{2,10},{3,11},{4,12},{5,13},{6,14},{7,15},{8,0},{9,1},... | collective-permute-start | bytes 196616 | tf_op jit(solution)/shard_map/ppermute | solution.py:43
  13.5 6.4 %collective-permute-start.7 = (bf16[256,512]{1,0:T(8,128)(2,1)S(1)}, bf16[256,512]{1,0:T(8,128)(2,1)S(1)}, u32[]{:S(2)}, u32[]{:S(2)}) collective-permute-start(bf16[256,512]{1,0:T(8,128)(2,1)S(1)} %pad_maximum_fusion.1.refs_1_), channel_id=1, source_target_pairs={{0,1},{1,0},{2,3},{3,2},{4,5},{5,4},{6,7},{7,6},{8,9},{9,8},{10,11... | collective-permute-start | bytes 786440 | tf_op jit(solution)/shard_map/ppermute | solution.py:43
  14.1 6.4 %collective-permute-start.8 = (bf16[256,512]{1,0:T(8,128)(2,1)S(1)}, bf16[256,512]{1,0:T(8,128)(2,1)S(1)}, u32[]{:S(2)}, u32[]{:S(2)}) collective-permute-start(bf16[256,512]{1,0:T(8,128)(2,1)S(1)} %pad_maximum_fusion.1.refs_1_), channel_id=1, source_target_pairs={{0,4},{1,5},{2,6},{3,7},{4,0},{5,1},{6,2},{7,3},{8,12},{9,13},{10,... | collective-permute-start | bytes 786440 | tf_op jit(solution)/shard_map/ppermute | solution.py:43
  14.7 6.5 %collective-permute-start.4 = (bf16[64,512]{1,0:T(8,128)(2,1)S(1)}, bf16[64,512]{1,0:T(8,128)(2,1)S(1)}, u32[]{:S(2)}, u32[]{:S(2)}) collective-permute-start(bf16[64,512]{1,0:T(8,128)(2,1)S(1)} %collective-permute-done.1.refs_2_), channel_id=1, source_target_pairs={{0,24},{1,25},{2,26},{3,27},{4,28},{5,29},{6,30},{7,31},{8,16},{9,... | collective-permute-start | bytes 196616 | tf_op jit(solution)/shard_map/ppermute | solution.py:43
  17.4 5.5 %collective-permute-start.5 = (bf16[64,512]{1,0:T(8,128)(2,1)S(1)}, bf16[64,512]{1,0:T(8,128)(2,1)S(1)}, u32[]{:S(2)}, u32[]{:S(2)}) collective-permute-start(bf16[64,512]{1,0:T(8,128)(2,1)S(1)} %collective-permute-done.1.refs_2_), channel_id=1, source_target_pairs={{0,16},{1,17},{2,18},{3,19},{4,20},{5,21},{6,22},{7,23},{8,24},{9,... | collective-permute-start | bytes 196616 | tf_op jit(solution)/shard_map/ppermute | solution.py:43
  17.4 5.5 %collective-permute-start.6 = (bf16[64,512]{1,0:T(8,128)(2,1)S(1)}, bf16[64,512]{1,0:T(8,128)(2,1)S(1)}, u32[]{:S(2)}, u32[]{:S(2)}) collective-permute-start(bf16[64,512]{1,0:T(8,128)(2,1)S(1)} %collective-permute-done.1.refs_2_), channel_id=1, source_target_pairs={{0,8},{1,9},{2,10},{3,11},{4,12},{5,13},{6,14},{7,15},{8,0},{9,1},... | collective-permute-start | bytes 196616 | tf_op jit(solution)/shard_map/ppermute | solution.py:43
  20.0 3.0 %collective-permute-start.11 = (bf16[320,512]{1,0:T(8,128)(2,1)S(1)}, bf16[320,512]{1,0:T(8,128)(2,1)S(1)}, u32[]{:S(2)}, u32[]{:S(2)}) collective-permute-start(bf16[320,512]{1,0:T(8,128)(2,1)S(1)} %pad_maximum_fusion), channel_id=1, source_target_pairs={{0,2},{1,3},{2,0},{3,1},{4,6},{5,7},{6,4},{7,5},{8,10},{9,11},{10,... | collective-permute-start | bytes 983048 | tf_op jit(solution)/shard_map/ppermute | solution.py:43
  20.5 2.5 %collective-permute-start.9 = (bf16[256,512]{1,0:T(8,128)(2,1)S(1)}, bf16[256,512]{1,0:T(8,128)(2,1)S(1)}, u32[]{:S(2)}, u32[]{:S(2)}) collective-permute-start(bf16[256,512]{1,0:T(8,128)(2,1)S(1)} %collective-permute-done.7.refs_4_), channel_id=1, source_target_pairs={{0,2},{1,3},{2,0},{3,1},{4,6},{5,7},{6,4},{7,5},{8,10},{9,11},{10,... | collective-permute-start | bytes 786440 | tf_op jit(solution)/shard_map/ppermute | solution.py:43
  21.1 1.9 %collective-permute-start.10 = (bf16[256,512]{1,0:T(8,128)(2,1)S(1)}, bf16[256,512]{1,0:T(8,128)(2,1)S(1)}, u32[]{:S(2)}, u32[]{:S(2)}) collective-permute-start(bf16[256,512]{1,0:T(8,128)(2,1)S(1)} %collective-permute-done.8.refs_5_), channel_id=1, source_target_pairs={{0,2},{1,3},{2,0},{3,1},{4,6},{5,7},{6,4},{7,5},{8,10},{9,11},{10,... | collective-permute-start | bytes 786440 | tf_op jit(solution)/shard_map/ppermute | solution.py:43
  22.9 1.5 %collective-permute-start.12 = (bf16[192,512]{1,0:T(8,128)(2,1)S(1)}, bf16[192,512]{1,0:T(8,128)(2,1)S(1)}, u32[]{:S(2)}, u32[]{:S(2)}) collective-permute-start(bf16[192,512]{1,0:T(8,128)(2,1)S(1)} %constant_dynamic-update-slice_fusion.2.refs_4_), channel_id=1, source_target_pairs={{0,2},{1,3},{2,0},{3,1},{4,6},{5,7},{6,4},{7,5},{8,10},{9,11},{10,... | collective-permute-start | bytes 589832 | tf_op jit(solution)/shard_map/ppermute | solution.py:43

commit v8 on v7

--- a/solution.py
+++ b/solution.py
@@ -48,33 +48,36 @@
 
 def fold_kernel(layout, sources, rows, groups, carried, last, *refs):
     plane = layout.split(layout.here())[0]
-    assert all(piece == sorted(piece, key=lambda steps: max(steps[0])) for piece in sources)
-
-    def upto(most):
-        return [[steps for steps in piece if max(steps[0]) <= most] for piece in sources]
-
-    def run(taken):
-        fold_blocks(layout, taken, rows, groups, carried, last, *refs)
-
-    if upto(0) == sources:
-        run(sources)
+
+    def run(ups):
+        fold_blocks(layout, sources, rows, groups, carried, last, ups, *refs)
+
+    every = {up for piece in sources for steps in piece for up in steps[0]}
+    if every == {0}:
+        run(every)
         return
-    pl.when(plane == 0)(lambda: run(upto(0)))
-    if layout.planes > 2:
-        pl.when(plane == 1)(lambda: run(upto(1)))
-        pl.when(plane > 1)(lambda: run(sources))
-    else:
-        pl.when(plane == 1)(lambda: run(sources))
-
-
-def fold_blocks(layout, sources, rows, groups, carried, last, *refs):
+    few = min(3, layout.planes - 1)
+    for at in range(few):
+        pl.when(plane == at)(functools.partial(run, {up for up in every if at ^ up <= at}))
+    pl.when(plane >= few)(lambda: run(every))
+
+
+def fold_blocks(layout, sources, rows, groups, carried, last, ups, *refs):
     refs = list(refs)
     query_ref = refs.pop(0)
     state_refs = [refs.pop(0) for _ in range(3)] if carried else None
     piece_refs, refs = refs[: len(sources)], refs[len(sources) :]
     out_refs, (score_ref, weight_ref) = refs[:-2], refs[-2:]
-    blocks = [steps for piece in sources for steps in piece]
-    taken = [(ref, len(piece) * rows) for ref, piece in zip(piece_refs, sources, strict=True) if piece]
+    blocks, runs = [], []
+    for ref, piece in zip(piece_refs, sources, strict=True):
+        for at, steps in enumerate(piece):
+            if not ups.issuperset(steps[0]):
+                continue
+            blocks.append(steps)
+            if runs and runs[-1][0] is ref and runs[-1][2] == at * rows:
+                runs[-1][2] += rows
+            else:
+                runs.append([ref, at * rows, (at + 1) * rows])
     width = len(blocks) * rows
     heads = query_ref.shape[1] // (groups * HD)
     tall = heads * rows
@@ -112,7 +115,7 @@
         first = group * heads * HD
         query = jnp.concatenate([query_ref[:, first + h * HD : first + (h + 1) * HD] for h in range(heads)], axis=0)
         at = group * HD
-        key = jnp.concatenate([ref[:size, at : at + HD] for ref, size in taken], axis=0)
+        key = jnp.concatenate([ref[begin:end, at : at + HD] for ref, begin, end in runs], axis=0)
         score_ref[group % 2, :, :width] = lax.dot_general(
             query, key, (((1,), (1,)), ((), ())), preferred_element_type=jnp.float32
         )
@@ -139,7 +142,7 @@
             sums.append(jnp.broadcast_to(jnp.sum(total, axis=1, keepdims=True) + rest, (rows, HD)))
         largest, totals = jnp.concatenate(tops, axis=0), jnp.concatenate(sums, axis=0)
         at = (groups + group) * HD
-        value = jnp.concatenate([ref[:size, at : at + HD] for ref, size in taken], axis=0)
+        value = jnp.concatenate([ref[begin:end, at : at + HD] for ref, begin, end in runs], axis=0)
         summed = jnp.dot(weight_ref[slot, :, :width], value, preferred_element_type=jnp.float32)
         if carried:
             decay = jnp.exp2(state_refs[0][group] - largest)
@@ -215,7 +218,7 @@
         corner = join([sent(own, steps) for steps in corners])
         column = [sent(own, steps) for steps in above]
         (longest, corner, *column), _ = tied([column[0], corner, *column[1:]])
-        near = join([own, *column[::-1], longest])
+        near = join([own, longest, *column])
         (near, corner), _ = tied([near, corner])
         far = [sent(corner, steps) for steps in above]
         sides = [sent(near, steps) for steps in columns + lines]
@@ -225,7 +228,7 @@
         others = swapped(sides) + swapped([join([corner, near])])
         state = fold(layout, queries, state, sides, groups)
         far, state = tied(far, state)
-        far = [join(far[::-1])]
+        far = [join(far)]
         far_others = swapped(far)
         state = fold(layout, queries, state, others, groups)
         return fold(layout, queries, state, far + far_others, groups, last=True)

time: 25.4 us -> 25.4 us (level)
  no operation moved by 1% of the time
where the time goes in v8:
time: 25.4 us; the launch traced here: 25.2 us
  starting transfers between devices  14.5 us (57%)
  waiting for transfers between devices  7 us (28%)
  Pallas kernels  2.73 us (11%)
  local copies, waits for them, and re-layouts  0.8 us (3%)
    ppermute x13, starting transfers between devices, exchange(): lax.ppermute(array, AXES, [(rank, self.partner(rank, steps)) for rank in...  14.5 us
    ppermute x13, waiting for transfers between devices, exchange(): lax.ppermute(array, AXES, [(rank, self.partner(rank, steps)) for rank in...  7 us
    pallas_call x4, Pallas kernels, fold(): pl.pallas_call(functools.partial(fold_kernel, layout, [blocks for _, bloc...  2.73 us
    unnamed x7, local copies, waits for them, and re-layouts  0.79 us
  transfers between devices with their start and end apart: 13, of which 6 were waited for; matrix products, arithmetic and copies ran while one was open for 0% of the time, Pallas kernels for 8%

profile of v8, /device:TPU:0, one launch (start us, length us, event | category | flops | bytes accessed | tf_op | source)
XLA Modules:
  0.0 25.2 jit_solution(15017335148577984174)
XLA Ops:
  0.0 0.0 copy-start.1
  0.0 0.8 %constant_dynamic-update-slice_fusion.1 = bf16[64,512]{1,0:T(8,128)(2,1)S(1)} fusion(bf16[64,256]{1,0:T(8,128)(2,1)} %param.4), kind=kLoop, calls=%fused_computation.3 | loop fusion | bytes 65536
  0.8 0.0 copy-done.1
  0.8 0.0 copy-start
  0.8 5.1 %collective-permute-start = (bf16[64,512]{1,0:T(8,128)(2,1)S(1)}, bf16[64,512]{1,0:T(8,128)(2,1)S(1)}, u32[]{:S(2)}, u32[]{:S(2)}) collective-permute-start(bf16[64,512]{1,0:T(8,128)(2,1)S(1)} %constant_dynamic-update-slice_fusion), channel_id=1, source_target_pairs={{0,24},{1,25},{2,26},{3,27},{4,28},{5,29},{6,30},{7,31},{8,16},{9,... | collective-permute-start | bytes 196616 | tf_op jit(solution)/shard_map/ppermute | solution.py:43
  5.9 2.4 %collective-permute-start.1 = (bf16[64,512]{1,0:T(8,128)(2,1)S(1)}, bf16[64,512]{1,0:T(8,128)(2,1)S(1)}, u32[]{:S(2)}, u32[]{:S(2)}) collective-permute-start(bf16[64,512]{1,0:T(8,128)(2,1)S(1)} %constant_dynamic-update-slice_fusion), channel_id=1, source_target_pairs={{0,5},{1,4},{2,7},{3,6},{4,1},{5,0},{6,3},{7,2},{8,13},{9,12},{10,... | collective-permute-start | bytes 196616 | tf_op jit(solution)/shard_map/ppermute | solution.py:43
  8.4 0.0 collective-permute-start.2
  8.4 0.8 %collective-permute-start.3 = (bf16[64,512]{1,0:T(8,128)(2,1)S(1)}, bf16[64,512]{1,0:T(8,128)(2,1)S(1)}, u32[]{:S(2)}, u32[]{:S(2)}) collective-permute-start(bf16[64,512]{1,0:T(8,128)(2,1)S(1)} %constant_dynamic-update-slice_fusion), channel_id=1, source_target_pairs={{0,8},{1,9},{2,10},{3,11},{4,12},{5,13},{6,14},{7,15},{8,0},{9,1},... | collective-permute-start | bytes 196616 | tf_op jit(solution)/shard_map/ppermute | solution.py:43
  9.1 0.0 collective-permute-done
  9.1 1.9 %collective-permute-done.1.refs_2_ = bf16[64,512]{1,0:T(8,128)(2,1)S(1)} collective-permute-done((bf16[64,512]{1,0:T(8,128)(2,1)S(1)}, bf16[64,512]{1,0:T(8,128)(2,1)S(1)}, u32[]{:S(2)}, u32[]{:S(2)}) %collective-permute-start.1) | collective-permute-done | bytes 65568 | tf_op jit(solution)/shard_map/ppermute | solution.py:43
  11.1 2.4 %collective-permute-done.2 = bf16[64,512]{1,0:T(8,128)(2,1)S(1)} collective-permute-done((bf16[64,512]{1,0:T(8,128)(2,1)S(1)}, bf16[64,512]{1,0:T(8,128)(2,1)S(1)}, u32[]{:S(2)}, u32[]{:S(2)}) %collective-permute-start.2) | collective-permute-done | bytes 65568 | tf_op jit(solution)/shard_map/ppermute | solution.py:43
  13.5 0.0 collective-permute-done.3
  13.5 0.6 %collective-permute-start.7 = (bf16[256,512]{1,0:T(8,128)(2,1)S(1)}, bf16[256,512]{1,0:T(8,128)(2,1)S(1)}, u32[]{:S(2)}, u32[]{:S(2)}) collective-permute-start(bf16[256,512]{1,0:T(8,128)(2,1)S(1)} %pad_maximum_fusion.1.refs_1_), channel_id=1, source_target_pairs={{0,1},{1,0},{2,3},{3,2},{4,5},{5,4},{6,7},{7,6},{8,9},{9,8},{10,11... | collective-permute-start | bytes 786440 | tf_op jit(solution)/shard_map/ppermute | solution.py:43
  14.1 0.5 %collective-permute-start.8 = (bf16[256,512]{1,0:T(8,128)(2,1)S(1)}, bf16[256,512]{1,0:T(8,128)(2,1)S(1)}, u32[]{:S(2)}, u32[]{:S(2)}) collective-permute-start(bf16[256,512]{1,0:T(8,128)(2,1)S(1)} %pad_maximum_fusion.1.refs_1_), channel_id=1, source_target_pairs={{0,4},{1,5},{2,6},{3,7},{4,0},{5,1},{6,2},{7,3},{8,12},{9,13},{10,... | collective-permute-start | bytes 786440 | tf_op jit(solution)/shard_map/ppermute | solution.py:43
  14.7 2.7 %collective-permute-start.4 = (bf16[64,512]{1,0:T(8,128)(2,1)S(1)}, bf16[64,512]{1,0:T(8,128)(2,1)S(1)}, u32[]{:S(2)}, u32[]{:S(2)}) collective-permute-start(bf16[64,512]{1,0:T(8,128)(2,1)S(1)} %collective-permute-done.1.refs_2_), channel_id=1, source_target_pairs={{0,24},{1,25},{2,26},{3,27},{4,28},{5,29},{6,30},{7,31},{8,16},{9,... | collective-permute-start | bytes 196616 | tf_op jit(solution)/shard_map/ppermute | solution.py:43
  17.4 0.0 collective-permute-start.5
  17.4 1.7 %collective-permute-start.6 = (bf16[64,512]{1,0:T(8,128)(2,1)S(1)}, bf16[64,512]{1,0:T(8,128)(2,1)S(1)}, u32[]{:S(2)}, u32[]{:S(2)}) collective-permute-start(bf16[64,512]{1,0:T(8,128)(2,1)S(1)} %collective-permute-done.1.refs_2_), channel_id=1, source_target_pairs={{0,8},{1,9},{2,10},{3,11},{4,12},{5,13},{6,14},{7,15},{8,0},{9,1},... | collective-permute-start | bytes 196616 | tf_op jit(solution)/shard_map/ppermute | solution.py:43
  19.0 0.0 copy-done
  19.0 0.6 %shard_map.37 = (f32[2,512,128]{2,1,0:T(8,128)S(1)}, f32[2,512,128]{2,1,0:T(8,128)S(1)}, f32[2,512,128]{2,1,0:T(8,128)S(1)}) custom-call(bf16[64,2048]{1,0:T(8,128)(2,1)S(1)} %copy-done, bf16[256,512]{1,0:T(8,128)(2,1)S(1)} %pad_maximum_fusion.1.refs_1_, bf16[64,512]{1,0:T(8,128)(2,1)S(1)} %collective-permute-done.1.refs_2_), custom_call_target="tpu_custom_call" | custom-call | tf_op jit(solution)/shard_map/pallas_call | solution.py:169
  19.6 0.3 %collective-permute-done.7.refs_4_ = bf16[256,512]{1,0:T(8,128)(2,1)S(1)} collective-permute-done((bf16[256,512]{1,0:T(8,128)(2,1)S(1)}, bf16[256,512]{1,0:T(8,128)(2,1)S(1)}, u32[]{:S(2)}, u32[]{:S(2)}) %collective-permute-start.7) | collective-permute-done | bytes 262176 | tf_op jit(solution)/shard_map/ppermute | solution.py:43
  20.0 0.0 collective-permute-start.11
  20.0 0.5 %collective-permute-done.8.refs_5_ = bf16[256,512]{1,0:T(8,128)(2,1)S(1)} collective-permute-done((bf16[256,512]{1,0:T(8,128)(2,1)S(1)}, bf16[256,512]{1,0:T(8,128)(2,1)S(1)}, u32[]{:S(2)}, u32[]{:S(2)}) %collective-permute-start.8) | collective-permute-done | bytes 262176 | tf_op jit(solution)/shard_map/ppermute | solution.py:43
  20.5 0.0 collective-permute-start.9
  20.5 0.6 %shard_map.38 = (f32[2,512,128]{2,1,0:T(8,128)S(1)}, f32[2,512,128]{2,1,0:T(8,128)S(1)}, f32[2,512,128]{2,1,0:T(8,128)S(1)}) custom-call(bf16[64,2048]{1,0:T(8,128)(2,1)S(1)} %copy-done, f32[2,512,128]{2,1,0:T(8,128)S(1)} %get-tuple-element.40.refs_1_, f32[2,512,128]{2,1,0:T(8,128)S(1)} %get-tuple-element.41.refs_2_, ...), custom_call_target="tpu_custom_call" | custom-call | tf_op jit(solution)/shard_map/pallas_call | solution.py:169
  21.1 0.0 collective-permute-done.4
  21.1 0.6 %collective-permute-start.10 = (bf16[256,512]{1,0:T(8,128)(2,1)S(1)}, bf16[256,512]{1,0:T(8,128)(2,1)S(1)}, u32[]{:S(2)}, u32[]{:S(2)}) collective-permute-start(bf16[256,512]{1,0:T(8,128)(2,1)S(1)} %collective-permute-done.8.refs_5_), channel_id=1, source_target_pairs={{0,2},{1,3},{2,0},{3,1},{4,6},{5,7},{6,4},{7,5},{8,10},{9,11},{10,... | collective-permute-start | bytes 786440 | tf_op jit(solution)/shard_map/ppermute | solution.py:43
  21.7 1.1 %collective-permute-done.5 = bf16[64,512]{1,0:T(8,128)(2,1)S(1)} collective-permute-done((bf16[64,512]{1,0:T(8,128)(2,1)S(1)}, bf16[64,512]{1,0:T(8,128)(2,1)S(1)}, u32[]{:S(2)}, u32[]{:S(2)}) %collective-permute-start.5) | collective-permute-done | bytes 65568 | tf_op jit(solution)/shard_map/ppermute | solution.py:43
  22.8 0.0 collective-permute-done.6
  22.9 0.1 collective-permute-start.12
  23.0 0.0 collective-permute-done.11.refs_6_
  23.0 0.0 collective-permute-done.9.refs_4_
  23.0 0.0 collective-permute-done.10.refs_5_
  23.0 0.8 %shard_map.39 = (f32[2,512,128]{2,1,0:T(8,128)S(1)}, f32[2,512,128]{2,1,0:T(8,128)S(1)}, f32[2,512,128]{2,1,0:T(8,128)S(1)}) custom-call(bf16[64,2048]{1,0:T(8,128)(2,1)S(1)} %copy-done, f32[2,512,128]{2,1,0:T(8,128)S(1)} %get-tuple-element.48.refs_1_, f32[2,512,128]{2,1,0:T(8,128)S(1)} %get-tuple-element.49.refs_2_, ...), custom_call_target="tpu_custom_call" | custom-call | tf_op jit(solution)/shard_map/pallas_call | solution.py:169
  23.8 0.6 %collective-permute-done.12.refs_5_ = bf16[192,512]{1,0:T(8,128)(2,1)S(1)} collective-permute-done((bf16[192,512]{1,0:T(8,128)(2,1)S(1)}, bf16[192,512]{1,0:T(8,128)(2,1)S(1)}, u32[]{:S(2)}, u32[]{:S(2)}) %collective-permute-start.12) | collective-permute-done | bytes 196640 | tf_op jit(solution)/shard_map/ppermute | solution.py:43
  24.4 0.8 %shard_map.40 = bf16[64,2048]{1,0:T(8,128)(2,1)} custom-call(bf16[64,2048]{1,0:T(8,128)(2,1)S(1)} %copy-done, f32[2,512,128]{2,1,0:T(8,128)S(1)} %get-tuple-element.51.refs_1_, f32[2,512,128]{2,1,0:T(8,128)S(1)} %get-tuple-element.52.refs_2_, f32[2,512,128]{2,1,0:T(8,128)S(1)} %get-tuple-element.53.refs_3_, ...), custom_call_target="tpu_custom_call" | custom-call | tf_op jit(solution)/shard_map/pallas_call | solution.py:169
  (6 shorter events, 0.1 us)
Async XLA Ops:
  0.0 0.8 %copy-start.1 = (bf16[64,256]{1,0:T(8,128)(2,1)S(1)}, bf16[64,256]{1,0:T(8,128)(2,1)}, u32[]{:S(2)}) copy-start(bf16[64,256]{1,0:T(8,128)(2,1)} %param.5) | copy-start | bytes 98308
  0.8 18.3 %copy-start = (bf16[64,2048]{1,0:T(8,128)(2,1)S(1)}, bf16[64,2048]{1,0:T(8,128)(2,1)}, u32[]{:S(2)}) copy-start(bf16[64,2048]{1,0:T(8,128)(2,1)} %refs_0_.7) | copy-start | bytes 786436
  0.8 8.4 %collective-permute-start = (bf16[64,512]{1,0:T(8,128)(2,1)S(1)}, bf16[64,512]{1,0:T(8,128)(2,1)S(1)}, u32[]{:S(2)}, u32[]{:S(2)}) collective-permute-start(bf16[64,512]{1,0:T(8,128)(2,1)S(1)} %constant_dynamic-update-slice_fusion), channel_id=1, source_target_pairs={{0,24},{1,25},{2,26},{3,27},{4,28},{5,29},{6,30},{7,31},{8,16},{9,... | collective-permute-start | bytes 196616 | tf_op jit(solution)/shard_map/ppermute | solution.py:43
  5.9 5.2 %collective-permute-start.1 = (bf16[64,512]{1,0:T(8,128)(2,1)S(1)}, bf16[64,512]{1,0:T(8,128)(2,1)S(1)}, u32[]{:S(2)}, u32[]{:S(2)}) collective-permute-start(bf16[64,512]{1,0:T(8,128)(2,1)S(1)} %constant_dynamic-update-slice_fusion), channel_id=1, source_target_pairs={{0,5},{1,4},{2,7},{3,6},{4,1},{5,0},{6,3},{7,2},{8,13},{9,12},{10,... | collective-permute-start | bytes 196616 | tf_op jit(solution)/shard_map/ppermute | solution.py:43
  8.4 5.2 %collective-permute-start.2 = (bf16[64,512]{1,0:T(8,128)(2,1)S(1)}, bf16[64,512]{1,0:T(8,128)(2,1)S(1)}, u32[]{:S(2)}, u32[]{:S(2)}) collective-permute-start(bf16[64,512]{1,0:T(8,128)(2,1)S(1)} %constant_dynamic-update-slice_fusion), channel_id=1, source_target_pairs={{0,16},{1,17},{2,18},{3,19},{4,20},{5,21},{6,22},{7,23},{8,24},{9,... | collective-permute-start | bytes 196616 | tf_op jit(solution)/shard_map/ppermute | solution.py:43
  8.4 5.2 %collective-permute-start.3 = (bf16[64,512]{1,0:T(8,128)(2,1)S(1)}, bf16[64,512]{1,0:T(8,128)(2,1)S(1)}, u32[]{:S(2)}, u32[]{:S(2)}) collective-permute-start(bf16[64,512]{1,0:T(8,128)(2,1)S(1)} %constant_dynamic-update-slice_fusion), channel_id=1, source_target_pairs={{0,8},{1,9},{2,10},{3,11},{4,12},{5,13},{6,14},{7,15},{8,0},{9,1},... | collective-permute-start | bytes 196616 | tf_op jit(solution)/shard_map/ppermute | solution.py:43
  13.5 6.4 %collective-permute-start.7 = (bf16[256,512]{1,0:T(8,128)(2,1)S(1)}, bf16[256,512]{1,0:T(8,128)(2,1)S(1)}, u32[]{:S(2)}, u32[]{:S(2)}) collective-permute-start(bf16[256,512]{1,0:T(8,128)(2,1)S(1)} %pad_maximum_fusion.1.refs_1_), channel_id=1, source_target_pairs={{0,1},{1,0},{2,3},{3,2},{4,5},{5,4},{6,7},{7,6},{8,9},{9,8},{10,11... | collective-permute-start | bytes 786440 | tf_op jit(solution)/shard_map/ppermute | solution.py:43
  14.1 6.4 %collective-permute-start.8 = (bf16[256,512]{1,0:T(8,128)(2,1)S(1)}, bf16[256,512]{1,0:T(8,128)(2,1)S(1)}, u32[]{:S(2)}, u32[]{:S(2)}) collective-permute-start(bf16[256,512]{1,0:T(8,128)(2,1)S(1)} %pad_maximum_fusion.1.refs_1_), channel_id=1, source_target_pairs={{0,4},{1,5},{2,6},{3,7},{4,0},{5,1},{6,2},{7,3},{8,12},{9,13},{10,... | collective-permute-start | bytes 786440 | tf_op jit(solution)/shard_map/ppermute | solution.py:43
  14.7 6.5 %collective-permute-start.4 = (bf16[64,512]{1,0:T(8,128)(2,1)S(1)}, bf16[64,512]{1,0:T(8,128)(2,1)S(1)}, u32[]{:S(2)}, u32[]{:S(2)}) collective-permute-start(bf16[64,512]{1,0:T(8,128)(2,1)S(1)} %collective-permute-done.1.refs_2_), channel_id=1, source_target_pairs={{0,24},{1,25},{2,26},{3,27},{4,28},{5,29},{6,30},{7,31},{8,16},{9,... | collective-permute-start | bytes 196616 | tf_op jit(solution)/shard_map/ppermute | solution.py:43
  17.4 5.5 %collective-permute-start.5 = (bf16[64,512]{1,0:T(8,128)(2,1)S(1)}, bf16[64,512]{1,0:T(8,128)(2,1)S(1)}, u32[]{:S(2)}, u32[]{:S(2)}) collective-permute-start(bf16[64,512]{1,0:T(8,128)(2,1)S(1)} %collective-permute-done.1.refs_2_), channel_id=1, source_target_pairs={{0,16},{1,17},{2,18},{3,19},{4,20},{5,21},{6,22},{7,23},{8,24},{9,... | collective-permute-start | bytes 196616 | tf_op jit(solution)/shard_map/ppermute | solution.py:43
  17.4 5.5 %collective-permute-start.6 = (bf16[64,512]{1,0:T(8,128)(2,1)S(1)}, bf16[64,512]{1,0:T(8,128)(2,1)S(1)}, u32[]{:S(2)}, u32[]{:S(2)}) collective-permute-start(bf16[64,512]{1,0:T(8,128)(2,1)S(1)} %collective-permute-done.1.refs_2_), channel_id=1, source_target_pairs={{0,8},{1,9},{2,10},{3,11},{4,12},{5,13},{6,14},{7,15},{8,0},{9,1},... | collective-permute-start | bytes 196616 | tf_op jit(solution)/shard_map/ppermute | solution.py:43
  20.0 3.0 %collective-permute-start.11 = (bf16[320,512]{1,0:T(8,128)(2,1)S(1)}, bf16[320,512]{1,0:T(8,128)(2,1)S(1)}, u32[]{:S(2)}, u32[]{:S(2)}) collective-permute-start(bf16[320,512]{1,0:T(8,128)(2,1)S(1)} %pad_maximum_fusion), channel_id=1, source_target_pairs={{0,2},{1,3},{2,0},{3,1},{4,6},{5,7},{6,4},{7,5},{8,10},{9,11},{10,... | collective-permute-start | bytes 983048 | tf_op jit(solution)/shard_map/ppermute | solution.py:43
  20.5 2.5 %collective-permute-start.9 = (bf16[256,512]{1,0:T(8,128)(2,1)S(1)}, bf16[256,512]{1,0:T(8,128)(2,1)S(1)}, u32[]{:S(2)}, u32[]{:S(2)}) collective-permute-start(bf16[256,512]{1,0:T(8,128)(2,1)S(1)} %collective-permute-done.7.refs_4_), channel_id=1, source_target_pairs={{0,2},{1,3},{2,0},{3,1},{4,6},{5,7},{6,4},{7,5},{8,10},{9,11},{10,... | collective-permute-start | bytes 786440 | tf_op jit(solution)/shard_map/ppermute | solution.py:43
  21.1 1.9 %collective-permute-start.10 = (bf16[256,512]{1,0:T(8,128)(2,1)S(1)}, bf16[256,512]{1,0:T(8,128)(2,1)S(1)}, u32[]{:S(2)}, u32[]{:S(2)}) collective-permute-start(bf16[256,512]{1,0:T(8,128)(2,1)S(1)} %collective-permute-done.8.refs_5_), channel_id=1, source_target_pairs={{0,2},{1,3},{2,0},{3,1},{4,6},{5,7},{6,4},{7,5},{8,10},{9,11},{10,... | collective-permute-start | bytes 786440 | tf_op jit(solution)/shard_map/ppermute | solution.py:43
  22.9 1.5 %collective-permute-start.12 = (bf16[192,512]{1,0:T(8,128)(2,1)S(1)}, bf16[192,512]{1,0:T(8,128)(2,1)S(1)}, u32[]{:S(2)}, u32[]{:S(2)}) collective-permute-start(bf16[192,512]{1,0:T(8,128)(2,1)S(1)} %constant_dynamic-update-slice_fusion.2.refs_4_), channel_id=1, source_target_pairs={{0,2},{1,3},{2,0},{3,1},{4,6},{5,7},{6,4},{7,5},{8,10},{9,11},{10,... | collective-permute-start | bytes 589832 | tf_op jit(solution)/shard_map/ppermute | solution.py:43

commit v9 on v8

--- a/solution.py
+++ b/solution.py
@@ -220,7 +220,7 @@
         (longest, corner, *column), _ = tied([column[0], corner, *column[1:]])
         near = join([own, longest, *column])
         (near, corner), _ = tied([near, corner])
-        far = [sent(corner, steps) for steps in above]
+        far = [sent(corner, steps) for steps in [above[0], *above[:0:-1]]]
         sides = [sent(near, steps) for steps in columns + lines]
 
         state = fold(layout, queries, None, [near, corner], groups)

time: 25.4 us -> 25.2 us (level)
  transfers between devices with their start and end apart: 13 -> 13, of which waited for: 6 -> 7; matrix products, arithmetic and copies ran while one was open for 0% -> 0% of each run, Pallas kernels for 8% -> 8%
where the time goes in v9:
time: 25.2 us; the launch traced here: 25 us
  starting transfers between devices  14.5 us (58%)
  waiting for transfers between devices  6.87 us (27%)
  Pallas kernels  2.72 us (11%)
  local copies, waits for them, and re-layouts  0.8 us (3%)
    ppermute x13, starting transfers between devices, exchange(): lax.ppermute(array, AXES, [(rank, self.partner(rank, steps)) for rank in...  14.5 us
    ppermute x13, waiting for transfers between devices, exchange(): lax.ppermute(array, AXES, [(rank, self.partner(rank, steps)) for rank in...  6.87 us
    pallas_call x4, Pallas kernels, fold(): pl.pallas_call(functools.partial(fold_kernel, layout, [blocks for _, bloc...  2.72 us
    unnamed x7, local copies, waits for them, and re-layouts  0.79 us
  transfers between devices with their start and end apart: 13, of which 7 were waited for; matrix products, arithmetic and copies ran while one was open for 0% of the time, Pallas kernels for 8%

profile of v9, /device:TPU:0, one launch (start us, length us, event | category | flops | bytes accessed | tf_op | source)
XLA Modules:
  0.0 25.0 jit_solution(7812019896289995999)
XLA Ops:
  0.0 0.0 copy-start.1
  0.0 0.8 %constant_dynamic-update-slice_fusion.1 = bf16[64,512]{1,0:T(8,128)(2,1)S(1)} fusion(bf16[64,256]{1,0:T(8,128)(2,1)} %param.4), kind=kLoop, calls=%fused_computation.3 | loop fusion | bytes 65536
  0.8 0.0 copy-done.1
  0.8 0.0 copy-start
  0.8 5.1 %collective-permute-start = (bf16[64,512]{1,0:T(8,128)(2,1)S(1)}, bf16[64,512]{1,0:T(8,128)(2,1)S(1)}, u32[]{:S(2)}, u32[]{:S(2)}) collective-permute-start(bf16[64,512]{1,0:T(8,128)(2,1)S(1)} %constant_dynamic-update-slice_fusion), channel_id=1, source_target_pairs={{0,24},{1,25},{2,26},{3,27},{4,28},{5,29},{6,30},{7,31},{8,16},{9,... | collective-permute-start | bytes 196616 | tf_op jit(solution)/shard_map/ppermute | solution.py:43
  5.9 2.4 %collective-permute-start.1 = (bf16[64,512]{1,0:T(8,128)(2,1)S(1)}, bf16[64,512]{1,0:T(8,128)(2,1)S(1)}, u32[]{:S(2)}, u32[]{:S(2)}) collective-permute-start(bf16[64,512]{1,0:T(8,128)(2,1)S(1)} %constant_dynamic-update-slice_fusion), channel_id=1, source_target_pairs={{0,5},{1,4},{2,7},{3,6},{4,1},{5,0},{6,3},{7,2},{8,13},{9,12},{10,... | collective-permute-start | bytes 196616 | tf_op jit(solution)/shard_map/ppermute | solution.py:43
  8.4 0.0 collective-permute-start.2
  8.4 0.8 %collective-permute-start.3 = (bf16[64,512]{1,0:T(8,128)(2,1)S(1)}, bf16[64,512]{1,0:T(8,128)(2,1)S(1)}, u32[]{:S(2)}, u32[]{:S(2)}) collective-permute-start(bf16[64,512]{1,0:T(8,128)(2,1)S(1)} %constant_dynamic-update-slice_fusion), channel_id=1, source_target_pairs={{0,8},{1,9},{2,10},{3,11},{4,12},{5,13},{6,14},{7,15},{8,0},{9,1},... | collective-permute-start | bytes 196616 | tf_op jit(solution)/shard_map/ppermute | solution.py:43
  9.1 0.0 collective-permute-done
  9.1 1.9 %collective-permute-done.1.refs_2_ = bf16[64,512]{1,0:T(8,128)(2,1)S(1)} collective-permute-done((bf16[64,512]{1,0:T(8,128)(2,1)S(1)}, bf16[64,512]{1,0:T(8,128)(2,1)S(1)}, u32[]{:S(2)}, u32[]{:S(2)}) %collective-permute-start.1) | collective-permute-done | bytes 65568 | tf_op jit(solution)/shard_map/ppermute | solution.py:43
  11.1 2.4 %collective-permute-done.2 = bf16[64,512]{1,0:T(8,128)(2,1)S(1)} collective-permute-done((bf16[64,512]{1,0:T(8,128)(2,1)S(1)}, bf16[64,512]{1,0:T(8,128)(2,1)S(1)}, u32[]{:S(2)}, u32[]{:S(2)}) %collective-permute-start.2) | collective-permute-done | bytes 65568 | tf_op jit(solution)/shard_map/ppermute | solution.py:43
  13.5 0.0 collective-permute-done.3
  13.5 0.6 %collective-permute-start.7 = (bf16[256,512]{1,0:T(8,128)(2,1)S(1)}, bf16[256,512]{1,0:T(8,128)(2,1)S(1)}, u32[]{:S(2)}, u32[]{:S(2)}) collective-permute-start(bf16[256,512]{1,0:T(8,128)(2,1)S(1)} %pad_maximum_fusion.1.refs_1_), channel_id=1, source_target_pairs={{0,1},{1,0},{2,3},{3,2},{4,5},{5,4},{6,7},{7,6},{8,9},{9,8},{10,11... | collective-permute-start | bytes 786440 | tf_op jit(solution)/shard_map/ppermute | solution.py:43
  14.1 0.5 %collective-permute-start.8 = (bf16[256,512]{1,0:T(8,128)(2,1)S(1)}, bf16[256,512]{1,0:T(8,128)(2,1)S(1)}, u32[]{:S(2)}, u32[]{:S(2)}) collective-permute-start(bf16[256,512]{1,0:T(8,128)(2,1)S(1)} %pad_maximum_fusion.1.refs_1_), channel_id=1, source_target_pairs={{0,4},{1,5},{2,6},{3,7},{4,0},{5,1},{6,2},{7,3},{8,12},{9,13},{10,... | collective-permute-start | bytes 786440 | tf_op jit(solution)/shard_map/ppermute | solution.py:43
  14.7 2.7 %collective-permute-start.4 = (bf16[64,512]{1,0:T(8,128)(2,1)S(1)}, bf16[64,512]{1,0:T(8,128)(2,1)S(1)}, u32[]{:S(2)}, u32[]{:S(2)}) collective-permute-start(bf16[64,512]{1,0:T(8,128)(2,1)S(1)} %collective-permute-done.1.refs_2_), channel_id=1, source_target_pairs={{0,24},{1,25},{2,26},{3,27},{4,28},{5,29},{6,30},{7,31},{8,16},{9,... | collective-permute-start | bytes 196616 | tf_op jit(solution)/shard_map/ppermute | solution.py:43
  17.4 0.0 collective-permute-start.5
  17.4 1.7 %collective-permute-start.6 = (bf16[64,512]{1,0:T(8,128)(2,1)S(1)}, bf16[64,512]{1,0:T(8,128)(2,1)S(1)}, u32[]{:S(2)}, u32[]{:S(2)}) collective-permute-start(bf16[64,512]{1,0:T(8,128)(2,1)S(1)} %collective-permute-done.1.refs_2_), channel_id=1, source_target_pairs={{0,16},{1,17},{2,18},{3,19},{4,20},{5,21},{6,22},{7,23},{8,24},{9,... | collective-permute-start | bytes 196616 | tf_op jit(solution)/shard_map/ppermute | solution.py:43
  19.0 0.0 copy-done
  19.0 0.6 %shard_map.37 = (f32[2,512,128]{2,1,0:T(8,128)S(1)}, f32[2,512,128]{2,1,0:T(8,128)S(1)}, f32[2,512,128]{2,1,0:T(8,128)S(1)}) custom-call(bf16[64,2048]{1,0:T(8,128)(2,1)S(1)} %copy-done, bf16[256,512]{1,0:T(8,128)(2,1)S(1)} %pad_maximum_fusion.1.refs_1_, bf16[64,512]{1,0:T(8,128)(2,1)S(1)} %collective-permute-done.1.refs_2_), custom_call_target="tpu_custom_call" | custom-call | tf_op jit(solution)/shard_map/pallas_call | solution.py:169
  19.6 0.3 %collective-permute-done.7.refs_4_ = bf16[256,512]{1,0:T(8,128)(2,1)S(1)} collective-permute-done((bf16[256,512]{1,0:T(8,128)(2,1)S(1)}, bf16[256,512]{1,0:T(8,128)(2,1)S(1)}, u32[]{:S(2)}, u32[]{:S(2)}) %collective-permute-start.7) | collective-permute-done | bytes 262176 | tf_op jit(solution)/shard_map/ppermute | solution.py:43
  20.0 0.0 collective-permute-start.11
  20.0 0.5 %collective-permute-done.8.refs_5_ = bf16[256,512]{1,0:T(8,128)(2,1)S(1)} collective-permute-done((bf16[256,512]{1,0:T(8,128)(2,1)S(1)}, bf16[256,512]{1,0:T(8,128)(2,1)S(1)}, u32[]{:S(2)}, u32[]{:S(2)}) %collective-permute-start.8) | collective-permute-done | bytes 262176 | tf_op jit(solution)/shard_map/ppermute | solution.py:43
  20.5 0.0 collective-permute-start.9
  20.5 0.6 %shard_map.38 = (f32[2,512,128]{2,1,0:T(8,128)S(1)}, f32[2,512,128]{2,1,0:T(8,128)S(1)}, f32[2,512,128]{2,1,0:T(8,128)S(1)}) custom-call(bf16[64,2048]{1,0:T(8,128)(2,1)S(1)} %copy-done, f32[2,512,128]{2,1,0:T(8,128)S(1)} %get-tuple-element.40.refs_1_, f32[2,512,128]{2,1,0:T(8,128)S(1)} %get-tuple-element.41.refs_2_, ...), custom_call_target="tpu_custom_call" | custom-call | tf_op jit(solution)/shard_map/pallas_call | solution.py:169
  21.1 0.0 collective-permute-done.4
  21.1 0.6 %collective-permute-start.10 = (bf16[256,512]{1,0:T(8,128)(2,1)S(1)}, bf16[256,512]{1,0:T(8,128)(2,1)S(1)}, u32[]{:S(2)}, u32[]{:S(2)}) collective-permute-start(bf16[256,512]{1,0:T(8,128)(2,1)S(1)} %collective-permute-done.8.refs_5_), channel_id=1, source_target_pairs={{0,2},{1,3},{2,0},{3,1},{4,6},{5,7},{6,4},{7,5},{8,10},{9,11},{10,... | collective-permute-start | bytes 786440 | tf_op jit(solution)/shard_map/ppermute | solution.py:43
  21.7 0.1 collective-permute-done.5
  21.8 0.9 %collective-permute-done.6 = bf16[64,512]{1,0:T(8,128)(2,1)S(1)} collective-permute-done((bf16[64,512]{1,0:T(8,128)(2,1)S(1)}, bf16[64,512]{1,0:T(8,128)(2,1)S(1)}, u32[]{:S(2)}, u32[]{:S(2)}) %collective-permute-start.6) | collective-permute-done | bytes 65568 | tf_op jit(solution)/shard_map/ppermute | solution.py:43
  22.7 0.1 collective-permute-start.12
  22.8 0.0 collective-permute-done.11.refs_6_
  22.8 0.0 collective-permute-done.9.refs_4_
  22.8 0.0 collective-permute-done.10.refs_5_
  22.9 0.8 %shard_map.39 = (f32[2,512,128]{2,1,0:T(8,128)S(1)}, f32[2,512,128]{2,1,0:T(8,128)S(1)}, f32[2,512,128]{2,1,0:T(8,128)S(1)}) custom-call(bf16[64,2048]{1,0:T(8,128)(2,1)S(1)} %copy-done, f32[2,512,128]{2,1,0:T(8,128)S(1)} %get-tuple-element.48.refs_1_, f32[2,512,128]{2,1,0:T(8,128)S(1)} %get-tuple-element.49.refs_2_, ...), custom_call_target="tpu_custom_call" | custom-call | tf_op jit(solution)/shard_map/pallas_call | solution.py:169
  23.7 0.6 %collective-permute-done.12.refs_5_ = bf16[192,512]{1,0:T(8,128)(2,1)S(1)} collective-permute-done((bf16[192,512]{1,0:T(8,128)(2,1)S(1)}, bf16[192,512]{1,0:T(8,128)(2,1)S(1)}, u32[]{:S(2)}, u32[]{:S(2)}) %collective-permute-start.12) | collective-permute-done | bytes 196640 | tf_op jit(solution)/shard_map/ppermute | solution.py:43
  24.2 0.8 %shard_map.40 = bf16[64,2048]{1,0:T(8,128)(2,1)} custom-call(bf16[64,2048]{1,0:T(8,128)(2,1)S(1)} %copy-done, f32[2,512,128]{2,1,0:T(8,128)S(1)} %get-tuple-element.51.refs_1_, f32[2,512,128]{2,1,0:T(8,128)S(1)} %get-tuple-element.52.refs_2_, f32[2,512,128]{2,1,0:T(8,128)S(1)} %get-tuple-element.53.refs_3_, ...), custom_call_target="tpu_custom_call" | custom-call | tf_op jit(solution)/shard_map/pallas_call | solution.py:169
  (6 shorter events, 0.1 us)
Async XLA Ops:
  0.0 0.8 %copy-start.1 = (bf16[64,256]{1,0:T(8,128)(2,1)S(1)}, bf16[64,256]{1,0:T(8,128)(2,1)}, u32[]{:S(2)}) copy-start(bf16[64,256]{1,0:T(8,128)(2,1)} %param.5) | copy-start | bytes 98308
  0.8 18.3 %copy-start = (bf16[64,2048]{1,0:T(8,128)(2,1)S(1)}, bf16[64,2048]{1,0:T(8,128)(2,1)}, u32[]{:S(2)}) copy-start(bf16[64,2048]{1,0:T(8,128)(2,1)} %refs_0_.7) | copy-start | bytes 786436
  0.8 8.4 %collective-permute-start = (bf16[64,512]{1,0:T(8,128)(2,1)S(1)}, bf16[64,512]{1,0:T(8,128)(2,1)S(1)}, u32[]{:S(2)}, u32[]{:S(2)}) collective-permute-start(bf16[64,512]{1,0:T(8,128)(2,1)S(1)} %constant_dynamic-update-slice_fusion), channel_id=1, source_target_pairs={{0,24},{1,25},{2,26},{3,27},{4,28},{5,29},{6,30},{7,31},{8,16},{9,... | collective-permute-start | bytes 196616 | tf_op jit(solution)/shard_map/ppermute | solution.py:43
  5.9 5.2 %collective-permute-start.1 = (bf16[64,512]{1,0:T(8,128)(2,1)S(1)}, bf16[64,512]{1,0:T(8,128)(2,1)S(1)}, u32[]{:S(2)}, u32[]{:S(2)}) collective-permute-start(bf16[64,512]{1,0:T(8,128)(2,1)S(1)} %constant_dynamic-update-slice_fusion), channel_id=1, source_target_pairs={{0,5},{1,4},{2,7},{3,6},{4,1},{5,0},{6,3},{7,2},{8,13},{9,12},{10,... | collective-permute-start | bytes 196616 | tf_op jit(solution)/shard_map/ppermute | solution.py:43
  8.4 5.2 %collective-permute-start.2 = (bf16[64,512]{1,0:T(8,128)(2,1)S(1)}, bf16[64,512]{1,0:T(8,128)(2,1)S(1)}, u32[]{:S(2)}, u32[]{:S(2)}) collective-permute-start(bf16[64,512]{1,0:T(8,128)(2,1)S(1)} %constant_dynamic-update-slice_fusion), channel_id=1, source_target_pairs={{0,16},{1,17},{2,18},{3,19},{4,20},{5,21},{6,22},{7,23},{8,24},{9,... | collective-permute-start | bytes 196616 | tf_op jit(solution)/shard_map/ppermute | solution.py:43
  8.4 5.2 %collective-permute-start.3 = (bf16[64,512]{1,0:T(8,128)(2,1)S(1)}, bf16[64,512]{1,0:T(8,128)(2,1)S(1)}, u32[]{:S(2)}, u32[]{:S(2)}) collective-permute-start(bf16[64,512]{1,0:T(8,128)(2,1)S(1)} %constant_dynamic-update-slice_fusion), channel_id=1, source_target_pairs={{0,8},{1,9},{2,10},{3,11},{4,12},{5,13},{6,14},{7,15},{8,0},{9,1},... | collective-permute-start | bytes 196616 | tf_op jit(solution)/shard_map/ppermute | solution.py:43
  13.5 6.4 %collective-permute-start.7 = (bf16[256,512]{1,0:T(8,128)(2,1)S(1)}, bf16[256,512]{1,0:T(8,128)(2,1)S(1)}, u32[]{:S(2)}, u32[]{:S(2)}) collective-permute-start(bf16[256,512]{1,0:T(8,128)(2,1)S(1)} %pad_maximum_fusion.1.refs_1_), channel_id=1, source_target_pairs={{0,1},{1,0},{2,3},{3,2},{4,5},{5,4},{6,7},{7,6},{8,9},{9,8},{10,11... | collective-permute-start | bytes 786440 | tf_op jit(solution)/shard_map/ppermute | solution.py:43
  14.1 6.4 %collective-permute-start.8 = (bf16[256,512]{1,0:T(8,128)(2,1)S(1)}, bf16[256,512]{1,0:T(8,128)(2,1)S(1)}, u32[]{:S(2)}, u32[]{:S(2)}) collective-permute-start(bf16[256,512]{1,0:T(8,128)(2,1)S(1)} %pad_maximum_fusion.1.refs_1_), channel_id=1, source_target_pairs={{0,4},{1,5},{2,6},{3,7},{4,0},{5,1},{6,2},{7,3},{8,12},{9,13},{10,... | collective-permute-start | bytes 786440 | tf_op jit(solution)/shard_map/ppermute | solution.py:43
  14.7 6.5 %collective-permute-start.4 = (bf16[64,512]{1,0:T(8,128)(2,1)S(1)}, bf16[64,512]{1,0:T(8,128)(2,1)S(1)}, u32[]{:S(2)}, u32[]{:S(2)}) collective-permute-start(bf16[64,512]{1,0:T(8,128)(2,1)S(1)} %collective-permute-done.1.refs_2_), channel_id=1, source_target_pairs={{0,24},{1,25},{2,26},{3,27},{4,28},{5,29},{6,30},{7,31},{8,16},{9,... | collective-permute-start | bytes 196616 | tf_op jit(solution)/shard_map/ppermute | solution.py:43
  17.4 4.4 %collective-permute-start.5 = (bf16[64,512]{1,0:T(8,128)(2,1)S(1)}, bf16[64,512]{1,0:T(8,128)(2,1)S(1)}, u32[]{:S(2)}, u32[]{:S(2)}) collective-permute-start(bf16[64,512]{1,0:T(8,128)(2,1)S(1)} %collective-permute-done.1.refs_2_), channel_id=1, source_target_pairs={{0,8},{1,9},{2,10},{3,11},{4,12},{5,13},{6,14},{7,15},{8,0},{9,1},... | collective-permute-start | bytes 196616 | tf_op jit(solution)/shard_map/ppermute | solution.py:43
  17.4 5.3 %collective-permute-start.6 = (bf16[64,512]{1,0:T(8,128)(2,1)S(1)}, bf16[64,512]{1,0:T(8,128)(2,1)S(1)}, u32[]{:S(2)}, u32[]{:S(2)}) collective-permute-start(bf16[64,512]{1,0:T(8,128)(2,1)S(1)} %collective-permute-done.1.refs_2_), channel_id=1, source_target_pairs={{0,16},{1,17},{2,18},{3,19},{4,20},{5,21},{6,22},{7,23},{8,24},{9,... | collective-permute-start | bytes 196616 | tf_op jit(solution)/shard_map/ppermute | solution.py:43
  20.0 2.8 %collective-permute-start.11 = (bf16[320,512]{1,0:T(8,128)(2,1)S(1)}, bf16[320,512]{1,0:T(8,128)(2,1)S(1)}, u32[]{:S(2)}, u32[]{:S(2)}) collective-permute-start(bf16[320,512]{1,0:T(8,128)(2,1)S(1)} %pad_maximum_fusion), channel_id=1, source_target_pairs={{0,2},{1,3},{2,0},{3,1},{4,6},{5,7},{6,4},{7,5},{8,10},{9,11},{10,... | collective-permute-start | bytes 983048 | tf_op jit(solution)/shard_map/ppermute | solution.py:43
  20.5 2.3 %collective-permute-start.9 = (bf16[256,512]{1,0:T(8,128)(2,1)S(1)}, bf16[256,512]{1,0:T(8,128)(2,1)S(1)}, u32[]{:S(2)}, u32[]{:S(2)}) collective-permute-start(bf16[256,512]{1,0:T(8,128)(2,1)S(1)} %collective-permute-done.7.refs_4_), channel_id=1, source_target_pairs={{0,2},{1,3},{2,0},{3,1},{4,6},{5,7},{6,4},{7,5},{8,10},{9,11},{10,... | collective-permute-start | bytes 786440 | tf_op jit(solution)/shard_map/ppermute | solution.py:43
  21.1 1.7 %collective-permute-start.10 = (bf16[256,512]{1,0:T(8,128)(2,1)S(1)}, bf16[256,512]{1,0:T(8,128)(2,1)S(1)}, u32[]{:S(2)}, u32[]{:S(2)}) collective-permute-start(bf16[256,512]{1,0:T(8,128)(2,1)S(1)} %collective-permute-done.8.refs_5_), channel_id=1, source_target_pairs={{0,2},{1,3},{2,0},{3,1},{4,6},{5,7},{6,4},{7,5},{8,10},{9,11},{10,... | collective-permute-start | bytes 786440 | tf_op jit(solution)/shard_map/ppermute | solution.py:43
  22.7 1.5 %collective-permute-start.12 = (bf16[192,512]{1,0:T(8,128)(2,1)S(1)}, bf16[192,512]{1,0:T(8,128)(2,1)S(1)}, u32[]{:S(2)}, u32[]{:S(2)}) collective-permute-start(bf16[192,512]{1,0:T(8,128)(2,1)S(1)} %constant_dynamic-update-slice_fusion.2.refs_4_), channel_id=1, source_target_pairs={{0,2},{1,3},{2,0},{3,1},{4,6},{5,7},{6,4},{7,5},{8,10},{9,11},{10,... | collective-permute-start | bytes 589832 | tf_op jit(solution)/shard_map/ppermute | solution.py:43

commit v10 on v9

--- a/solution.py
+++ b/solution.py
@@ -225,7 +225,7 @@
 
         state = fold(layout, queries, None, [near, corner], groups)
         sides, state = tied(sides, state)
-        others = swapped(sides) + swapped([join([corner, near])])
+        others = swapped([join([corner, near])]) + swapped(sides)
         state = fold(layout, queries, state, sides, groups)
         far, state = tied(far, state)
         far = [join(far)]

time: 25.2 us -> 25.3 us (level)
  no operation moved by 1% of the time
where the time goes in v10:
time: 25.3 us; the launch traced here: 25 us
  starting transfers between devices  14.5 us (57%)
  waiting for transfers between devices  6.87 us (27%)
  Pallas kernels  2.72 us (11%)
  local copies, waits for them, and re-layouts  0.8 us (3%)
    ppermute x13, starting transfers between devices, exchange(): lax.ppermute(array, AXES, [(rank, self.partner(rank, steps)) for rank in...  14.5 us
    ppermute x13, waiting for transfers between devices, exchange(): lax.ppermute(array, AXES, [(rank, self.partner(rank, steps)) for rank in...  6.87 us
    pallas_call x4, Pallas kernels, fold(): pl.pallas_call(functools.partial(fold_kernel, layout, [blocks for _, bloc...  2.72 us
    unnamed x7, local copies, waits for them, and re-layouts  0.79 us
  transfers between devices with their start and end apart: 13, of which 7 were waited for; matrix products, arithmetic and copies ran while one was open for 0% of the time, Pallas kernels for 8%

profile of v10, /device:TPU:0, one launch (start us, length us, event | category | flops | bytes accessed | tf_op | source)
XLA Modules:
  0.0 25.0 jit_solution(16361872573315583867)
XLA Ops:
  0.0 0.0 copy-start.1
  0.0 0.8 %constant_dynamic-update-slice_fusion.1 = bf16[64,512]{1,0:T(8,128)(2,1)S(1)} fusion(bf16[64,256]{1,0:T(8,128)(2,1)} %param.4), kind=kLoop, calls=%fused_computation.3 | loop fusion | bytes 65536
  0.8 0.0 copy-done.1
  0.8 0.0 copy-start
  0.8 5.1 %collective-permute-start = (bf16[64,512]{1,0:T(8,128)(2,1)S(1)}, bf16[64,512]{1,0:T(8,128)(2,1)S(1)}, u32[]{:S(2)}, u32[]{:S(2)}) collective-permute-start(bf16[64,512]{1,0:T(8,128)(2,1)S(1)} %constant_dynamic-update-slice_fusion), channel_id=1, source_target_pairs={{0,24},{1,25},{2,26},{3,27},{4,28},{5,29},{6,30},{7,31},{8,16},{9,... | collective-permute-start | bytes 196616 | tf_op jit(solution)/shard_map/ppermute | solution.py:43
  5.9 2.4 %collective-permute-start.1 = (bf16[64,512]{1,0:T(8,128)(2,1)S(1)}, bf16[64,512]{1,0:T(8,128)(2,1)S(1)}, u32[]{:S(2)}, u32[]{:S(2)}) collective-permute-start(bf16[64,512]{1,0:T(8,128)(2,1)S(1)} %constant_dynamic-update-slice_fusion), channel_id=1, source_target_pairs={{0,5},{1,4},{2,7},{3,6},{4,1},{5,0},{6,3},{7,2},{8,13},{9,12},{10,... | collective-permute-start | bytes 196616 | tf_op jit(solution)/shard_map/ppermute | solution.py:43
  8.4 0.0 collective-permute-start.2
  8.4 0.8 %collective-permute-start.3 = (bf16[64,512]{1,0:T(8,128)(2,1)S(1)}, bf16[64,512]{1,0:T(8,128)(2,1)S(1)}, u32[]{:S(2)}, u32[]{:S(2)}) collective-permute-start(bf16[64,512]{1,0:T(8,128)(2,1)S(1)} %constant_dynamic-update-slice_fusion), channel_id=1, source_target_pairs={{0,8},{1,9},{2,10},{3,11},{4,12},{5,13},{6,14},{7,15},{8,0},{9,1},... | collective-permute-start | bytes 196616 | tf_op jit(solution)/shard_map/ppermute | solution.py:43
  9.1 0.0 collective-permute-done
  9.1 1.9 %collective-permute-done.1.refs_2_ = bf16[64,512]{1,0:T(8,128)(2,1)S(1)} collective-permute-done((bf16[64,512]{1,0:T(8,128)(2,1)S(1)}, bf16[64,512]{1,0:T(8,128)(2,1)S(1)}, u32[]{:S(2)}, u32[]{:S(2)}) %collective-permute-start.1) | collective-permute-done | bytes 65568 | tf_op jit(solution)/shard_map/ppermute | solution.py:43
  11.1 2.4 %collective-permute-done.2 = bf16[64,512]{1,0:T(8,128)(2,1)S(1)} collective-permute-done((bf16[64,512]{1,0:T(8,128)(2,1)S(1)}, bf16[64,512]{1,0:T(8,128)(2,1)S(1)}, u32[]{:S(2)}, u32[]{:S(2)}) %collective-permute-start.2) | collective-permute-done | bytes 65568 | tf_op jit(solution)/shard_map/ppermute | solution.py:43
  13.5 0.0 collective-permute-done.3
  13.5 0.6 %collective-permute-start.7 = (bf16[256,512]{1,0:T(8,128)(2,1)S(1)}, bf16[256,512]{1,0:T(8,128)(2,1)S(1)}, u32[]{:S(2)}, u32[]{:S(2)}) collective-permute-start(bf16[256,512]{1,0:T(8,128)(2,1)S(1)} %pad_maximum_fusion.1.refs_1_), channel_id=1, source_target_pairs={{0,1},{1,0},{2,3},{3,2},{4,5},{5,4},{6,7},{7,6},{8,9},{9,8},{10,11... | collective-permute-start | bytes 786440 | tf_op jit(solution)/shard_map/ppermute | solution.py:43
  14.1 0.5 %collective-permute-start.8 = (bf16[256,512]{1,0:T(8,128)(2,1)S(1)}, bf16[256,512]{1,0:T(8,128)(2,1)S(1)}, u32[]{:S(2)}, u32[]{:S(2)}) collective-permute-start(bf16[256,512]{1,0:T(8,128)(2,1)S(1)} %pad_maximum_fusion.1.refs_1_), channel_id=1, source_target_pairs={{0,4},{1,5},{2,6},{3,7},{4,0},{5,1},{6,2},{7,3},{8,12},{9,13},{10,... | collective-permute-start | bytes 786440 | tf_op jit(solution)/shard_map/ppermute | solution.py:43
  14.7 2.7 %collective-permute-start.4 = (bf16[64,512]{1,0:T(8,128)(2,1)S(1)}, bf16[64,512]{1,0:T(8,128)(2,1)S(1)}, u32[]{:S(2)}, u32[]{:S(2)}) collective-permute-start(bf16[64,512]{1,0:T(8,128)(2,1)S(1)} %collective-permute-done.1.refs_2_), channel_id=1, source_target_pairs={{0,24},{1,25},{2,26},{3,27},{4,28},{5,29},{6,30},{7,31},{8,16},{9,... | collective-permute-start | bytes 196616 | tf_op jit(solution)/shard_map/ppermute | solution.py:43
  17.4 0.0 collective-permute-start.5
  17.4 1.7 %collective-permute-start.6 = (bf16[64,512]{1,0:T(8,128)(2,1)S(1)}, bf16[64,512]{1,0:T(8,128)(2,1)S(1)}, u32[]{:S(2)}, u32[]{:S(2)}) collective-permute-start(bf16[64,512]{1,0:T(8,128)(2,1)S(1)} %collective-permute-done.1.refs_2_), channel_id=1, source_target_pairs={{0,16},{1,17},{2,18},{3,19},{4,20},{5,21},{6,22},{7,23},{8,24},{9,... | collective-permute-start | bytes 196616 | tf_op jit(solution)/shard_map/ppermute | solution.py:43
  19.0 0.0 copy-done
  19.0 0.6 %shard_map.37 = (f32[2,512,128]{2,1,0:T(8,128)S(1)}, f32[2,512,128]{2,1,0:T(8,128)S(1)}, f32[2,512,128]{2,1,0:T(8,128)S(1)}) custom-call(bf16[64,2048]{1,0:T(8,128)(2,1)S(1)} %copy-done, bf16[256,512]{1,0:T(8,128)(2,1)S(1)} %pad_maximum_fusion.1.refs_1_, bf16[64,512]{1,0:T(8,128)(2,1)S(1)} %collective-permute-done.1.refs_2_), custom_call_target="tpu_custom_call" | custom-call | tf_op jit(solution)/shard_map/pallas_call | solution.py:169
  19.6 0.3 %collective-permute-done.7.refs_4_ = bf16[256,512]{1,0:T(8,128)(2,1)S(1)} collective-permute-done((bf16[256,512]{1,0:T(8,128)(2,1)S(1)}, bf16[256,512]{1,0:T(8,128)(2,1)S(1)}, u32[]{:S(2)}, u32[]{:S(2)}) %collective-permute-start.7) | collective-permute-done | bytes 262176 | tf_op jit(solution)/shard_map/ppermute | solution.py:43
  20.0 0.0 collective-permute-start.9
  20.0 0.5 %collective-permute-done.8.refs_5_ = bf16[256,512]{1,0:T(8,128)(2,1)S(1)} collective-permute-done((bf16[256,512]{1,0:T(8,128)(2,1)S(1)}, bf16[256,512]{1,0:T(8,128)(2,1)S(1)}, u32[]{:S(2)}, u32[]{:S(2)}) %collective-permute-start.8) | collective-permute-done | bytes 262176 | tf_op jit(solution)/shard_map/ppermute | solution.py:43
  20.5 0.0 collective-permute-start.10
  20.5 0.6 %shard_map.38 = (f32[2,512,128]{2,1,0:T(8,128)S(1)}, f32[2,512,128]{2,1,0:T(8,128)S(1)}, f32[2,512,128]{2,1,0:T(8,128)S(1)}) custom-call(bf16[64,2048]{1,0:T(8,128)(2,1)S(1)} %copy-done, f32[2,512,128]{2,1,0:T(8,128)S(1)} %get-tuple-element.40.refs_1_, f32[2,512,128]{2,1,0:T(8,128)S(1)} %get-tuple-element.41.refs_2_, ...), custom_call_target="tpu_custom_call" | custom-call | tf_op jit(solution)/shard_map/pallas_call | solution.py:169
  21.1 0.0 collective-permute-done.4
  21.1 0.6 %collective-permute-start.11 = (bf16[256,512]{1,0:T(8,128)(2,1)S(1)}, bf16[256,512]{1,0:T(8,128)(2,1)S(1)}, u32[]{:S(2)}, u32[]{:S(2)}) collective-permute-start(bf16[256,512]{1,0:T(8,128)(2,1)S(1)} %collective-permute-done.8.refs_5_), channel_id=1, source_target_pairs={{0,2},{1,3},{2,0},{3,1},{4,6},{5,7},{6,4},{7,5},{8,10},{9,11},{10,... | collective-permute-start | bytes 786440 | tf_op jit(solution)/shard_map/ppermute | solution.py:43
  21.7 0.1 collective-permute-done.5
  21.8 0.9 %collective-permute-done.6 = bf16[64,512]{1,0:T(8,128)(2,1)S(1)} collective-permute-done((bf16[64,512]{1,0:T(8,128)(2,1)S(1)}, bf16[64,512]{1,0:T(8,128)(2,1)S(1)}, u32[]{:S(2)}, u32[]{:S(2)}) %collective-permute-start.6) | collective-permute-done | bytes 65568 | tf_op jit(solution)/shard_map/ppermute | solution.py:43
  22.7 0.1 collective-permute-start.12
  22.8 0.0 collective-permute-done.9.refs_4_
  22.8 0.0 collective-permute-done.10.refs_5_
  22.8 0.0 collective-permute-done.11.refs_6_
  22.9 0.8 %shard_map.39 = (f32[2,512,128]{2,1,0:T(8,128)S(1)}, f32[2,512,128]{2,1,0:T(8,128)S(1)}, f32[2,512,128]{2,1,0:T(8,128)S(1)}) custom-call(bf16[64,2048]{1,0:T(8,128)(2,1)S(1)} %copy-done, f32[2,512,128]{2,1,0:T(8,128)S(1)} %get-tuple-element.48.refs_1_, f32[2,512,128]{2,1,0:T(8,128)S(1)} %get-tuple-element.49.refs_2_, ...), custom_call_target="tpu_custom_call" | custom-call | tf_op jit(solution)/shard_map/pallas_call | solution.py:169
  23.7 0.6 %collective-permute-done.12.refs_5_ = bf16[192,512]{1,0:T(8,128)(2,1)S(1)} collective-permute-done((bf16[192,512]{1,0:T(8,128)(2,1)S(1)}, bf16[192,512]{1,0:T(8,128)(2,1)S(1)}, u32[]{:S(2)}, u32[]{:S(2)}) %collective-permute-start.12) | collective-permute-done | bytes 196640 | tf_op jit(solution)/shard_map/ppermute | solution.py:43
  24.2 0.8 %shard_map.40 = bf16[64,2048]{1,0:T(8,128)(2,1)} custom-call(bf16[64,2048]{1,0:T(8,128)(2,1)S(1)} %copy-done, f32[2,512,128]{2,1,0:T(8,128)S(1)} %get-tuple-element.51.refs_1_, f32[2,512,128]{2,1,0:T(8,128)S(1)} %get-tuple-element.52.refs_2_, f32[2,512,128]{2,1,0:T(8,128)S(1)} %get-tuple-element.53.refs_3_, ...), custom_call_target="tpu_custom_call" | custom-call | tf_op jit(solution)/shard_map/pallas_call | solution.py:169
  (6 shorter events, 0.1 us)
Async XLA Ops:
  0.0 0.8 %copy-start.1 = (bf16[64,256]{1,0:T(8,128)(2,1)S(1)}, bf16[64,256]{1,0:T(8,128)(2,1)}, u32[]{:S(2)}) copy-start(bf16[64,256]{1,0:T(8,128)(2,1)} %param.5) | copy-start | bytes 98308
  0.8 18.3 %copy-start = (bf16[64,2048]{1,0:T(8,128)(2,1)S(1)}, bf16[64,2048]{1,0:T(8,128)(2,1)}, u32[]{:S(2)}) copy-start(bf16[64,2048]{1,0:T(8,128)(2,1)} %refs_0_.7) | copy-start | bytes 786436
  0.8 8.4 %collective-permute-start = (bf16[64,512]{1,0:T(8,128)(2,1)S(1)}, bf16[64,512]{1,0:T(8,128)(2,1)S(1)}, u32[]{:S(2)}, u32[]{:S(2)}) collective-permute-start(bf16[64,512]{1,0:T(8,128)(2,1)S(1)} %constant_dynamic-update-slice_fusion), channel_id=1, source_target_pairs={{0,24},{1,25},{2,26},{3,27},{4,28},{5,29},{6,30},{7,31},{8,16},{9,... | collective-permute-start | bytes 196616 | tf_op jit(solution)/shard_map/ppermute | solution.py:43
  5.9 5.2 %collective-permute-start.1 = (bf16[64,512]{1,0:T(8,128)(2,1)S(1)}, bf16[64,512]{1,0:T(8,128)(2,1)S(1)}, u32[]{:S(2)}, u32[]{:S(2)}) collective-permute-start(bf16[64,512]{1,0:T(8,128)(2,1)S(1)} %constant_dynamic-update-slice_fusion), channel_id=1, source_target_pairs={{0,5},{1,4},{2,7},{3,6},{4,1},{5,0},{6,3},{7,2},{8,13},{9,12},{10,... | collective-permute-start | bytes 196616 | tf_op jit(solution)/shard_map/ppermute | solution.py:43
  8.4 5.2 %collective-permute-start.2 = (bf16[64,512]{1,0:T(8,128)(2,1)S(1)}, bf16[64,512]{1,0:T(8,128)(2,1)S(1)}, u32[]{:S(2)}, u32[]{:S(2)}) collective-permute-start(bf16[64,512]{1,0:T(8,128)(2,1)S(1)} %constant_dynamic-update-slice_fusion), channel_id=1, source_target_pairs={{0,16},{1,17},{2,18},{3,19},{4,20},{5,21},{6,22},{7,23},{8,24},{9,... | collective-permute-start | bytes 196616 | tf_op jit(solution)/shard_map/ppermute | solution.py:43
  8.4 5.2 %collective-permute-start.3 = (bf16[64,512]{1,0:T(8,128)(2,1)S(1)}, bf16[64,512]{1,0:T(8,128)(2,1)S(1)}, u32[]{:S(2)}, u32[]{:S(2)}) collective-permute-start(bf16[64,512]{1,0:T(8,128)(2,1)S(1)} %constant_dynamic-update-slice_fusion), channel_id=1, source_target_pairs={{0,8},{1,9},{2,10},{3,11},{4,12},{5,13},{6,14},{7,15},{8,0},{9,1},... | collective-permute-start | bytes 196616 | tf_op jit(solution)/shard_map/ppermute | solution.py:43
  13.5 6.4 %collective-permute-start.7 = (bf16[256,512]{1,0:T(8,128)(2,1)S(1)}, bf16[256,512]{1,0:T(8,128)(2,1)S(1)}, u32[]{:S(2)}, u32[]{:S(2)}) collective-permute-start(bf16[256,512]{1,0:T(8,128)(2,1)S(1)} %pad_maximum_fusion.1.refs_1_), channel_id=1, source_target_pairs={{0,1},{1,0},{2,3},{3,2},{4,5},{5,4},{6,7},{7,6},{8,9},{9,8},{10,11... | collective-permute-start | bytes 786440 | tf_op jit(solution)/shard_map/ppermute | solution.py:43
  14.1 6.4 %collective-permute-start.8 = (bf16[256,512]{1,0:T(8,128)(2,1)S(1)}, bf16[256,512]{1,0:T(8,128)(2,1)S(1)}, u32[]{:S(2)}, u32[]{:S(2)}) collective-permute-start(bf16[256,512]{1,0:T(8,128)(2,1)S(1)} %pad_maximum_fusion.1.refs_1_), channel_id=1, source_target_pairs={{0,4},{1,5},{2,6},{3,7},{4,0},{5,1},{6,2},{7,3},{8,12},{9,13},{10,... | collective-permute-start | bytes 786440 | tf_op jit(solution)/shard_map/ppermute | solution.py:43
  14.7 6.5 %collective-permute-start.4 = (bf16[64,512]{1,0:T(8,128)(2,1)S(1)}, bf16[64,512]{1,0:T(8,128)(2,1)S(1)}, u32[]{:S(2)}, u32[]{:S(2)}) collective-permute-start(bf16[64,512]{1,0:T(8,128)(2,1)S(1)} %collective-permute-done.1.refs_2_), channel_id=1, source_target_pairs={{0,24},{1,25},{2,26},{3,27},{4,28},{5,29},{6,30},{7,31},{8,16},{9,... | collective-permute-start | bytes 196616 | tf_op jit(solution)/shard_map/ppermute | solution.py:43
  17.4 4.4 %collective-permute-start.5 = (bf16[64,512]{1,0:T(8,128)(2,1)S(1)}, bf16[64,512]{1,0:T(8,128)(2,1)S(1)}, u32[]{:S(2)}, u32[]{:S(2)}) collective-permute-start(bf16[64,512]{1,0:T(8,128)(2,1)S(1)} %collective-permute-done.1.refs_2_), channel_id=1, source_target_pairs={{0,8},{1,9},{2,10},{3,11},{4,12},{5,13},{6,14},{7,15},{8,0},{9,1},... | collective-permute-start | bytes 196616 | tf_op jit(solution)/shard_map/ppermute | solution.py:43
  17.4 5.3 %collective-permute-start.6 = (bf16[64,512]{1,0:T(8,128)(2,1)S(1)}, bf16[64,512]{1,0:T(8,128)(2,1)S(1)}, u32[]{:S(2)}, u32[]{:S(2)}) collective-permute-start(bf16[64,512]{1,0:T(8,128)(2,1)S(1)} %collective-permute-done.1.refs_2_), channel_id=1, source_target_pairs={{0,16},{1,17},{2,18},{3,19},{4,20},{5,21},{6,22},{7,23},{8,24},{9,... | collective-permute-start | bytes 196616 | tf_op jit(solution)/shard_map/ppermute | solution.py:43
  20.0 2.8 %collective-permute-start.9 = (bf16[320,512]{1,0:T(8,128)(2,1)S(1)}, bf16[320,512]{1,0:T(8,128)(2,1)S(1)}, u32[]{:S(2)}, u32[]{:S(2)}) collective-permute-start(bf16[320,512]{1,0:T(8,128)(2,1)S(1)} %pad_maximum_fusion), channel_id=1, source_target_pairs={{0,2},{1,3},{2,0},{3,1},{4,6},{5,7},{6,4},{7,5},{8,10},{9,11},{10,... | collective-permute-start | bytes 983048 | tf_op jit(solution)/shard_map/ppermute | solution.py:43
  20.5 2.3 %collective-permute-start.10 = (bf16[256,512]{1,0:T(8,128)(2,1)S(1)}, bf16[256,512]{1,0:T(8,128)(2,1)S(1)}, u32[]{:S(2)}, u32[]{:S(2)}) collective-permute-start(bf16[256,512]{1,0:T(8,128)(2,1)S(1)} %collective-permute-done.7.refs_4_), channel_id=1, source_target_pairs={{0,2},{1,3},{2,0},{3,1},{4,6},{5,7},{6,4},{7,5},{8,10},{9,11},{10,... | collective-permute-start | bytes 786440 | tf_op jit(solution)/shard_map/ppermute | solution.py:43
  21.1 1.7 %collective-permute-start.11 = (bf16[256,512]{1,0:T(8,128)(2,1)S(1)}, bf16[256,512]{1,0:T(8,128)(2,1)S(1)}, u32[]{:S(2)}, u32[]{:S(2)}) collective-permute-start(bf16[256,512]{1,0:T(8,128)(2,1)S(1)} %collective-permute-done.8.refs_5_), channel_id=1, source_target_pairs={{0,2},{1,3},{2,0},{3,1},{4,6},{5,7},{6,4},{7,5},{8,10},{9,11},{10,... | collective-permute-start | bytes 786440 | tf_op jit(solution)/shard_map/ppermute | solution.py:43
  22.7 1.5 %collective-permute-start.12 = (bf16[192,512]{1,0:T(8,128)(2,1)S(1)}, bf16[192,512]{1,0:T(8,128)(2,1)S(1)}, u32[]{:S(2)}, u32[]{:S(2)}) collective-permute-start(bf16[192,512]{1,0:T(8,128)(2,1)S(1)} %constant_dynamic-update-slice_fusion.2.refs_4_), channel_id=1, source_target_pairs={{0,2},{1,3},{2,0},{3,1},{4,6},{5,7},{6,4},{7,5},{8,10},{9,11},{10,... | collective-permute-start | bytes 589832 | tf_op jit(solution)/shard_map/ppermute | solution.py:43
